TPU v7x, 32 devices: a whole 2x2x4 slice. The times are simulated.
32 devices in a mesh: group: 4 (over y, core), shard: 8 (over z, x).
Axes of the slice: x: 2, y: 2, z: 4, core: 2. Of those that a mesh axis runs over, the one named last changes fastest.
Arguments:
- tokens: bfloat16 [4096, 2048], P(('group', 'shard')), may hold values from -6 to 6
- lengths: int32 [32, 4], P(('group', 'shard')), may hold values from 1 to 96, as said below
- cotangent: bfloat16 [4096, 2048], P(('group', 'shard')), may hold values from -6 to 6
- norm1_gain: bfloat16 [2048], P('shard'), may hold values from 0.099609375 to 1.8984375
- gate_in: bfloat16 [2048, 2560], P('shard'), may hold values from -0.125 to 0.125
- linear_in: bfloat16 [2048, 2560], P('shard'), may hold values from -0.125 to 0.125
- conv_kernel: bfloat16 [4, 2560], P(None, 'shard'), may hold values from -3 to 3
- conv_bias: bfloat16 [2560], P('shard'), may hold values from -3 to 3
- rate_weight: bfloat16 [2560, 160], P('shard'), may hold values from -0.5 to 0.5
- rate_bias: bfloat16 [2560], P('shard'), may hold values from -4 to 4
- input_weight: bfloat16 [2560, 160], P('shard'), may hold values from -0.5 to 0.5
- input_bias: bfloat16 [2560], P('shard'), may hold values from -4 to 4
- decay_param: bfloat16 [2560], P('shard'), may hold values from 4 to 8
- out_proj: bfloat16 [2560, 2048], P('shard'), may hold values from -0.25 to 0.25
- norm2_gain: bfloat16 [2048], P('shard'), may hold values from 0.099609375 to 1.8984375
- mlp_gate: bfloat16 [2048, 6144], P('shard'), may hold values from -0.125 to 0.125
- mlp_up: bfloat16 [2048, 6144], P('shard'), may hold values from -0.125 to 0.125
- mlp_down: bfloat16 [6144, 2048], P('shard'), may hold values from -0.109375 to 0.109375
Outputs:
- mixed: bfloat16 [4096, 2048], P(('group', 'shard'))
- grad_tokens: bfloat16 [4096, 2048], P(('group', 'shard'))
- grad_norm1_gain: float32 [2048], P('shard')
- grad_gate_in: float32 [2048, 2560], P('shard')
- grad_linear_in: float32 [2048, 2560], P('shard')
- grad_conv_kernel: float32 [4, 2560], P(None, 'shard')
- grad_conv_bias: float32 [2560], P('shard')
- grad_rate_weight: float32 [2560, 160], P('shard')
- grad_rate_bias: float32 [2560], P('shard')
- grad_input_weight: float32 [2560, 160], P('shard')
- grad_input_bias: float32 [2560], P('shard')
- grad_decay: float32 [2560], P('shard')
- grad_out_proj: float32 [2560, 2048], P('shard')
- grad_norm2_gain: float32 [2048], P('shard')
- grad_mlp_gate: float32 [2048, 6144], P('shard')
- grad_mlp_up: float32 [2048, 6144], P('shard')
- grad_mlp_down: float32 [6144, 2048], P('shard')
Inputs may be any that keep to these rules, and one draw needn't show every extreme that they name: Each row belongs to one device; its first 3 entries are the lengths of that device's sequences in order, one of them exactly 96, and its last entry is its padding, 1 to 16 rows; every row sums to 128.
All inputs are finite; a program needn't handle non-finite values.
Results may differ from a plain program's by a relative error of at most 0.018.
Values may be sent and summed in bfloat16 or wider, within the bound.
A program may use at most 448 MiB of HBM per device.

v0:
```python
from functools import partial

import jax
import jax.numpy as jnp
from jax import lax
from jax.sharding import PartitionSpec as P

RATE_SCALE = 8.0
EPSILON = 1e-06


def as_sent(shard):
    return jax.tree.map(lambda a: a.astype(jnp.bfloat16) if a.dtype == jnp.float32 else a, shard)


def layout(counts, row_count):
    run_ends = jnp.cumsum(counts)
    positions = jnp.arange(row_count, dtype=jnp.int32)
    segment_ids = jnp.sum((positions[:, None] >= run_ends[None, :-1]).astype(jnp.int32), axis=1)
    live_rows = (positions < run_ends[-2]).astype(jnp.float32)
    return (segment_ids, live_rows)


def earlier_ids(segment_ids, offset):
    filler = jnp.full((offset,), -1, dtype=jnp.int32)
    return jnp.concatenate([filler, segment_ids[:-offset]])


def normalize(values, gain_vec):
    scale = lax.rsqrt(jnp.mean(values * values, axis=1, keepdims=True) + EPSILON)
    return values * scale * gain_vec


def convolve(linear_out, kernel, shift_vec, segment_ids):
    summed = linear_out * kernel[0] + shift_vec
    for offset in range(1, kernel.shape[0]):
        shifted = jnp.concatenate(
            [jnp.zeros((offset, linear_out.shape[1]), linear_out.dtype), linear_out[:-offset]],
            axis=0,
        )
        same_seq = (earlier_ids(segment_ids, offset) == segment_ids).astype(linear_out.dtype)
        summed = summed + kernel[offset] * shifted * same_seq[:, None]
    return summed


def combine_pairs(earlier_pair, later_pair):
    return (earlier_pair[0] * later_pair[0], later_pair[0] * earlier_pair[1] + later_pair[1])


def recurrence(rate_pre, input_pre, inflow, decay_vec, segment_ids):
    rate_gate = jax.nn.sigmoid(rate_pre)
    opened = jax.nn.sigmoid(input_pre)
    log_keep = -RATE_SCALE * rate_gate * jax.nn.softplus(-decay_vec)
    factor = jnp.exp(log_keep)
    weight_in = jnp.sqrt(-jnp.expm1(2.0 * log_keep))
    same_run = (earlier_ids(segment_ids, 1) == segment_ids).astype(factor.dtype)
    carried, states = lax.associative_scan(
        combine_pairs, (factor * same_run[:, None], weight_in * opened * inflow), axis=0
    )
    return states


def gated_gelu(gate_vals, up_vals):
    return jax.nn.gelu(gate_vals) * up_vals


def product(left, right):
    return jnp.dot(left, right, preferred_element_type=jnp.float32)


def contract(left, right):
    return jnp.einsum("ti,tj->ij", left, right, preferred_element_type=jnp.float32)


def back_dot(grad_vals, weight):
    return jnp.einsum("tj,ij->ti", grad_vals, weight, preferred_element_type=jnp.float32)


def blocked(values, weight):
    row_count = values.shape[0]
    size = weight.shape[1]
    heads = weight.shape[0] // size
    return jnp.einsum(
        "thj,hjk->thk",
        values.reshape(row_count, heads, size),
        weight.reshape(heads, size, size),
        preferred_element_type=jnp.float32,
    ).reshape(row_count, heads * size)


def block_terms(values, grad_vals, size):
    row_count = values.shape[0]
    heads = values.shape[1] // size
    terms = jnp.einsum(
        "thj,thk->hjk",
        values.reshape(row_count, heads, size),
        grad_vals.reshape(row_count, heads, size),
        preferred_element_type=jnp.float32,
    )
    return terms.reshape(heads * size, size)


def block_back(grad_vals, weight):
    row_count = grad_vals.shape[0]
    size = weight.shape[1]
    heads = weight.shape[0] // size
    return jnp.einsum(
        "thk,hjk->thj",
        grad_vals.reshape(row_count, heads, size),
        weight.reshape(heads, size, size),
        preferred_element_type=jnp.float32,
    ).reshape(row_count, heads * size)


def per_device(
    tokens,
    lengths,
    cotangent,
    norm1_gain,
    gate_in,
    linear_in,
    conv_kernel,
    conv_bias,
    rate_weight,
    rate_bias,
    input_weight,
    input_bias,
    decay_param,
    out_proj,
    norm2_gain,
    mlp_gate,
    mlp_up,
    mlp_down,
):
    row_count = tokens.shape[0]
    segment_ids, live_rows = layout(lengths[0], row_count)
    live_col = live_rows[:, None]
    mixer_full = (
        lax.all_gather(norm1_gain, "shard", axis=0, tiled=True),
        lax.all_gather(gate_in, "shard", axis=0, tiled=True),
        lax.all_gather(linear_in, "shard", axis=0, tiled=True),
        lax.all_gather(conv_kernel, "shard", axis=1, tiled=True),
        lax.all_gather(conv_bias, "shard", axis=0, tiled=True),
        lax.all_gather(rate_weight, "shard", axis=0, tiled=True),
        lax.all_gather(rate_bias, "shard", axis=0, tiled=True),
        lax.all_gather(input_weight, "shard", axis=0, tiled=True),
        lax.all_gather(input_bias, "shard", axis=0, tiled=True),
        lax.all_gather(decay_param, "shard", axis=0, tiled=True),
        lax.all_gather(out_proj, "shard", axis=0, tiled=True),
    )
    gain_first = mixer_full[0].astype(jnp.float32)
    kernel_full = mixer_full[3].astype(jnp.float32)
    kernel_shift = mixer_full[4].astype(jnp.float32)
    rate_shift = mixer_full[6].astype(jnp.float32)
    input_shift = mixer_full[8].astype(jnp.float32)
    decay_full = mixer_full[9].astype(jnp.float32)
    block_size = mixer_full[5].shape[1]
    masked_in = tokens.astype(jnp.float32) * live_col
    normed_low = normalize(masked_in, gain_first).astype(jnp.bfloat16)
    gate_pre = product(normed_low, mixer_full[1])
    linear_out = product(normed_low, mixer_full[2])
    gate_act = jax.nn.gelu(gate_pre)
    conv_out = convolve(linear_out, kernel_full, kernel_shift, segment_ids)
    conv_low = conv_out.astype(jnp.bfloat16)
    rate_pre = blocked(conv_low, mixer_full[5]) + rate_shift
    input_pre = blocked(conv_low, mixer_full[7]) + input_shift
    states = recurrence(rate_pre, input_pre, conv_out, decay_full, segment_ids)
    merged_low = (gate_act * states).astype(jnp.bfloat16)
    middle = masked_in + product(merged_low, mixer_full[10])
    mlp_full = (
        lax.all_gather(norm2_gain, "shard", axis=0, tiled=True),
        lax.all_gather(mlp_gate, "shard", axis=0, tiled=True),
        lax.all_gather(mlp_up, "shard", axis=0, tiled=True),
        lax.all_gather(mlp_down, "shard", axis=0, tiled=True),
    )
    gain_second = mlp_full[0].astype(jnp.float32)
    normed_two = normalize(middle, gain_second).astype(jnp.bfloat16)
    gate_mlp = product(normed_two, mlp_full[1])
    up_mlp = product(normed_two, mlp_full[2])
    hidden_low = gated_gelu(gate_mlp, up_mlp).astype(jnp.bfloat16)
    mixed_out = ((middle + product(hidden_low, mlp_full[3])) * live_col).astype(jnp.bfloat16)
    grad_out = cotangent.astype(jnp.float32) * live_col
    grad_down = grad_out.astype(jnp.bfloat16)
    again_mlp = (
        lax.all_gather(mlp_gate, "shard", axis=0, tiled=True),
        lax.all_gather(mlp_up, "shard", axis=0, tiled=True),
        lax.all_gather(mlp_down, "shard", axis=0, tiled=True),
    )
    term_down = contract(hidden_low, grad_down)
    part_down = lax.psum_scatter(
        term_down.astype(jnp.bfloat16), "shard", scatter_dimension=0, tiled=True
    ).astype(jnp.float32)
    grad_hidden = back_dot(grad_down, again_mlp[2])
    unused_val, hidden_back = jax.vjp(gated_gelu, gate_mlp, up_mlp)
    grad_gate_mlp, grad_up_mlp = hidden_back(grad_hidden)
    gate_mlp_low = grad_gate_mlp.astype(jnp.bfloat16)
    up_mlp_low = grad_up_mlp.astype(jnp.bfloat16)
    term_gate_mlp = contract(normed_two, gate_mlp_low)
    term_up_mlp = contract(normed_two, up_mlp_low)
    grad_normed_two = back_dot(gate_mlp_low, again_mlp[0]) + back_dot(up_mlp_low, again_mlp[1])
    unused_two, second_back = jax.vjp(normalize, middle, gain_second)
    grad_middle_norm, term_gain_two = second_back(grad_normed_two)
    parts_mlp = (
        lax.psum_scatter(
            term_gain_two.astype(jnp.bfloat16), "shard", scatter_dimension=0, tiled=True
        ).astype(jnp.float32),
        lax.psum_scatter(
            term_gate_mlp.astype(jnp.bfloat16), "shard", scatter_dimension=0, tiled=True
        ).astype(jnp.float32),
        lax.psum_scatter(
            term_up_mlp.astype(jnp.bfloat16), "shard", scatter_dimension=0, tiled=True
        ).astype(jnp.float32),
    )
    grad_middle = grad_out + grad_middle_norm
    grad_mix_low = grad_middle.astype(jnp.bfloat16)
    again_mixer = (
        lax.all_gather(gate_in, "shard", axis=0, tiled=True),
        lax.all_gather(linear_in, "shard", axis=0, tiled=True),
        lax.all_gather(rate_weight, "shard", axis=0, tiled=True),
        lax.all_gather(input_weight, "shard", axis=0, tiled=True),
        lax.all_gather(out_proj, "shard", axis=0, tiled=True),
    )
    term_out = contract(merged_low, grad_mix_low)
    grad_merged = back_dot(grad_mix_low, again_mixer[4])
    grad_states = grad_merged * gate_act
    unused_three, gelu_back = jax.vjp(jax.nn.gelu, gate_pre)
    gate_low = gelu_back(grad_merged * states)[0].astype(jnp.bfloat16)
    unused_four, scan_back = jax.vjp(
        partial(recurrence, segment_ids=segment_ids), rate_pre, input_pre, conv_out, decay_full
    )
    grad_rate, grad_input, grad_flow, term_decay = scan_back(grad_states)
    rate_low = grad_rate.astype(jnp.bfloat16)
    input_low = grad_input.astype(jnp.bfloat16)
    term_rate = block_terms(conv_low, rate_low, block_size)
    term_input = block_terms(conv_low, input_low, block_size)
    term_rate_shift = jnp.sum(rate_low.astype(jnp.float32), axis=0)
    term_input_shift = jnp.sum(input_low.astype(jnp.float32), axis=0)
    grad_conv = (
        grad_flow + block_back(rate_low, again_mixer[2]) + block_back(input_low, again_mixer[3])
    )
    unused_five, conv_back = jax.vjp(
        partial(convolve, segment_ids=segment_ids), linear_out, kernel_full, kernel_shift
    )
    grad_linear, term_kernel, term_kernel_shift = conv_back(grad_conv)
    linear_low = grad_linear.astype(jnp.bfloat16)
    term_gate_in = contract(normed_low, gate_low)
    term_linear = contract(normed_low, linear_low)
    grad_normed = back_dot(gate_low, again_mixer[0]) + back_dot(linear_low, again_mixer[1])
    unused_six, first_back = jax.vjp(normalize, masked_in, gain_first)
    grad_masked, term_gain_one = first_back(grad_normed)
    grad_tokens = ((grad_middle + grad_masked) * live_col).astype(jnp.bfloat16)
    small_terms = (
        term_gain_one,
        term_kernel,
        term_kernel_shift,
        term_rate,
        term_rate_shift,
        term_input,
        term_input_shift,
        term_decay,
    )
    placed = tuple((term for term in small_terms))
    mixer_terms = (
        placed[0],
        term_gate_in,
        term_linear,
        placed[1],
        placed[2],
        placed[3],
        placed[4],
        placed[5],
        placed[6],
        placed[7],
        term_out,
    )
    parts_mixer = (
        lax.psum_scatter(
            mixer_terms[0].astype(jnp.bfloat16), "shard", scatter_dimension=0, tiled=True
        ).astype(jnp.float32),
        lax.psum_scatter(
            mixer_terms[1].astype(jnp.bfloat16), "shard", scatter_dimension=0, tiled=True
        ).astype(jnp.float32),
        lax.psum_scatter(
            mixer_terms[2].astype(jnp.bfloat16), "shard", scatter_dimension=0, tiled=True
        ).astype(jnp.float32),
        lax.psum_scatter(
            mixer_terms[3].astype(jnp.bfloat16), "shard", scatter_dimension=1, tiled=True
        ).astype(jnp.float32),
        lax.psum_scatter(
            mixer_terms[4].astype(jnp.bfloat16), "shard", scatter_dimension=0, tiled=True
        ).astype(jnp.float32),
        lax.psum_scatter(
            mixer_terms[5].astype(jnp.bfloat16), "shard", scatter_dimension=0, tiled=True
        ).astype(jnp.float32),
        lax.psum_scatter(
            mixer_terms[6].astype(jnp.bfloat16), "shard", scatter_dimension=0, tiled=True
        ).astype(jnp.float32),
        lax.psum_scatter(
            mixer_terms[7].astype(jnp.bfloat16), "shard", scatter_dimension=0, tiled=True
        ).astype(jnp.float32),
        lax.psum_scatter(
            mixer_terms[8].astype(jnp.bfloat16), "shard", scatter_dimension=0, tiled=True
        ).astype(jnp.float32),
        lax.psum_scatter(
            mixer_terms[9].astype(jnp.bfloat16), "shard", scatter_dimension=0, tiled=True
        ).astype(jnp.float32),
        lax.psum_scatter(
            mixer_terms[10].astype(jnp.bfloat16), "shard", scatter_dimension=0, tiled=True
        ).astype(jnp.float32),
    )
    shard_parts = tuple(parts_mixer) + (parts_mlp[0], parts_mlp[1], parts_mlp[2], part_down)
    totals = jax.tree.map(
        lambda part: part.astype(jnp.float32), lax.psum(as_sent(shard_parts), "group")
    )
    return (mixed_out, grad_tokens) + tuple(totals)


def solution(mesh):
    placed = (
        P(("group", "shard"), None),
        P(("group", "shard"), None),
        P(("group", "shard"), None),
        P("shard"),
        P("shard", None),
        P("shard", None),
        P(None, "shard"),
        P("shard"),
        P("shard", None),
        P("shard"),
        P("shard", None),
        P("shard"),
        P("shard"),
        P("shard", None),
        P("shard"),
        P("shard", None),
        P("shard", None),
        P("shard", None),
    )
    return jax.shard_map(
        per_device,
        mesh=mesh,
        in_specs=placed,
        out_specs=(
            P(("group", "shard"), None),
            P(("group", "shard"), None),
            P("shard"),
            P("shard", None),
            P("shard", None),
            P(None, "shard"),
            P("shard"),
            P("shard", None),
            P("shard"),
            P("shard", None),
            P("shard"),
            P("shard"),
            P("shard", None),
            P("shard"),
            P("shard", None),
            P("shard", None),
            P("shard", None),
        ),
        check_vma=False,
    )
```

profile of v0, /device:TPU:0, one launch (start us, length us, event | category | flops | bytes accessed | tf_op | source)
XLA Modules:
  0.0 4428.3 jit_solution(15484600515460773507)
XLA Ops:
  12.1 22.4 all-gather
  36.8 34.1 all-reduce.88
  70.9 30.8 all-gather.1
  101.8 36.2 all-gather.3
  139.5 34.1 all-gather.2
  175.2 18.5 all-gather.4
  200.5 5.6 fusion.58
  349.3 4.8 pad.307
  356.9 4.9 pad.306
  361.8 8.9 multiply_convert_fusion.2
  370.6 132.6 %all-gather.16.cloned.1.call-done = bf16[2560,2048]{1,0:T(8,128)(2,1)} async-done(((bf16[320,2048]{1,0:T(8,128)(2,1)}), bf16[2560,2048]{1,0:T(8,128)(2,1)}) %all-gather.16.cloned.1.call-update) | async-done | bytes 10485776 | tf_op jit(solution)/shard_map/all_gather | solution.py:149
  503.2 5.8 multiply_reduce_fusion.9
  511.0 472.2 %all-gather.18.cloned.1.call-done = bf16[2048,6144]{1,0:T(8,128)(2,1)} async-done(((bf16[256,6144]{1,0:T(8,128)(2,1)}), bf16[2048,6144]{1,0:T(8,128)(2,1)}) %all-gather.18.cloned.1.call-update) | async-done | bytes 25165840 | tf_op jit(solution)/shard_map/all_gather | solution.py:172
  983.2 13.7 fusion.89
  997.0 468.1 %all-gather.20.cloned.1.call-done = bf16[2048,6144]{1,0:T(8,128)(2,1)} async-done(((bf16[256,6144]{1,0:T(8,128)(2,1)}), bf16[2048,6144]{1,0:T(8,128)(2,1)}) %all-gather.20.cloned.1.call-update) | async-done | bytes 25165840 | tf_op jit(solution)/shard_map/all_gather | solution.py:173
  1465.1 13.7 fusion.90
  1478.8 468.1 %all-gather.22.cloned.1.call-done = bf16[6144,2048]{1,0:T(8,128)(2,1)} async-done(((bf16[768,2048]{1,0:T(8,128)(2,1)}), bf16[6144,2048]{1,0:T(8,128)(2,1)}) %all-gather.22.cloned.1.call-update) | async-done | bytes 25165840 | tf_op jit(solution)/shard_map/all_gather | solution.py:174
  1946.9 17.4 multiply_convert_fusion
  1964.3 14.3 fusion.91
  1978.6 15.7 multiply_reduce_fusion.5
  1997.6 9.1 fusion.27
  2141.3 5.0 pad.352
  2146.2 4.9 pad.353
  2151.1 4.9 pad.371
  2160.9 5.0 pad.310
  2165.9 4.9 pad.354
  2170.9 6.3 multiply_reduce_fusion
  2201.3 5.2 multiply_reduce_fusion.4
  2213.6 5.8 convolution_convert_fusion.4
  2220.8 5.5 convolution_convert_fusion.3
  2227.4 5.6 convolution_convert_fusion.5
  2234.6 11.8 convolution_convert_fusion.2
  2247.9 12.0 convolution_convert_fusion.1
  2261.4 12.1 convolution_convert_fusion
  2276.5 55.3 %reduce-scatter.32.cloned.1.call-done = bf16[320,160]{1,0:T(8,128)(2,1)} async-done(((bf16[2560,160]{1,0:T(8,128)(2,1)}), bf16[320,160]{1,0:T(8,128)(2,1)}) %reduce-scatter.32.cloned.1.call-update) | async-done | bytes 102416
  2333.6 179.0 %reduce-scatter.18.cloned.1.call-done = bf16[256,2560]{1,0:T(8,128)(2,1)} async-done(((bf16[2048,2560]{1,0:T(8,128)(2,1)}), bf16[256,2560]{1,0:T(8,128)(2,1)}) %reduce-scatter.18.cloned.1.call-update) | async-done | bytes 1310736 | tf_op jit(solution)/shard_map/reduce_scatter | solution.py:283
  2512.5 180.6 %reduce-scatter.20.cloned.1.call-done = bf16[320,2048]{1,0:T(8,128)(2,1)} async-done(((bf16[2560,2048]{1,0:T(8,128)(2,1)}), bf16[320,2048]{1,0:T(8,128)(2,1)}) %reduce-scatter.20.cloned.1.call-update) | async-done | bytes 1310736 | tf_op jit(solution)/shard_map/reduce_scatter | solution.py:307
  2693.1 180.8 %reduce-scatter.16.cloned.1.call-done = bf16[256,2560]{1,0:T(8,128)(2,1)} async-done(((bf16[2048,2560]{1,0:T(8,128)(2,1)}), bf16[256,2560]{1,0:T(8,128)(2,1)}) %reduce-scatter.16.cloned.1.call-update) | async-done | bytes 1310736 | tf_op jit(solution)/shard_map/reduce_scatter | solution.py:280
  2873.9 406.5 %reduce-scatter.22.cloned.1.call-done = bf16[256,6144]{1,0:T(8,128)(2,1)} async-done(((bf16[2048,6144]{1,0:T(8,128)(2,1)}), bf16[256,6144]{1,0:T(8,128)(2,1)}) %reduce-scatter.22.cloned.1.call-update) | async-done | bytes 3145744 | tf_op jit(solution)/shard_map/reduce_scatter | solution.py:207
  3280.5 406.6 %reduce-scatter.24.cloned.1.call-done = bf16[256,6144]{1,0:T(8,128)(2,1)} async-done(((bf16[2048,6144]{1,0:T(8,128)(2,1)}), bf16[256,6144]{1,0:T(8,128)(2,1)}) %reduce-scatter.24.cloned.1.call-update) | async-done | bytes 3145744 | tf_op jit(solution)/shard_map/reduce_scatter | solution.py:210
  3687.1 406.4 %reduce-scatter.26.cloned.1.call-done = bf16[768,2048]{1,0:T(8,128)(2,1)} async-done(((bf16[6144,2048]{1,0:T(8,128)(2,1)}), bf16[768,2048]{1,0:T(8,128)(2,1)}) %reduce-scatter.26.cloned.1.call-update) | async-done | bytes 3145744 | tf_op jit(solution)/shard_map/reduce_scatter | solution.py:190
  4094.8 7.5 fusion.92
  4102.4 8.6 multiply_reduce_fusion.6
  4111.0 35.6 all-reduce.87
  4149.7 12.5 fusion.8
  4163.2 5.8 all-reduce.89
  4173.0 229.2 %all-reduce.93.cloned.1.call-done = (bf16[256,2560]{1,0:T(8,128)(2,1)}, bf16[256,2560]{1,0:T(8,128)(2,1)}, bf16[320,160]{0,1:T(8,128)(2,1)}, bf16[320,160]{0,1:T...) async-done(((bf16[256,2560]{1,0:T(8,128)(2,1)}, bf16[256,2560]{1,0:T(8,128)(2,1)}, ...) | async-done | bytes 13574160 | tf_op jit(solution)/shard_map/psum | solution.py:313
  4402.2 5.5 convert_element_type.278
  (469 shorter events, 371.1 us)
Async XLA Ops:
  7.2 193.3 %all-gather.14.cloned.1.call-start = ((), (), s32[]{:S(2)}) async-start(), calls=%async_computation.10 | async-start | bytes 11796480 | tf_op jit(solution)/shard_map/all_gather | solution.py:141
  7.9 353.8 %all-gather.12.cloned.1.call-start = ((), (), s32[]{:S(2)}) async-start(), calls=%async_computation.9 | async-start | bytes 11796480 | tf_op jit(solution)/shard_map/all_gather | solution.py:140
  8.7 494.5 %all-gather.16.cloned.1.call-start = ((), (), s32[]{:S(2)}) async-start(), calls=%async_computation.11 | async-start | bytes 11796480 | tf_op jit(solution)/shard_map/all_gather | solution.py:149
  9.4 973.8 %all-gather.18.cloned.1.call-start = ((), (), s32[]{:S(2)}) async-start(), calls=%async_computation.12 | async-start | bytes 28311552 | tf_op jit(solution)/shard_map/all_gather | solution.py:172
  10.0 1455.1 %all-gather.20.cloned.1.call-start = ((), (), s32[]{:S(2)}) async-start(), calls=%async_computation.13 | async-start | bytes 28311552 | tf_op jit(solution)/shard_map/all_gather | solution.py:173
  10.6 23.9 copy-start.84
  10.6 25.1 copy-start.85
  10.6 25.4 copy-start.86
  10.6 25.6 copy-start.87
  10.6 25.9 copy-start.88
  10.6 60.2 %copy-start.83 = (bf16[4,320]{1,0:T(4,128)(2,1)S(1)}, bf16[4,320]{1,0:T(4,128)(2,1)}, u32[]{:S(2)}) copy-start(bf16[4,320]{1,0:T(4,128)(2,1)} %param.24) | copy-start | bytes 7684
  10.7 91.1 %copy-start.53 = (bf16[320,160]{0,1:T(8,128)(2,1)S(1)}, bf16[320,160]{0,1:T(8,128)(2,1)}, u32[]{:S(2)}) copy-start(bf16[320,160]{0,1:T(8,128)(2,1)} %param.28) | copy-start | bytes 307204
  10.7 1936.2 %all-gather.22.cloned.1.call-start = ((), (), s32[]{:S(2)}) async-start(), calls=%async_computation.14 | async-start | bytes 28311552 | tf_op jit(solution)/shard_map/all_gather | solution.py:174
  11.2 2263.6 %reduce-scatter.30.cloned.1.call-start = ((), (), s32[]{:S(2)}) async-start(), calls=%async_computation.22 | async-start | bytes 1474560
  70.9 125.2 %copy-start.73 = (bf16[2560]{0:T(1024)(128)(2,1)}, bf16[2560]{0:T(1024)(128)(2,1)S(1)}, u32[]{:S(2)}) copy-start(bf16[2560]{0:T(1024)(128)(2,1)S(1)} %get-tuple-element.34) | copy-start | bytes 15364
  173.6 21.6 copy-start
  175.2 44.6 %copy-start.43 = (f32[2560]{0:T(1024)}, f32[2560]{0:T(1024)S(1)}, u32[]{:S(2)}) copy-start(f32[2560]{0:T(1024)S(1)} %convert_element_type.237) | copy-start | bytes 30724
  195.0 11.1 copy-start.57
  195.2 10.9 copy-start.59
  195.2 10.9 copy-start.61
  195.2 10.9 copy-start.63
  195.2 10.9 copy-start.65
  195.5 10.5 copy-start.67
  196.1 10.1 copy-start.79
  196.1 10.1 copy-start.81
  196.1 23.7 copy-start.76
  196.1 23.7 copy-start.45
  269.7 25.6 copy-start.40
  296.8 9.9 copy-start.47
  1997.3 9.5 copy-start.17
  2045.0 21.7 copy-start.41
  2056.5 23.3 slice-start.4
  2079.8 17.5 slice-start.3
  2103.3 12.1 slice-start.2
  2200.7 131.2 %reduce-scatter.32.cloned.1.call-start = ((), (), s32[]{:S(2)}) async-start(), calls=%async_computation.23 | async-start | bytes 1474560
  2208.3 304.3 %reduce-scatter.18.cloned.1.call-start = ((), (), s32[]{:S(2)}) async-start(), calls=%async_computation.16 | async-start | bytes 11796480 | tf_op jit(solution)/shard_map/reduce_scatter | solution.py:283
  2219.4 473.7 %reduce-scatter.20.cloned.1.call-start = ((), (), s32[]{:S(2)}) async-start(), calls=%async_computation.17 | async-start | bytes 11796480 | tf_op jit(solution)/shard_map/reduce_scatter | solution.py:307
  2226.3 647.6 %reduce-scatter.16.cloned.1.call-start = ((), (), s32[]{:S(2)}) async-start(), calls=%async_computation.15 | async-start | bytes 11796480 | tf_op jit(solution)/shard_map/reduce_scatter | solution.py:280
  2233.1 1047.4 %reduce-scatter.22.cloned.1.call-start = ((), (), s32[]{:S(2)}) async-start(), calls=%async_computation.18 | async-start | bytes 28311552 | tf_op jit(solution)/shard_map/reduce_scatter | solution.py:207
  2246.5 1440.6 %reduce-scatter.24.cloned.1.call-start = ((), (), s32[]{:S(2)}) async-start(), calls=%async_computation.19 | async-start | bytes 28311552 | tf_op jit(solution)/shard_map/reduce_scatter | solution.py:210
  2259.9 1833.7 %reduce-scatter.26.cloned.1.call-start = ((), (), s32[]{:S(2)}) async-start(), calls=%async_computation.20 | async-start | bytes 28311552 | tf_op jit(solution)/shard_map/reduce_scatter | solution.py:190
  2273.5 1888.8 %reduce-scatter.28.cloned.1.call-start = ((), (), s32[]{:S(2)}) async-start(), calls=%async_computation.21 | async-start | bytes 737280
  2274.8 2127.4 %all-reduce.93.cloned.1.call-start = ((), (), s32[]{:S(2)}) async-start(), calls=%async_computation.24 | async-start | bytes 27230208 | tf_op jit(solution)/shard_map/psum | solution.py:313
  4102.3 8.7 copy-start.71
  4102.3 8.7 copy-start.72
  4102.3 8.7 copy-start.75
  4102.4 44.8 %copy-start.91 = (f32[128]{0:T(128)S(1)}, f32[128]{0:T(128)}, u32[]{:S(2)}) copy-start(f32[128]{0:T(128)} %copy-done.90) | copy-start | bytes 1540
  4102.4 44.8 %copy-start.19 = (f32[128,2048]{1,0:T(8,128)S(1)}, f32[128,2048]{1,0:T(8,128)}, u32[]{:S(2)}) copy-start(f32[128,2048]{1,0:T(8,128)} %copy-done.17) | copy-start | bytes 3145732
  (68 other events, 175.7 us)
Sparse Core Ops, SparseCore 0:
  10.2 190.2 all-gather.13
  202.7 149.2 all-gather.11
  354.1 149.0 all-gather.15
  504.6 478.6 all-gather.17
  984.6 480.3 all-gather.19
  1466.5 480.3 all-gather.21
  2200.8 64.2 reduce-scatter.29
  2268.5 63.3 reduce-scatter.31
  2335.5 177.0 reduce-scatter.17
  2516.0 177.1 reduce-scatter.19
  2696.7 177.1 reduce-scatter.15
  2877.7 402.7 reduce-scatter.21
  3284.3 402.6 reduce-scatter.23
  3690.8 402.6 reduce-scatter.25
  4097.2 61.2 reduce-scatter.27
  4163.1 239.0 all-reduce.92
where the time goes:
time: 4440 us; the launch traced here: 4430 us
  waiting for transfers between devices  3590 us (81%)
  local copies, waits for them, and re-layouts  266 us (6%)
  blocking collectives  218 us (5%)
  matrix products  202 us (5%)
  other arithmetic  131 us (3%)
    all_gather x1, waiting for transfers between devices, per_device(): lax.all_gather(mlp_gate, 'shard', axis=0, tiled=True)  472 us
    all_gather x1, waiting for transfers between devices, per_device(): lax.all_gather(mlp_down, 'shard', axis=0, tiled=True)  468 us
    all_gather x1, waiting for transfers between devices, per_device(): lax.all_gather(mlp_up, 'shard', axis=0, tiled=True)  468 us
    reduce_scatter x1, waiting for transfers between devices, per_device(): lax.psum_scatter(term_up_mlp.astype(jnp.bfloat16), 'shard', scatter_dimen...  407 us
    reduce_scatter x1, waiting for transfers between devices, per_device(): lax.psum_scatter(term_gate_mlp.astype(jnp.bfloat16), 'shard', scatter_dim...  407 us
    reduce_scatter x1, waiting for transfers between devices, per_device(): lax.psum_scatter(term_down.astype(jnp.bfloat16), 'shard', scatter_dimensi...  406 us
    psum x1, waiting for transfers between devices, per_device(): lax.psum(as_sent(shard_parts), 'group')  229 us
    reduce_scatter x1, waiting for transfers between devices, per_device(): lax.psum_scatter(mixer_terms[1].astype(jnp.bfloat16), 'shard', scatter_di...  181 us
  transfers between devices with their start and end apart: 16, of which 13 were waited for; matrix products, arithmetic and copies ran while one was open for 7% of the time, Pallas kernels for 0%

commit v1 on v0

--- a/solution.py
+++ b/solution.py
@@ -3,10 +3,304 @@
 import jax
 import jax.numpy as jnp
 from jax import lax
+from jax.experimental import pallas as pl
+from jax.experimental.pallas import tpu as pltpu
 from jax.sharding import PartitionSpec as P
 
+FAST_MESH = (4, 8)
 RATE_SCALE = 8.0
 EPSILON = 1e-06
+F32 = jnp.float32
+BF16 = jnp.bfloat16
+GELU_C = 0.7978845608028654
+GELU_K = 0.044715
+
+
+def positions_in_run(counts, row_count):
+    first = counts[0]
+    second = first + counts[1]
+    third = second + counts[2]
+    rows = lax.broadcasted_iota(jnp.int32, (row_count, 1), 0)
+    start = jnp.where(rows >= first, first, 0)
+    start = jnp.where(rows >= second, second, start)
+    start = jnp.where(rows >= third, third, start)
+    return rows - start, (rows < third).astype(F32)
+
+
+def gelu_parts(x):
+    t = jnp.tanh(GELU_C * (x + GELU_K * x * x * x))
+    value = 0.5 * x * (1.0 + t)
+    slope = 0.5 * (1.0 + t) + 0.5 * x * (1.0 - t * t) * GELU_C * (1.0 + 3.0 * GELU_K * x * x)
+    return value, slope
+
+
+def gelu_value(x):
+    return 0.5 * x * (1.0 + jnp.tanh(GELU_C * (x + GELU_K * x * x * x)))
+
+
+def sigmoid(x):
+    return 0.5 * (1.0 + jnp.tanh(0.5 * x))
+
+
+def one_less_exp(z):
+    series = 1.0 - z * (1.0 / 7.0)
+    for k in (6.0, 5.0, 4.0, 3.0, 2.0):
+        series = 1.0 - z * (1.0 / k) * series
+    return jnp.where(z < 0.35, z * series, 1.0 - jnp.exp(-z))
+
+
+def softplus_neg(x):
+    return jnp.maximum(-x, 0.0) + jnp.log1p(jnp.exp(-jnp.abs(x)))
+
+
+def mm(a, b):
+    return jnp.dot(a, b, preferred_element_type=F32)
+
+
+def mm_nt(a, b):
+    return lax.dot_general(a, b, (((1,), (1,)), ((), ())), preferred_element_type=F32)
+
+
+def mm_tn(a, b):
+    return lax.dot_general(a, b, (((0,), (0,)), ((), ())), preferred_element_type=F32)
+
+
+def roll_rows(x, n):
+    return pltpu.roll(x, n % x.shape[0], 0)
+
+
+def conv_rows(linear, kernel, bias, masks):
+    out = linear * kernel[0:1] + bias
+    for k in range(1, 4):
+        out = out + kernel[k : k + 1] * (roll_rows(linear, k) * masks[k - 1])
+    return out
+
+
+def decay_terms(rate_pre, decay):
+    rate = sigmoid(rate_pre)
+    keep = RATE_SCALE * rate * softplus_neg(decay)
+    return rate, jnp.exp(-keep), jnp.sqrt(one_less_exp(2.0 * keep))
+
+
+def mixer_forward_kernel(pos_ref, gate_ref, linear_ref, ck_ref, vec_ref, rw_ref, iw_ref,
+                         merged_ref, rate_ref, input_ref, state_ref):
+    pos = pos_ref[...]
+    masks = [(pos >= k).astype(F32) for k in (1, 2, 3)]
+    linear = linear_ref[...]
+    conv = conv_rows(linear, ck_ref[...], vec_ref[0:1], masks)
+    low = conv.astype(BF16)
+    rate_pre = mm(low, rw_ref[...]) + vec_ref[1:2]
+    input_pre = mm(low, iw_ref[...]) + vec_ref[2:3]
+    _, a, weight_in = decay_terms(rate_pre, vec_ref[3:4])
+    mult = a * masks[0]
+    total = weight_in * sigmoid(input_pre) * conv
+    step = 1
+    rows = total.shape[0]
+    while step < rows:
+        total = total + mult * roll_rows(total, step)
+        if 2 * step < rows:
+            mult = mult * roll_rows(mult, step)
+        step *= 2
+    rate_ref[...] = rate_pre
+    input_ref[...] = input_pre
+    state_ref[...] = total
+    merged_ref[...] = (gelu_value(gate_ref[...]) * total).astype(BF16)
+
+
+def mixer_backward_kernel(pos_ref, gm_ref, gate_ref, linear_ref, rate_ref, input_ref, state_ref,
+                          ck_ref, vec_ref, rw_ref, iw_ref,
+                          gg_ref, gl_ref, small_ref, rate_out_ref, input_out_ref, tr_ref, ti_ref):
+    @pl.when(pl.program_id(0) == 0)
+    def _():
+        small_ref[...] = jnp.zeros_like(small_ref)
+        tr_ref[...] = jnp.zeros_like(tr_ref)
+        ti_ref[...] = jnp.zeros_like(ti_ref)
+
+    pos = pos_ref[...]
+    rows = pos.shape[0]
+    masks = [(pos >= k).astype(F32) for k in (1, 2, 3)]
+    index = lax.broadcasted_iota(jnp.int32, pos.shape, 0)
+    later = [
+        jnp.where(index < rows - k, roll_rows(masks[k - 1], -k), 0.0) for k in (1, 2, 3)
+    ]
+    linear = linear_ref[...]
+    kernel = ck_ref[...]
+    conv = conv_rows(linear, kernel, vec_ref[0:1], masks)
+    low = conv.astype(BF16)
+    input_gate = sigmoid(input_ref[...])
+    decay = vec_ref[3:4]
+    rate, a, weight_in = decay_terms(rate_ref[...], decay)
+    state = state_ref[...]
+    g_merged = gm_ref[...]
+    act, slope = gelu_parts(gate_ref[...])
+    gg_ref[...] = (g_merged * state * slope).astype(BF16)
+    lam = g_merged * act
+    mult = roll_rows(a, -1) * later[0]
+    step = 1
+    while step < rows:
+        lam = lam + mult * roll_rows(lam, -step)
+        if 2 * step < rows:
+            mult = mult * roll_rows(mult, -step)
+        step *= 2
+    g_a = lam * (roll_rows(state, 1) * masks[0])
+    opened = input_gate * conv
+    g_keep = g_a * a - lam * opened * (a * a) / weight_in
+    slow = RATE_SCALE * rate
+    g_rate = (g_keep * (-RATE_SCALE * softplus_neg(decay)) * (rate * (1.0 - rate))).astype(BF16)
+    g_decay = g_keep * slow * sigmoid(-decay)
+    flow = lam * weight_in
+    g_inp = (flow * conv * (input_gate * (1.0 - input_gate))).astype(BF16)
+    g_conv = flow * input_gate + mm_nt(g_rate, rw_ref[...]) + mm_nt(g_inp, iw_ref[...])
+    g_linear = g_conv * kernel[0:1]
+    sums = [jnp.sum(g_conv * linear, axis=0, keepdims=True)]
+    for k in (1, 2, 3):
+        g_linear = g_linear + kernel[k : k + 1] * (roll_rows(g_conv, -k) * later[k - 1])
+        sums.append(jnp.sum(g_conv * (roll_rows(linear, k) * masks[k - 1]), axis=0, keepdims=True))
+    gl_ref[...] = g_linear.astype(BF16)
+    sums.append(jnp.sum(g_conv, axis=0, keepdims=True))
+    sums.append(jnp.sum(g_rate.astype(F32), axis=0, keepdims=True))
+    sums.append(jnp.sum(g_inp.astype(F32), axis=0, keepdims=True))
+    sums.append(jnp.sum(g_decay, axis=0, keepdims=True))
+    small_ref[...] += jnp.concatenate(sums, axis=0)
+    tr_ref[...] += mm_tn(low, g_rate)
+    ti_ref[...] += mm_tn(low, g_inp)
+
+    @pl.when(pl.program_id(0) == pl.num_programs(0) - 1)
+    def _():
+        size = rate_out_ref.shape[1]
+        for h in range(rate_out_ref.shape[0] // size):
+            part = slice(h * size, (h + 1) * size)
+            rate_out_ref[part] = tr_ref[part, part].astype(BF16)
+            input_out_ref[part] = ti_ref[part, part].astype(BF16)
+
+
+def block_diagonal(weight):
+    size = weight.shape[1]
+    heads = weight.shape[0] // size
+    parts = []
+    for h in range(heads):
+        parts.append(
+            jnp.pad(weight[h * size : (h + 1) * size], ((0, 0), (h * size, (heads - 1 - h) * size)))
+        )
+    return jnp.concatenate(parts, axis=0)
+
+
+def per_device_split(
+    tokens, lengths, cotangent, norm1_gain, gate_in, linear_in, conv_kernel, conv_bias, rate_weight,
+    rate_bias, input_weight, input_bias, decay_param, out_proj, norm2_gain, mlp_gate, mlp_up, mlp_down,
+):
+    rows, width = tokens.shape
+    n_shard = lax.axis_size("shard")
+    size = rate_weight.shape[1]
+    chans = rate_weight.shape[0]
+    total_rows = rows * n_shard
+
+    def gather(x):
+        return lax.all_gather(x, "shard", axis=0, tiled=True)
+
+    def scatter(x):
+        return lax.psum_scatter(x.astype(BF16), "shard", scatter_dimension=0, tiled=True).astype(F32)
+
+    def columns(w):
+        return lax.all_to_all(w, "shard", split_axis=1, concat_axis=0, tiled=True)
+
+    pos, live = positions_in_run(lengths[0], rows)
+    gains = lax.all_gather(jnp.stack([norm1_gain, norm2_gain]), "shard", axis=1, tiled=True).astype(F32)
+    masked = tokens.astype(F32) * live
+    scale1 = lax.rsqrt(jnp.mean(masked * masked, axis=1, keepdims=True) + EPSILON)
+    normed = (masked * scale1 * gains[0:1]).astype(BF16)
+    sent = jnp.concatenate([normed, jnp.broadcast_to(pos.astype(BF16), (rows, 128))], axis=1)
+    got = gather(sent)
+    normed_all = got[:, :width]
+    pos_all = got[:, width : width + 1].astype(jnp.int32)
+    gate_w, linear_w = columns(gate_in), columns(linear_in)
+    mg_w, mu_w = columns(mlp_gate), columns(mlp_up)
+    gate_pre = mm(normed_all, gate_w)
+    linear_pre = mm(normed_all, linear_w)
+    vec = jnp.stack([conv_bias, rate_bias, input_bias, decay_param]).astype(F32)
+    ck = conv_kernel.astype(F32)
+    rate_bd, input_bd = block_diagonal(rate_weight), block_diagonal(input_weight)
+    row_spec = pl.BlockSpec((rows, chans), lambda i: (i, 0))
+    pos_spec = pl.BlockSpec((rows, 1), lambda i: (i, 0))
+
+    def whole(a):
+        return pl.BlockSpec(a.shape, lambda i: (0,) * a.ndim)
+
+    f_shape = jax.ShapeDtypeStruct((total_rows, chans), F32)
+    b_shape = jax.ShapeDtypeStruct((total_rows, chans), BF16)
+    merged, rate_pre, input_pre, state = pl.pallas_call(
+        mixer_forward_kernel,
+        grid=(n_shard,),
+        in_specs=[pos_spec, row_spec, row_spec, whole(ck), whole(vec), whole(rate_bd), whole(input_bd)],
+        out_specs=[row_spec] * 4,
+        out_shape=[b_shape, f_shape, f_shape, f_shape],
+        compiler_params=pltpu.CompilerParams(vmem_limit_bytes=32 * 2**20),
+        name="mixer_forward",
+    )(pos_all, gate_pre, linear_pre, ck, vec, rate_bd, input_bd)
+    middle = masked + scatter(mm(merged, out_proj))
+    scale2 = lax.rsqrt(jnp.mean(middle * middle, axis=1, keepdims=True) + EPSILON)
+    normed_two = gather((middle * scale2 * gains[1:2]).astype(BF16))
+    g_out = cotangent.astype(F32) * live
+    g_low = gather(g_out.astype(BF16))
+    gate_mlp = mm(normed_two, mg_w)
+    up_mlp = mm(normed_two, mu_w)
+    act, slope = gelu_parts(gate_mlp)
+    hidden = (act * up_mlp).astype(BF16)
+    mixed = ((middle + scatter(mm(hidden, mlp_down))) * live).astype(BF16)
+    term_down = mm_tn(hidden, g_low).astype(BF16)
+    g_hidden = mm_nt(g_low, mlp_down)
+    g_gate_mlp = (g_hidden * up_mlp * slope).astype(BF16)
+    g_up = (g_hidden * act).astype(BF16)
+    term_mg = mm_tn(normed_two, g_gate_mlp).astype(BF16)
+    term_mu = mm_tn(normed_two, g_up).astype(BF16)
+    g_normed_two = scatter(mm_nt(g_gate_mlp, mg_w) + mm_nt(g_up, mu_w))
+    e2 = g_normed_two * gains[1:2]
+    g_middle = (
+        g_out + scale2 * e2
+        - middle * (scale2 * scale2 * scale2) * jnp.mean(middle * e2, axis=1, keepdims=True)
+    )
+    gain2_term = jnp.sum(g_normed_two * middle * scale2, axis=0)
+    g_mix = gather(g_middle.astype(BF16))
+    term_out = mm_tn(merged, g_mix).astype(BF16)
+    g_merged = mm_nt(g_mix, out_proj)
+    small_shape = jax.ShapeDtypeStruct((8, chans), F32)
+    bd_shape = jax.ShapeDtypeStruct((chans, size), BF16)
+    g_gate, g_linear, small, tr, ti = pl.pallas_call(
+        mixer_backward_kernel,
+        grid=(n_shard,),
+        in_specs=[pos_spec] + [row_spec] * 6 + [whole(ck), whole(vec), whole(rate_bd), whole(input_bd)],
+        out_specs=[row_spec] * 2 + [whole(small_shape), whole(bd_shape), whole(bd_shape)],
+        out_shape=[b_shape, b_shape, small_shape, bd_shape, bd_shape],
+        scratch_shapes=[pltpu.VMEM((chans, chans), F32)] * 2,
+        compiler_params=pltpu.CompilerParams(vmem_limit_bytes=32 * 2**20),
+        name="mixer_backward",
+    )(pos_all, g_merged, gate_pre, linear_pre, rate_pre, input_pre, state, ck, vec, rate_bd, input_bd)
+    term_gi = mm_tn(normed_all, g_gate).astype(BF16)
+    term_li = mm_tn(normed_all, g_linear).astype(BF16)
+    g_normed = scatter(mm_nt(g_gate, gate_w) + mm_nt(g_linear, linear_w))
+    e1 = g_normed * gains[0:1]
+    g_masked = (
+        scale1 * e1
+        - masked * (scale1 * scale1 * scale1) * jnp.mean(masked * e1, axis=1, keepdims=True)
+    )
+    gain1_term = jnp.sum(g_normed * masked * scale1, axis=0)
+    grad_tokens = ((g_middle + g_masked) * live).astype(BF16)
+
+    def back_columns(t):
+        return lax.all_to_all(t, "shard", split_axis=0, concat_axis=1, tiled=True)
+
+    gain_terms = lax.psum_scatter(
+        jnp.stack([gain1_term, gain2_term]).astype(BF16), "shard", scatter_dimension=1, tiled=True
+    )
+    sums = lax.psum(
+        (gain_terms, back_columns(term_gi), back_columns(term_li), small.astype(BF16), tr, ti, term_out,
+         back_columns(term_mg), back_columns(term_mu), term_down), "group",
+    )
+    gain_s, gi_s, li_s, small_s, tr_s, ti_s, out_s, mg_s, mu_s, down_s = [s.astype(F32) for s in sums]
+    return (
+        mixed, grad_tokens, gain_s[0], gi_s, li_s, small_s[0:4], small_s[4], tr_s, small_s[5], ti_s,
+        small_s[6], small_s[7], out_s, gain_s[1], mg_s, mu_s, down_s,
+    )
 
 
 def as_sent(shard):
@@ -14,7 +308,9 @@
 
 
 def layout(counts, row_count):
-    run_ends = jnp.cumsum(counts)
+    first = counts[0]
+    second = first + counts[1]
+    run_ends = jnp.stack([first, second, second + counts[2], second + counts[2] + counts[3]])
     positions = jnp.arange(row_count, dtype=jnp.int32)
     segment_ids = jnp.sum((positions[:, None] >= run_ends[None, :-1]).astype(jnp.int32), axis=1)
     live_rows = (positions < run_ends[-2]).astype(jnp.float32)
@@ -112,7 +408,7 @@
     ).reshape(row_count, heads * size)
 
 
-def per_device(
+def per_device_general(
     tokens,
     lengths,
     cotangent,
@@ -336,8 +632,9 @@
         P("shard", None),
         P("shard", None),
     )
+    split_fits = FAST_MESH == tuple(mesh.shape[axis] for axis in ("group", "shard"))
     return jax.shard_map(
-        per_device,
+        per_device_split if split_fits else per_device_general,
         mesh=mesh,
         in_specs=placed,
         out_specs=(

time: 4440 us -> 1430 us (0.32)
  waiting for transfers between devices: 3590 us -> 1120 us
  local copies, waits for them, and re-layouts: 266 us -> 66 us
  blocking collectives: 218 us -> 28 us
  matrix products: 202 us -> 97.8 us
  other arithmetic: 131 us -> 32.4 us
    reduce_scatter x6 -> x4, waiting for transfers between devices: 1760 us -> 256 us  [scatter(): lax.psum_scatter(x.astype(BF16), 'shard', scatter_dimension=0, tiled=True)]
    all_gather x6 -> x4, waiting for transfers between devices: 1550 us -> 111 us  [gather(): return lax.all_gather(x, 'shard', axis=0, tiled=True)]
    all_to_all x0 -> x8, waiting for transfers between devices: none -> 467 us  [the longest x4 329 us: columns(): return lax.all_to_all(w, 'shard', split_axis=1, concat_axis=0, tiled=True)]
    pad x52 -> x0, local copies, waits for them, and re-layouts: 131 us -> none  [recurrence(): lax.associative_scan(combine_pairs, (factor * same_run[:, None], weight_i...]
    all_gather x5 -> x1, blocking collectives: 142 us -> 22.2 us  [per_device_split(): lax.all_gather(jnp.stack([norm1_gain, norm2_gain]), 'shard', axis=1, tile...]
    dot_general x24 -> x18, matrix products: 202 us -> 97.8 us  [the longest x6 34.9 us: mm_tn(): lax.dot_general(a, b, (((0,), (0,)), ((), ())), preferred_element_type=F32)]
    slice x53 -> x7, local copies, waits for them, and re-layouts: 93.8 us -> 4.36 us  [the longest x1 1.42 us: positions_in_run(): third = second + counts[2]]
    unnamed x2 -> x0, blocking collectives: 69.7 us -> none
  transfers between devices with their start and end apart: 16 -> 18, of which waited for: 13 -> 13; matrix products, arithmetic and copies ran while one was open for 7% -> 8% of each run, Pallas kernels for 0% -> 1%
where the time goes in v1:
time: 1430 us; the launch traced here: 1420 us
  waiting for transfers between devices  1120 us (78%)
  matrix products  97.8 us (7%)
  local copies, waits for them, and re-layouts  66 us (5%)
  starting transfers between devices  35.9 us (3%)
  other arithmetic  32.4 us (2%)
  blocking collectives  28 us (2%)
  Pallas kernels  21.5 us (2%)
  between operations  17.1 us (1%)
    all_to_all x4, waiting for transfers between devices, columns(): return lax.all_to_all(w, 'shard', split_axis=1, concat_axis=0, tiled=True)  329 us
    reduce_scatter x4, waiting for transfers between devices, scatter(): lax.psum_scatter(x.astype(BF16), 'shard', scatter_dimension=0, tiled=True)  256 us
    psum x1, waiting for transfers between devices, per_device_split(): lax.psum((gain_terms, back_columns(term_gi), back_columns(term_li), small...  236 us
    all_to_all x4, waiting for transfers between devices, back_columns(): return lax.all_to_all(t, 'shard', split_axis=0, concat_axis=1, tiled=True)  138 us
    all_gather x4, waiting for transfers between devices, gather(): return lax.all_gather(x, 'shard', axis=0, tiled=True)  111 us
    unnamed x11, waiting for transfers between devices  47.2 us
    unnamed x118, local copies, waits for them, and re-layouts  35.5 us
    dot_general x6, matrix products, mm_tn(): lax.dot_general(a, b, (((0,), (0,)), ((), ())), preferred_element_type=F32)  34.9 us
  transfers between devices with their start and end apart: 18, of which 13 were waited for; matrix products, arithmetic and copies ran while one was open for 8% of the time, Pallas kernels for 1%

profile of v1, /device:TPU:0, one launch (start us, length us, event | category | flops | bytes accessed | tf_op | source)
XLA Modules:
  0.0 1416.3 jit_solution(13121971276281976359)
XLA Ops:
  14.0 22.2 %all_gather.15 = bf16[2,2048]{1,0:T(2,128)(2,1)S(1)} all-gather(bf16[2,256]{1,0:T(2,128)(2,1)S(1)} %pad_maximum_fusion.2), channel_id=1, replica_groups=mesh['group'=4,'shard'=8] {'shard'}, dimensions={1}, use_global_device_ids=true | all-gather | bytes 9216 | tf_op jit(solution)/shard_map/all_gather | solution.py:208
  41.0 4.3 all-to-all-start
  47.9 43.4 %all-to-all-done = bf16[256,8,320]{0,2,1:T(8,128)(2,1)} async-done(((bf16[256,8,320]{0,2,1:T(8,128)(2,1)}), bf16[256,8,320]{0,2,1:T(8,128)(2,1)}, u32[]{:S(2)}, u32[]{:S(2)}) %all-to-all-start) | async-done | bytes 1310752 | tf_op jit(solution)/shard_map/all_to_all | solution.py:205
  91.3 4.3 all-to-all-start.1
  103.6 53.7 %all-to-all-done.1 = bf16[256,8,320]{0,2,1:T(8,128)(2,1)} async-done(((bf16[256,8,320]{0,2,1:T(8,128)(2,1)}), bf16[256,8,320]{0,2,1:T(8,128)(2,1)}, u32[]{:S(2)}, u32[]{:S(2)}) %all-to-all-start.1) | async-done | bytes 1310752 | tf_op jit(solution)/shard_map/all_to_all | solution.py:205
  161.1 5.4 fusion.11.linear_ref
  169.0 7.8 mixer_forward.1
  181.3 4.3 convolution_convert_fusion
  185.7 86.4 %reduce-scatter.8.cloned.1.call-done = bf16[128,2048]{1,0:T(8,128)(2,1)} async-done(((bf16[1024,2048]{1,0:T(8,128)(2,1)}), bf16[128,2048]{1,0:T(8,128)(2,1)}) %reduce-scatter.8.cloned.1.call-update) | async-done | bytes 524304 | tf_op jit(solution)/shard_map/reduce_scatter | solution.py:202
  276.3 4.6 copy.106
  281.0 4.5 all-to-all-start.2
  286.0 4.6 copy.108
  290.7 115.3 %all-to-all-done.2 = bf16[256,8,768]{0,2,1:T(8,128)(2,1)} async-done(((bf16[256,8,768]{0,2,1:T(8,128)(2,1)}), bf16[256,8,768]{0,2,1:T(8,128)(2,1)}, u32[]{:S(2)}, u32[]{:S(2)}) %all-to-all-start.2) | async-done | bytes 3145760 | tf_op jit(solution)/shard_map/all_to_all | solution.py:205
  406.0 4.5 all-to-all-start.3
  410.7 4.6 copy.107
  415.3 116.5 %all-to-all-done.3 = bf16[256,8,768]{0,2,1:T(8,128)(2,1)} async-done(((bf16[256,8,768]{0,2,1:T(8,128)(2,1)}), bf16[256,8,768]{0,2,1:T(8,128)(2,1)}, u32[]{:S(2)}, u32[]{:S(2)}) %all-to-all-start.3) | async-done | bytes 3145760 | tf_op jit(solution)/shard_map/all_to_all | solution.py:205
  531.8 4.6 copy.109
  536.5 8.4 fusion.54
  544.9 5.1 fusion.53
  550.0 10.7 multiply_convert_fusion
  564.2 5.0 add_convert_fusion.1
  569.7 6.3 convolution_convert_fusion.1
  576.1 79.7 %reduce-scatter.12.cloned.1.call-done = bf16[128,2048]{1,0:T(8,128)(2,1)} async-done(((bf16[1024,2048]{1,0:T(8,128)(2,1)}), bf16[128,2048]{1,0:T(8,128)(2,1)}) %reduce-scatter.12.cloned.1.call-update) | async-done | bytes 524304 | tf_op jit(solution)/shard_map/reduce_scatter | solution.py:202
  657.4 90.1 %reduce-scatter.10.cloned.1.call-done = bf16[128,2048]{1,0:T(8,128)(2,1)} async-done(((bf16[1024,2048]{1,0:T(8,128)(2,1)}), bf16[128,2048]{1,0:T(8,128)(2,1)}) %reduce-scatter.10.cloned.1.call-update) | async-done | bytes 524304 | tf_op jit(solution)/shard_map/reduce_scatter | solution.py:202
  750.7 7.4 convolution_convert_fusion.3
  758.1 4.6 all-to-all-start.7
  762.7 7.4 convolution_convert_fusion.4
  770.1 111.2 %all-gather.11.cloned.1.call-done = bf16[1024,2048]{1,0:T(8,128)(2,1)} async-done(((bf16[128,2048]{1,0:T(8,128)(2,1)}), bf16[1024,2048]{1,0:T(8,128)(2,1)}) %all-gather.11.cloned.1.call-update) | async-done | bytes 4194320 | tf_op jit(solution)/shard_map/all_gather | solution.py:199
  881.3 5.1 fusion.56.gm_ref
  886.5 13.7 mixer_backward.1
  902.0 4.6 all-to-all-start.6
  909.2 4.4 add_convert_fusion
  913.6 3.7 fusion.15
  918.5 93.0 %all-to-all-done.6 = bf16[8,256,768]{2,1,0:T(8,128)(2,1)} async-done(((bf16[8,256,768]{2,1,0:T(8,128)(2,1)}), bf16[8,256,768]{2,1,0:T(8,128)(2,1)}, u32[]{:S(2)}, u32[]{:S(2)}) %all-to-all-start.6) | async-done | bytes 3145760 | tf_op jit(solution)/shard_map/all_to_all | solution.py:290
  1011.5 3.6 all-to-all-start.4
  1015.1 3.8 fusion.18
  1020.1 35.6 %all-to-all-done.4 = bf16[8,256,320]{1,2,0:T(8,128)(2,1)S(1)} async-done(((bf16[8,256,320]{1,2,0:T(8,128)(2,1)}), bf16[8,256,320]{1,2,0:T(8,128)(2,1)S(1)}, u32[]{:S(2)}, u32[]{:S(2)}) %all-to-all-start.4) | async-done | bytes 1310752 | tf_op jit(solution)/shard_map/all_to_all | solution.py:290
  1055.7 4.3 all-to-all-start.5
  1060.0 7.8 convolution_convert_fusion.2
  1067.8 3.9 copy.135
  1071.7 4.0 copy.134
  1078.7 4.8 convolution_convert_fusion.5
  1083.5 9.0 all-to-all-done.5
  1095.1 46.6 %reduce-scatter.16.cloned.1.call-done = bf16[256,2]{1,0:T(8,128)(2,1)} async-done(((bf16[2048,2]{1,0:T(8,128)(2,1)}), bf16[256,2]{1,0:T(8,128)(2,1)}) %reduce-scatter.16.cloned.1.call-update) | async-done | bytes 1040
  1142.5 5.8 all-reduce.4
  1150.1 236.4 %all-reduce.8.cloned.1.call-done = (bf16[256,2560]{0,1:T(8,128)(2,1)}, bf16[256,2560]{0,1:T(8,128)(2,1)}, bf16[320,160]{1,0:T(8,128)(2,1)}, bf16[320,160]{1,0:T(...) async-done(((bf16[256,2560]{0,1:T(8,128)(2,1)}, bf16[256,2560]{0,1:T(8,128)(2,1)}, ...) | async-done | bytes 13574160 | tf_op jit(solution)/shard_map/psum | solution.py:295
  1402.3 3.4 convert_element_type.182
  1405.7 3.6 convert_element_type.184
  (190 shorter events, 75.1 us)
Async XLA Ops:
  7.2 542.8 %copy-start = (bf16[768,2048]{1,0:T(8,128)(2,1)S(1)}, bf16[768,2048]{1,0:T(8,128)(2,1)}, u32[]{:S(2)}) copy-start(bf16[768,2048]{1,0:T(8,128)(2,1)} %param.35) | copy-start | bytes 9437188
  7.2 152.7 %all-gather.5.cloned.1.call-start = ((), (), s32[]{:S(2)}) async-start(), calls=%async_computation.13 | async-start | bytes 5013504 | tf_op jit(solution)/shard_map/all_gather | solution.py:199
  41.0 50.3 %all-to-all-start = ((bf16[256,8,320]{0,2,1:T(8,128)(2,1)}), bf16[256,8,320]{0,2,1:T(8,128)(2,1)}, u32[]{:S(2)}, u32[]{:S(2)}) async-start(bf16[256,8,320]{0,2,1:T(8,128)(2,1)} %bitcast.86), calls=%async_computation | async-start | bytes 2621440 | tf_op jit(solution)/shard_map/all_to_all | solution.py:205
  45.3 50.3 %copy-start.40 = (bf16[320]{0:T(512)(128)(2,1)S(1)}, bf16[320]{0:T(512)(128)(2,1)}, u32[]{:S(2)}) copy-start(bf16[320]{0:T(512)(128)(2,1)} %param.25) | copy-start | bytes 1924
  45.3 50.3 %copy-start.41 = (bf16[320]{0:T(512)(128)(2,1)S(1)}, bf16[320]{0:T(512)(128)(2,1)}, u32[]{:S(2)}) copy-start(bf16[320]{0:T(512)(128)(2,1)} %param.27) | copy-start | bytes 1924
  45.3 50.3 %copy-start.42 = (bf16[320]{0:T(512)(128)(2,1)S(1)}, bf16[320]{0:T(512)(128)(2,1)}, u32[]{:S(2)}) copy-start(bf16[320]{0:T(512)(128)(2,1)} %param.29) | copy-start | bytes 1924
  45.4 50.3 %copy-start.43 = (bf16[320]{0:T(512)(128)(2,1)S(1)}, bf16[320]{0:T(512)(128)(2,1)}, u32[]{:S(2)}) copy-start(bf16[320]{0:T(512)(128)(2,1)} %param.30) | copy-start | bytes 1924
  45.4 50.4 %copy-start.39 = (bf16[4,320]{1,0:T(4,128)(2,1)S(1)}, bf16[4,320]{1,0:T(4,128)(2,1)}, u32[]{:S(2)}) copy-start(bf16[4,320]{1,0:T(4,128)(2,1)} %param.24) | copy-start | bytes 7684
  45.4 50.4 %copy-start.38 = (bf16[320,160]{0,1:T(8,128)(2,1)S(1)}, bf16[320,160]{0,1:T(8,128)(2,1)}, u32[]{:S(2)}) copy-start(bf16[320,160]{0,1:T(8,128)(2,1)} %param.26) | copy-start | bytes 307204
  91.3 66.0 %all-to-all-start.1 = ((bf16[256,8,320]{0,2,1:T(8,128)(2,1)}), bf16[256,8,320]{0,2,1:T(8,128)(2,1)}, u32[]{:S(2)}, u32[]{:S(2)}) async-start(bf16[256,8,320]{0,2,1:T(8,128)(2,1)} %bitcast.85), calls=%async_computation.1 | async-start | bytes 2621440 | tf_op jit(solution)/shard_map/all_to_all | solution.py:205
  95.6 176.5 %reduce-scatter.8.cloned.1.call-start = ((), (), s32[]{:S(2)}) async-start(), calls=%async_computation.14 | async-start | bytes 4718592 | tf_op jit(solution)/shard_map/reduce_scatter | solution.py:202
  159.9 6.6 slice-start
  161.1 7.9 copy-start.6
  161.1 5.4 copy-start.25
  161.1 5.4 slice-start.1
  168.9 7.9 copy-start.4
  168.9 12.4 copy-start.45
  185.7 350.8 %all-gather.7.cloned.1.call-start = ((), (), s32[]{:S(2)}) async-start(), calls=%async_computation.15 | async-start | bytes 4718592 | tf_op jit(solution)/shard_map/all_gather | solution.py:199
  281.0 125.0 %all-to-all-start.2 = ((bf16[256,8,768]{0,2,1:T(8,128)(2,1)}), bf16[256,8,768]{0,2,1:T(8,128)(2,1)}, u32[]{:S(2)}, u32[]{:S(2)}) async-start(bf16[256,8,768]{0,2,1:T(8,128)(2,1)} %bitcast.77), calls=%async_computation.3 | async-start | bytes 6291456 | tf_op jit(solution)/shard_map/all_to_all | solution.py:205
  285.5 264.5 %all-gather.9.cloned.1.call-start = ((), (), s32[]{:S(2)}) async-start(), calls=%async_computation.17 | async-start | bytes 4718592 | tf_op jit(solution)/shard_map/all_gather | solution.py:199
  406.0 125.9 %all-to-all-start.3 = ((bf16[256,8,768]{0,2,1:T(8,128)(2,1)}), bf16[256,8,768]{0,2,1:T(8,128)(2,1)}, u32[]{:S(2)}, u32[]{:S(2)}) async-start(bf16[256,8,768]{0,2,1:T(8,128)(2,1)} %bitcast.78), calls=%async_computation.4 | async-start | bytes 6291456 | tf_op jit(solution)/shard_map/all_to_all | solution.py:205
  410.5 245.3 %reduce-scatter.12.cloned.1.call-start = ((), (), s32[]{:S(2)}) async-start(), calls=%async_computation.18 | async-start | bytes 4718592 | tf_op jit(solution)/shard_map/reduce_scatter | solution.py:202
  536.5 8.4 copy-start.30
  536.5 8.4 copy-start.44
  549.9 10.8 copy-start.31
  569.2 178.3 %reduce-scatter.10.cloned.1.call-start = ((), (), s32[]{:S(2)}) async-start(), calls=%async_computation.16 | async-start | bytes 4718592 | tf_op jit(solution)/shard_map/reduce_scatter | solution.py:202
  576.0 79.8 %copy-start.22 = (bf16[128,2048]{1,0:T(8,128)(2,1)S(1)}, bf16[128,2048]{1,0:T(8,128)(2,1)}, u32[]{:S(2)}) copy-start(bf16[128,2048]{1,0:T(8,128)(2,1)} %param.18) | copy-start | bytes 1572868
  576.0 79.8 %copy-start.24 = (bf16[128,2048]{1,0:T(8,128)(2,1)S(1)}, bf16[128,2048]{1,0:T(8,128)(2,1)}, u32[]{:S(2)}) copy-start(bf16[128,2048]{1,0:T(8,128)(2,1)} %reduce-scatter.8.cloned.1.call-done) | copy-start | bytes 1572868
  576.0 171.5 %copy-start.36 = (bf16[128,2048]{1,0:T(8,128)(2,1)S(1)}, bf16[128,2048]{1,0:T(8,128)(2,1)}, u32[]{:S(2)}) copy-start(bf16[128,2048]{1,0:T(8,128)(2,1)} %param.20) | copy-start | bytes 1572868
  576.1 174.7 %copy-start.49 = (bf16[1024,768]{1,0:T(8,128)(2,1)S(1)}, bf16[1024,768]{1,0:T(8,128)(2,1)}, u32[]{:S(2)}) copy-start(bf16[1024,768]{1,0:T(8,128)(2,1)} %copy-done.48) | copy-start | bytes 4718596
  576.1 305.3 %all-gather.11.cloned.1.call-start = ((), (), s32[]{:S(2)}) async-start(), calls=%async_computation.19 | async-start | bytes 4718592 | tf_op jit(solution)/shard_map/all_gather | solution.py:199
  758.1 143.9 %all-to-all-start.7 = ((bf16[8,256,768]{2,1,0:T(8,128)(2,1)}), bf16[8,256,768]{2,1,0:T(8,128)(2,1)}, u32[]{:S(2)}, u32[]{:S(2)}) async-start(bf16[8,256,768]{2,1,0:T(8,128)(2,1)} %bitcast.23), calls=%async_computation.11 | async-start | bytes 6291456 | tf_op jit(solution)/shard_map/all_to_all | solution.py:290
  770.1 116.3 %copy-start.3 = (f32[1024,320]{1,0:T(8,128)S(1)}, f32[1024,320]{1,0:T(8,128)}, u32[]{:S(2)}) copy-start(f32[1024,320]{1,0:T(8,128)} %copy-done.2) | copy-start | bytes 3932164
  770.1 116.3 %copy-start.5 = (f32[1024,320]{1,0:T(8,128)S(1)}, f32[1024,320]{1,0:T(8,128)}, u32[]{:S(2)}) copy-start(f32[1024,320]{1,0:T(8,128)} %copy-done.4) | copy-start | bytes 3932164
  881.3 5.1 copy-start.7
  881.3 5.1 copy-start.9
  881.3 5.1 copy-start.11
  881.3 5.1 copy-start.13
  881.3 5.1 copy-start.15
  902.0 109.6 %all-to-all-start.6 = ((bf16[8,256,768]{2,1,0:T(8,128)(2,1)}), bf16[8,256,768]{2,1,0:T(8,128)(2,1)}, u32[]{:S(2)}, u32[]{:S(2)}) async-start(bf16[8,256,768]{2,1,0:T(8,128)(2,1)} %bitcast.88), calls=%async_computation.10 | async-start | bytes 6291456 | tf_op jit(solution)/shard_map/all_to_all | solution.py:290
  906.6 169.2 %reduce-scatter.14.cloned.1.call-start = ((), (), s32[]{:S(2)}) async-start(), calls=%async_computation.20 | async-start | bytes 4718592 | tf_op jit(solution)/shard_map/reduce_scatter | solution.py:202
  1011.5 44.1 %all-to-all-start.4 = ((bf16[8,256,320]{1,2,0:T(8,128)(2,1)}), bf16[8,256,320]{1,2,0:T(8,128)(2,1)S(1)}, u32[]{:S(2)}, u32[]{:S(2)}) async-start(bf16[8,256,320]{1,2,0:T(8,128)(2,1)} %bitcast.76), calls=%async_computation.8 | async-start | bytes 2621440 | tf_op jit(solution)/shard_map/all_to_all | solution.py:290
  1055.7 12.1 copy-start.28
  1055.7 36.8 %all-to-all-start.5 = ((bf16[8,256,320]{1,2,0:T(8,128)(2,1)}), bf16[8,256,320]{1,2,0:T(8,128)(2,1)}, u32[]{:S(2)}, u32[]{:S(2)}) async-start(bf16[8,256,320]{1,2,0:T(8,128)(2,1)} %bitcast.75), calls=%async_computation.9 | async-start | bytes 2621440 | tf_op jit(solution)/shard_map/all_to_all | solution.py:290
  1059.9 81.7 %reduce-scatter.16.cloned.1.call-start = ((), (), s32[]{:S(2)}) async-start(), calls=%async_computation.21 | async-start | bytes 589824
  1071.7 7.0 copy-start.21
  1078.4 308.0 %all-reduce.8.cloned.1.call-start = ((), (), s32[]{:S(2)}) async-start(), calls=%async_computation.22 | async-start | bytes 27394048 | tf_op jit(solution)/shard_map/psum | solution.py:295
  1392.7 6.1 copy-start.35
  (22 other events, 57.7 us)
Sparse Core Ops, SparseCore 0:
  38.7 120.2 all-gather.4
  185.8 86.2 reduce-scatter.7
  276.4 131.0 all-gather.6
  410.3 123.1 all-gather.8
  569.3 86.3 reduce-scatter.11
  659.9 87.6 reduce-scatter.9
  750.8 130.4 all-gather.10
  913.7 151.5 reduce-scatter.13
  1078.6 63.0 reduce-scatter.15
  1146.2 240.2 all-reduce.7

commit v2 on v1

--- a/solution.py
+++ b/solution.py
@@ -14,6 +14,7 @@
 BF16 = jnp.bfloat16
 GELU_C = 0.7978845608028654
 GELU_K = 0.044715
+CAP = 128
 
 
 def positions_in_run(counts, row_count):
@@ -82,29 +83,499 @@
     return rate, jnp.exp(-keep), jnp.sqrt(one_less_exp(2.0 * keep))
 
 
-def mixer_forward_kernel(pos_ref, gate_ref, linear_ref, ck_ref, vec_ref, rw_ref, iw_ref,
-                         merged_ref, rate_ref, input_ref, state_ref):
-    pos = pos_ref[...]
+MESH_ID = pl.DeviceIdType.MESH
+VMEM_LIMIT = 62 * 2**20
+N_Z, N_X = 4, 2
+
+
+def place():
+    shard = lax.axis_index("shard")
+    return lax.axis_index("group"), shard, shard // N_X, shard % N_X
+
+
+def greet(peers):
+    bar = pltpu.get_barrier_semaphore()
+    count = 0
+    for device, there in peers:
+        if there is True:
+            pl.semaphore_signal(bar, inc=1, device_id=device, device_id_type=MESH_ID)
+            count = count + 1
+        else:
+            @pl.when(there)
+            def _(device=device):
+                pl.semaphore_signal(bar, inc=1, device_id=device, device_id_type=MESH_ID)
+            count = count + there.astype(jnp.int32)
+    pl.semaphore_wait(bar, count)
+
+
+def line_peers():
+    group, shard, z, x = place()
+    return [
+        ((group, shard + N_X), z < N_Z - 1),
+        ((group, shard - N_X), z > 0),
+        ((group, z * N_X + 1 - x), True),
+    ]
+
+
+class Gather:
+    CHUNKS = 2
+
+    @classmethod
+    def scratch(cls):
+        return [pltpu.SemaphoreType.DMA((3, N_Z, cls.CHUNKS)), pltpu.SemaphoreType.DMA((N_Z * N_X, cls.CHUNKS))]
+
+    def __init__(self, buf, sems):
+        self.buf, (self.send, self.recv) = buf, sems
+        self.group, self.shard, self.z, self.x = place()
+        self.rows = buf.shape[1] // self.CHUNKS
+
+    def copy(self, origin, column, c, way):
+        slot = origin * N_X + column
+        z = (self.z + 1, self.z - 1, self.z)[way]
+        x = 1 - self.x if way == 2 else self.x
+        piece = self.buf.at[slot, pl.ds(c * self.rows, self.rows)]
+        return pltpu.make_async_remote_copy(
+            src_ref=piece, dst_ref=piece, send_sem=self.send.at[way, origin, c],
+            recv_sem=self.recv.at[slot, c], device_id=(self.group, z * N_X + x), device_id_type=MESH_ID,
+        )
+
+    def start(self):
+        for c in range(self.CHUNKS):
+            self.forward(self.z, c, True, True)
+
+    def forward(self, origin, c, up, down):
+        if up:
+            @pl.when(self.z < N_Z - 1)
+            def _():
+                self.copy(origin, self.x, c, 0).start()
+        if down:
+            @pl.when(self.z > 0)
+            def _():
+                self.copy(origin, self.x, c, 1).start()
+        self.copy(origin, self.x, c, 2).start()
+
+    def step(self, k):
+        for c in range(self.CHUNKS):
+            @pl.when(self.z >= k)
+            def _(c=c):
+                self.copy(self.z - k, self.x, c, 2).wait_recv()
+                self.forward(self.z - k, c, True, False)
+
+            @pl.when(self.z + k < N_Z)
+            def _(c=c):
+                self.copy(self.z + k, self.x, c, 2).wait_recv()
+                self.forward(self.z + k, c, False, True)
+
+    def wait_across(self, origin):
+        for c in range(self.CHUNKS):
+            self.copy(origin, 1 - self.x, c, 2).wait_recv()
+
+    def finish(self):
+        for c in range(self.CHUNKS):
+            for origin in range(N_Z):
+                @pl.when((self.z < N_Z - 1) & (origin <= self.z))
+                def _():
+                    self.copy(origin, self.x, c, 0).wait_send()
+
+                @pl.when((self.z > 0) & (origin >= self.z))
+                def _():
+                    self.copy(origin, self.x, c, 1).wait_send()
+                self.copy(origin, self.x, c, 2).wait_send()
+
+
+class Scatter:
+    CHUNKS = 2
+
+    @classmethod
+    def scratch(cls, rows, width):
+        dma = pltpu.SemaphoreType.DMA
+        return [
+            pltpu.VMEM((N_Z, rows, width), BF16),
+            pltpu.VMEM((N_Z + 1, rows, width), BF16),
+            pltpu.VMEM((N_Z, rows, width), BF16),
+            dma((2, N_Z, cls.CHUNKS)), dma((N_Z, cls.CHUNKS)), dma((N_Z + 1, cls.CHUNKS)),
+        ]
+
+    def __init__(self, parts, scratch):
+        self.parts = parts
+        self.across, self.along, self.held, self.send, self.recv_x, self.recv_z = scratch
+        self.group, self.shard, self.z, self.x = place()
+        self.rows = parts.shape[1] // self.CHUNKS
+
+    def dest(self, i):
+        low = jnp.minimum(self.z, N_Z - 1 - self.z)
+        value = (N_Z - 1, N_Z - 2, jnp.where(low == 0, 1, 0), low)[i]
+        return jnp.where(self.z >= N_Z // 2, N_Z - 1 - value, value)
+
+    def span(self, c):
+        return pl.ds(c * self.rows, self.rows)
+
+    def copy_x(self, dest, c):
+        return pltpu.make_async_remote_copy(
+            src_ref=self.parts.at[dest * N_X + 1 - self.x, self.span(c)],
+            dst_ref=self.across.at[dest, self.span(c)],
+            send_sem=self.send.at[0, dest, c], recv_sem=self.recv_x.at[dest, c],
+            device_id=(self.group, self.z * N_X + 1 - self.x), device_id_type=MESH_ID,
+        )
+
+    def copy_z(self, dest, slot, c, step):
+        return pltpu.make_async_remote_copy(
+            src_ref=self.held.at[dest, self.span(c)], dst_ref=self.along.at[slot, self.span(c)],
+            send_sem=self.send.at[1, dest, c], recv_sem=self.recv_z.at[slot, c],
+            device_id=(self.group, (self.z + step) * N_X + self.x), device_id_type=MESH_ID,
+        )
+
+    def start(self, i):
+        for c in range(self.CHUNKS):
+            self.copy_x(self.dest(i), c).start()
+
+    def arrived(self, slot, c):
+        self.copy_z(0, slot, c, 0).wait_recv()
+        return self.along[slot, self.span(c)].astype(F32)
+
+    def step(self, i):
+        dest = self.dest(i)
+        for c in range(self.CHUNKS):
+            self.copy_x(dest, c).wait_recv()
+            own = dest * N_X + self.x
+            self.held[dest, self.span(c)] = (
+                self.parts[own, self.span(c)].astype(F32) + self.across[dest, self.span(c)].astype(F32)
+            ).astype(BF16)
+
+            @pl.when(((dest > self.z) & (self.z > 0)) | ((dest < self.z) & (self.z < N_Z - 1)))
+            def _(c=c):
+                self.held[dest, self.span(c)] = (
+                    self.parts[own, self.span(c)].astype(F32) + self.across[dest, self.span(c)].astype(F32)
+                    + self.arrived(dest, c)
+                ).astype(BF16)
+
+            @pl.when(dest > self.z)
+            def _(c=c):
+                self.copy_z(dest, dest, c, 1).start()
+
+            @pl.when(dest < self.z)
+            def _(c=c):
+                self.copy_z(dest, jnp.where(dest == self.z - 1, N_Z, dest), c, -1).start()
+
+    def last(self, out):
+        for c in range(self.CHUNKS):
+            self.copy_x(self.z, c).wait_recv()
+            out[self.span(c)] = self.parts[self.shard, self.span(c)].astype(F32) + self.across[self.z, self.span(c)].astype(F32)
+
+            @pl.when(self.z > 0)
+            def _(c=c):
+                out[self.span(c)] += self.arrived(self.z, c)
+
+            @pl.when(self.z < N_Z - 1)
+            def _(c=c):
+                out[self.span(c)] += self.arrived(N_Z, c)
+
+    def finish(self):
+        for c in range(self.CHUNKS):
+            for dest in range(N_Z):
+                self.copy_x(dest, c).wait_send()
+
+                @pl.when(dest != self.z)
+                def _():
+                    self.copy_z(dest, 0, c, 0).wait_send()
+
+
+class Exchange:
+    @classmethod
+    def scratch(cls, shards, sources):
+        dma = pltpu.SemaphoreType.DMA
+        return [dma((sources, shards)), dma((sources, shards)), dma((3, shards)), dma((3, shards))]
+
+    def __init__(self, sources, full, spans, sems):
+        self.sources, self.full, self.spans = sources, full, spans
+        self.send_first, self.recv_first, self.send, self.recv = sems
+        self.group, self.shard, _, _ = place()
+        self.shards = full.shape[0]
+        self.core_mate, self.y_mate = mates()
+
+    def first(self, j, to, origin):
+        return pltpu.make_async_remote_copy(
+            src_ref=self.sources[j](to), dst_ref=self.full.at[origin, self.group, :, self.spans[j]],
+            send_sem=self.send_first.at[j, to], recv_sem=self.recv_first.at[j, origin],
+            device_id=(self.group, to), device_id_type=MESH_ID,
+        )
+
+    def own(self, j):
+        return pltpu.make_async_copy(
+            self.sources[j](self.shard), self.full.at[self.shard, self.group, :, self.spans[j]],
+            self.recv_first.at[j, self.shard],
+        )
+
+    def pass_on(self, origin, quarter, mate, way):
+        piece = self.full.at[origin, quarter]
+        return pltpu.make_async_remote_copy(
+            src_ref=piece, dst_ref=piece, send_sem=self.send.at[way, origin], recv_sem=self.recv.at[way, origin],
+            device_id=(mate, self.shard), device_id_type=MESH_ID,
+        )
+
+    def start(self):
+        for j in range(len(self.sources)):
+            self.own(j).start()
+
+        @pl.loop(1, self.shards)
+        def _(i):
+            to = (self.shard + i) % self.shards
+            for j in range(len(self.sources)):
+                self.first(j, to, self.shard).start()
+
+    def spread(self):
+        for j in range(len(self.sources)):
+            self.own(j).wait()
+        self.pass_on(self.shard, self.group, self.core_mate, 0).start()
+        self.pass_on(self.shard, self.group, self.y_mate, 1).start()
+
+        @pl.loop(1, self.shards)
+        def _(i):
+            origin = (self.shard + self.shards - i) % self.shards
+            for j in range(len(self.sources)):
+                self.first(j, origin, origin).wait_recv()
+            self.pass_on(origin, self.group, self.core_mate, 0).start()
+            self.pass_on(origin, self.group, self.y_mate, 1).start()
+
+    def relay(self):
+        @pl.loop(0, self.shards)
+        def _(i):
+            origin = (self.shard + self.shards - i) % self.shards
+            self.pass_on(origin, self.y_mate, self.core_mate, 1).wait_recv()
+            self.pass_on(origin, self.y_mate, self.core_mate, 2).start()
+
+    def arrive(self):
+        @pl.loop(0, self.shards)
+        def _(origin):
+            self.pass_on(origin, self.group, self.core_mate, 0).wait_recv()
+            self.pass_on(origin, self.group, self.core_mate, 2).wait_recv()
+
+    def finish(self):
+        @pl.loop(1, self.shards)
+        def _(i):
+            to = (self.shard + i) % self.shards
+            for j in range(len(self.sources)):
+                self.first(j, to, self.shard).wait_send()
+
+        @pl.loop(0, self.shards)
+        def _(origin):
+            for way in range(3):
+                self.pass_on(origin, self.group, self.core_mate, way).wait_send()
+
+
+def mates():
+    group = lax.axis_index("group")
+    return group + 1 - 2 * (group % 2), group + 2 - 4 * (group // 2)
+
+
+def all_peers():
+    group, shard, _, _ = place()
+    core_mate, y_mate = mates()
+    others = [((group, (shard + i) % (N_Z * N_X)), True) for i in range(1, N_Z * N_X)]
+    return others + [((core_mate, shard), True), ((y_mate, shard), True)]
+
+
+def mixer_forward(linear, gate, pos, vec, gates):
     masks = [(pos >= k).astype(F32) for k in (1, 2, 3)]
-    linear = linear_ref[...]
-    conv = conv_rows(linear, ck_ref[...], vec_ref[0:1], masks)
-    low = conv.astype(BF16)
-    rate_pre = mm(low, rw_ref[...]) + vec_ref[1:2]
-    input_pre = mm(low, iw_ref[...]) + vec_ref[2:3]
-    _, a, weight_in = decay_terms(rate_pre, vec_ref[3:4])
+    conv = conv_rows(linear, vec[0:4], vec[4:5], masks)
+    width = linear.shape[1]
+    both = mm(conv.astype(BF16), gates)
+    rate_pre = both[:, :width] + vec[5:6]
+    input_pre = both[:, width:] + vec[6:7]
+    _, a, weight_in = decay_terms(rate_pre, vec[7:8])
     mult = a * masks[0]
     total = weight_in * sigmoid(input_pre) * conv
     step = 1
-    rows = total.shape[0]
-    while step < rows:
+    while step < CAP:
         total = total + mult * roll_rows(total, step)
-        if 2 * step < rows:
+        if 2 * step < CAP:
             mult = mult * roll_rows(mult, step)
         step *= 2
-    rate_ref[...] = rate_pre
-    input_ref[...] = input_pre
-    state_ref[...] = total
-    merged_ref[...] = (gelu_value(gate_ref[...]) * total).astype(BF16)
+    return rate_pre, input_pre, total, (gelu_value(gate) * total).astype(BF16)
+
+
+def rms_scale(values):
+    return lax.rsqrt(jnp.mean(values * values, axis=1, keepdims=True) + EPSILON)
+
+
+def forward_kernel(
+    lengths_ref, tokens_ref, gains_ref, vec_ref, gates_ref, out_proj_ref, gate_in_ref, linear_in_ref, mlp_gate_ref, mlp_up_ref,
+    gather_out, weights_out, mlp_out, gains_out, saved_out, merged_out, middle_ref, normed_two_ref,
+    buf, weights, quarter, raw, masked, saved, merged, parts,
+    gather_a, gather_b, ex_a, ex_b, ex_c, ex_d, mx_a, mx_b, mx_c, mx_d, *rest,
+):
+    scatter_scratch, (gain_send, gain_recv, raw_sem, out_sem, pair_sem) = rest[:-5], rest[-5:]
+    group, shard, z, x = place()
+    shards = N_Z * N_X
+    rows, width = tokens_ref.shape
+    quarter_rows = raw.shape[1]
+    chans = linear_in_ref.shape[1] // shards
+    padded = vec_ref.shape[1]
+    fetch = [
+        pltpu.make_async_copy(ref.at[pl.ds(group * quarter_rows, quarter_rows)], raw.at[i], raw_sem.at[i])
+        for i, ref in enumerate((gate_in_ref, linear_in_ref))
+    ]
+    for copy in fetch:
+        copy.start()
+    greet(all_peers())
+
+    def gain_copy(to, origin):
+        return pltpu.make_async_remote_copy(
+            src_ref=gains_ref, dst_ref=gains_out.at[origin], send_sem=gain_send.at[to], recv_sem=gain_recv.at[origin],
+            device_id=(group, to), device_id_type=MESH_ID,
+        )
+
+    for i in range(1, shards):
+        gain_copy((shard + i) % shards, shard).start()
+    gains_out[shard] = gains_ref[...]
+    inside = lax.broadcasted_iota(jnp.int32, (quarter_rows, padded), 1) < chans
+    for i, copy in enumerate(fetch):
+        copy.wait()
+        for to in range(shards):
+            piece = raw[i, :, to * chans : (to + 1) * chans].astype(F32)
+            piece = jnp.concatenate([piece, jnp.zeros((quarter_rows, padded - chans), F32)], axis=1)
+            quarter[to, :, i * padded : (i + 1) * padded] = piece.astype(BF16)
+    exchange = Exchange([lambda to: quarter.at[to]], weights, [slice(None)], (ex_a, ex_b, ex_c, ex_d))
+    exchange.start()
+    hidden = mlp_up_ref.shape[1] // shards
+
+    def part_of(ref):
+        return lambda to: ref.at[pl.ds(group * quarter_rows, quarter_rows), pl.ds(to * hidden, hidden)]
+
+    mlp_exchange = Exchange(
+        [part_of(mlp_gate_ref), part_of(mlp_up_ref)], mlp_out, [slice(0, hidden), slice(hidden, 2 * hidden)], (mx_a, mx_b, mx_c, mx_d)
+    )
+    pos, live = positions_in_run([lengths_ref[0, i] for i in range(3)], rows)
+    masked[...] = tokens_ref[...].astype(F32) * live
+    for i in range(1, shards):
+        gain_copy(shard, (shard + i) % shards).wait_recv()
+    gains = jnp.concatenate([gains_out[i] for i in range(shards)], axis=1)
+    gather = Gather(buf, (gather_a, gather_b))
+    buf[shard, :, :width] = (masked[...] * rms_scale(masked[...]) * gains[0:1]).astype(BF16)
+    buf[shard, :, width:] = jnp.broadcast_to(pos.astype(F32).astype(BF16), (rows, buf.shape[2] - width))
+    gather.start()
+    gather.step(1)
+    exchange.spread()
+    gather.step(2)
+    exchange.relay()
+    mlp_exchange.start()
+    exchange.arrive()
+    scatter = Scatter(parts, scatter_scratch)
+
+    def pair_copies(origin):
+        return [
+            pltpu.make_async_copy(saved.at[origin], saved_out.at[origin], pair_sem.at[0, origin]),
+            pltpu.make_async_copy(merged.at[origin], merged_out.at[origin], pair_sem.at[1, origin]),
+        ]
+
+    @pl.loop(0, N_Z)
+    def _(i):
+        @pl.when(i == 1)
+        def _():
+            gather.step(3)
+
+        origin = nearest(z, i)
+        gather.wait_across(origin)
+        pair = pl.ds(origin * N_X, N_X)
+        both = buf[pair].reshape(N_X * rows, buf.shape[2])
+        pre = mm(both[:, :width], weights[...].reshape(width, 2 * padded))
+        gate, linear = pre[:, :padded], pre[:, padded:]
+        where = both[:, width : width + 1].astype(F32)
+        rate_pre, input_pre, state, merge = mixer_forward(linear, gate, where, vec_ref[...], gates_ref[...])
+        for j, value in enumerate((gate, linear, rate_pre, input_pre, state)):
+            saved[origin, j] = value
+        merged[origin] = merge
+        for copy in pair_copies(origin):
+            copy.start()
+        parts[pair] = mm(merge[:, :chans], out_proj_ref[...]).astype(BF16).reshape(N_X, rows, width)
+
+    outs = [
+        pltpu.make_async_copy(buf, gather_out, out_sem.at[0]),
+        pltpu.make_async_copy(weights, weights_out, out_sem.at[1]),
+    ]
+    for copy in outs:
+        copy.start()
+    for i in range(N_Z):
+        scatter.start(i)
+    mlp_exchange.spread()
+    scatter.step(0)
+    mlp_exchange.relay()
+    scatter.step(1)
+    scatter.step(2)
+    scatter.last(middle_ref)
+    middle_ref[...] += masked[...]
+    normed_two_ref[...] = (middle_ref[...] * rms_scale(middle_ref[...]) * gains[1:2]).astype(BF16)
+    for i in range(1, shards):
+        gain_copy((shard + i) % shards, shard).wait_send()
+    gather.finish()
+    exchange.finish()
+    mlp_exchange.arrive()
+    mlp_exchange.finish()
+    scatter.finish()
+    for copy in outs:
+        copy.wait()
+
+    @pl.loop(0, N_Z)
+    def _(origin):
+        for copy in pair_copies(origin):
+            copy.wait()
+
+
+def nearest(z, i):
+    low = jnp.minimum(z, N_Z - 1 - z)
+    value = jnp.where(low == 0, i, jnp.where(i == 0, 1, jnp.where(i == 1, 0, i)))
+    return jnp.where(z >= N_Z // 2, N_Z - 1 - value, value)
+
+
+def any_spec():
+    return pl.BlockSpec(memory_space=pl.ANY)
+
+
+def vmem_spec():
+    return pl.BlockSpec(memory_space=pltpu.VMEM)
+
+
+def forward_call(lengths, tokens, gains, vec, gates, out_proj, gate_in, linear_in, mlp_gate, mlp_up):
+    rows, width = tokens.shape
+    shards, groups = lax.axis_size("shard"), lax.axis_size("group")
+    padded = vec.shape[1]
+    quarter_rows = gate_in.shape[0] // groups
+    hidden = mlp_up.shape[1] // shards
+    dma = pltpu.SemaphoreType.DMA
+    shape = jax.ShapeDtypeStruct
+    out_shape = [
+        shape((shards, rows, width + 128), BF16),
+        shape((shards, groups, quarter_rows, 2 * padded), BF16),
+        shape((shards, groups, quarter_rows, 2 * hidden), BF16),
+        shape((shards,) + gains.shape, F32),
+        shape((N_Z, 5, N_X * rows, padded), F32),
+        shape((N_Z, N_X * rows, padded), BF16),
+        shape((rows, width), F32),
+        shape((rows, width), BF16),
+    ]
+    return pl.pallas_call(
+        forward_kernel,
+        out_shape=out_shape,
+        in_specs=[pl.BlockSpec(memory_space=pltpu.SMEM)] + [vmem_spec()] * 5 + [any_spec()] * 4,
+        out_specs=[any_spec()] * 3 + [vmem_spec()] + [any_spec()] * 2 + [vmem_spec()] * 2,
+        scratch_shapes=[
+            pltpu.VMEM((shards, rows, width + 128), BF16),
+            pltpu.VMEM((shards, groups, quarter_rows, 2 * padded), BF16),
+            pltpu.VMEM((shards, quarter_rows, 2 * padded), BF16),
+            pltpu.VMEM((2, quarter_rows, gate_in.shape[1]), BF16),
+            pltpu.VMEM((rows, width), F32),
+            pltpu.VMEM((N_Z, 5, N_X * rows, padded), F32),
+            pltpu.VMEM((N_Z, N_X * rows, padded), BF16),
+            pltpu.VMEM((shards, rows, width), BF16),
+        ]
+        + Gather.scratch()
+        + Exchange.scratch(shards, 1)
+        + Exchange.scratch(shards, 2)
+        + Scatter.scratch(rows, width)
+        + [dma((shards,)), dma((shards,)), dma((2,)), dma((2,)), dma((2, N_Z))],
+        compiler_params=pltpu.CompilerParams(collective_id=1, has_side_effects=True, vmem_limit_bytes=VMEM_LIMIT),
+        name="mixer_forward",
+    )(lengths, tokens, gains, vec, gates, out_proj, gate_in, linear_in, mlp_gate, mlp_up)
 
 
 def mixer_backward_kernel(pos_ref, gm_ref, gate_ref, linear_ref, rate_ref, input_ref, state_ref,
@@ -205,41 +676,40 @@
         return lax.all_to_all(w, "shard", split_axis=1, concat_axis=0, tiled=True)
 
     pos, live = positions_in_run(lengths[0], rows)
-    gains = lax.all_gather(jnp.stack([norm1_gain, norm2_gain]), "shard", axis=1, tiled=True).astype(F32)
+    padded = -(-chans // 128) * 128
     masked = tokens.astype(F32) * live
     scale1 = lax.rsqrt(jnp.mean(masked * masked, axis=1, keepdims=True) + EPSILON)
-    normed = (masked * scale1 * gains[0:1]).astype(BF16)
-    sent = jnp.concatenate([normed, jnp.broadcast_to(pos.astype(BF16), (rows, 128))], axis=1)
-    got = gather(sent)
+    own_gains = jnp.pad(jnp.stack([norm1_gain, norm2_gain]).astype(F32), ((0, 6), (0, 0)))
+    rate_bd, input_bd = block_diagonal(rate_weight), block_diagonal(input_weight)
+    fill = ((0, padded - chans), (0, padded - chans))
+    gates = jnp.concatenate([jnp.pad(rate_bd, fill), jnp.pad(input_bd, fill)], axis=1)
+    vec = jnp.concatenate([conv_kernel, jnp.stack([conv_bias, rate_bias, input_bias, decay_param])]).astype(F32)
+    vec8 = jnp.pad(vec, ((0, 0), (0, padded - chans)))
+    got, gl_w, mlp_w, gains, saved, merged, middle, normed_two_own = forward_call(
+        lengths, tokens, own_gains, vec8, gates, out_proj, gate_in, linear_in, mlp_gate, mlp_up
+    )
+    gains = gains.transpose(1, 0, 2).reshape(8, width)
+    got = got.reshape(total_rows, -1)
     normed_all = got[:, :width]
     pos_all = got[:, width : width + 1].astype(jnp.int32)
-    gate_w, linear_w = columns(gate_in), columns(linear_in)
-    mg_w, mu_w = columns(mlp_gate), columns(mlp_up)
-    gate_pre = mm(normed_all, gate_w)
-    linear_pre = mm(normed_all, linear_w)
-    vec = jnp.stack([conv_bias, rate_bias, input_bias, decay_param]).astype(F32)
-    ck = conv_kernel.astype(F32)
-    rate_bd, input_bd = block_diagonal(rate_weight), block_diagonal(input_weight)
+    gl_w = gl_w.reshape(width, -1)
+    gate_w, linear_w = gl_w[:, :chans], gl_w[:, padded : padded + chans]
+    mlp_w = mlp_w.reshape(width, -1)
+    mg_w, mu_w = mlp_w[:, : mlp_w.shape[1] // 2], mlp_w[:, mlp_w.shape[1] // 2 :]
+    gate_pre, linear_pre, rate_pre, input_pre, state = [
+        saved[:, j].reshape(total_rows, padded)[:, :chans] for j in range(5)
+    ]
+    merged = merged.reshape(total_rows, padded)[:, :chans]
+    vec, ck = vec[4:], vec[:4]
     row_spec = pl.BlockSpec((rows, chans), lambda i: (i, 0))
     pos_spec = pl.BlockSpec((rows, 1), lambda i: (i, 0))
 
     def whole(a):
         return pl.BlockSpec(a.shape, lambda i: (0,) * a.ndim)
 
-    f_shape = jax.ShapeDtypeStruct((total_rows, chans), F32)
     b_shape = jax.ShapeDtypeStruct((total_rows, chans), BF16)
-    merged, rate_pre, input_pre, state = pl.pallas_call(
-        mixer_forward_kernel,
-        grid=(n_shard,),
-        in_specs=[pos_spec, row_spec, row_spec, whole(ck), whole(vec), whole(rate_bd), whole(input_bd)],
-        out_specs=[row_spec] * 4,
-        out_shape=[b_shape, f_shape, f_shape, f_shape],
-        compiler_params=pltpu.CompilerParams(vmem_limit_bytes=32 * 2**20),
-        name="mixer_forward",
-    )(pos_all, gate_pre, linear_pre, ck, vec, rate_bd, input_bd)
-    middle = masked + scatter(mm(merged, out_proj))
     scale2 = lax.rsqrt(jnp.mean(middle * middle, axis=1, keepdims=True) + EPSILON)
-    normed_two = gather((middle * scale2 * gains[1:2]).astype(BF16))
+    normed_two = gather(normed_two_own)
     g_out = cotangent.astype(F32) * live
     g_low = gather(g_out.astype(BF16))
     gate_mlp = mm(normed_two, mg_w)

time: 1430 us -> 1190 us (0.83)
  waiting for transfers between devices: 1120 us -> 820 us
  Pallas kernels: 21.5 us -> 162 us
  blocking collectives: 28 us -> 5.76 us
  local copies, waits for them, and re-layouts: 66 us -> 44 us
  starting transfers between devices: 35.9 us -> 17.8 us
    all_to_all x4 -> x0, waiting for transfers between devices: 329 us -> none  [columns(): return lax.all_to_all(w, 'shard', split_axis=1, concat_axis=0, tiled=True)]
    pallas_call x1, Pallas kernels: 7.8 us -> 148 us  [forward_call(): pl.pallas_call(forward_kernel, out_shape=out_shape, in_specs=[pl.BlockSpe...]
    all_gather x4 -> x3, waiting for transfers between devices: 111 us -> 233 us  [gather(): return lax.all_gather(x, 'shard', axis=0, tiled=True)]
    reduce_scatter x4 -> x3, waiting for transfers between devices: 256 us -> 168 us  [scatter(): lax.psum_scatter(x.astype(BF16), 'shard', scatter_dimension=0, tiled=True)]
    all_gather x1 -> x0, blocking collectives: 22.2 us -> none  [per_device_split(): lax.all_gather(jnp.stack([norm1_gain, norm2_gain]), 'shard', axis=1, tile...]
    unnamed x118 -> x70, local copies, waits for them, and re-layouts: 35.5 us -> 17.1 us
    all_to_all x4 -> x0, starting transfers between devices: 17.5 us -> none  [columns(): return lax.all_to_all(w, 'shard', split_axis=1, concat_axis=0, tiled=True)]
    all_to_all x4 -> x0, local copies, waits for them, and re-layouts: 14.4 us -> none  [columns(): return lax.all_to_all(w, 'shard', split_axis=1, concat_axis=0, tiled=True)]
  transfers between devices with their start and end apart: 18 -> 12, of which waited for: 13 -> 10; matrix products, arithmetic and copies ran while one was open for 8% -> 8% of each run, Pallas kernels for 1% -> 1%
where the time goes in v2:
time: 1190 us; the launch traced here: 1180 us
  waiting for transfers between devices  820 us (69%)
  Pallas kernels  162 us (14%)
  matrix products  92.2 us (8%)
  local copies, waits for them, and re-layouts  44 us (4%)
  other arithmetic  25.4 us (2%)
  starting transfers between devices  17.8 us (1%)
  between operations  17.2 us (1%)
    psum x1, waiting for transfers between devices, per_device_split(): lax.psum((gain_terms, back_columns(term_gi), back_columns(term_li), small...  236 us
    all_gather x3, waiting for transfers between devices, gather(): return lax.all_gather(x, 'shard', axis=0, tiled=True)  233 us
    reduce_scatter x3, waiting for transfers between devices, scatter(): lax.psum_scatter(x.astype(BF16), 'shard', scatter_dimension=0, tiled=True)  168 us
    pallas_call x1, Pallas kernels, forward_call(): pl.pallas_call(forward_kernel, out_shape=out_shape, in_specs=[pl.BlockSpe...  148 us
    all_to_all x4, waiting for transfers between devices, back_columns(): return lax.all_to_all(t, 'shard', split_axis=0, concat_axis=1, tiled=True)  137 us
    unnamed x9, waiting for transfers between devices  46.3 us
    dot_general x6, matrix products, mm_nt(): lax.dot_general(a, b, (((1,), (1,)), ((), ())), preferred_element_type=F32)  37.7 us
    dot_general x6, matrix products, mm_tn(): lax.dot_general(a, b, (((0,), (0,)), ((), ())), preferred_element_type=F32)  32.1 us
  transfers between devices with their start and end apart: 12, of which 10 were waited for; matrix products, arithmetic and copies ran while one was open for 8% of the time, Pallas kernels for 1%

profile of v2, /device:TPU:0, one launch (start us, length us, event | category | flops | bytes accessed | tf_op | source)
XLA Modules:
  0.0 1183.7 jit_solution(9302945263984520238)
XLA Ops:
  17.4 147.9 %mixer_forward.1 = (bf16[8,128,2176]{2,1,0:T(8,128)(2,1)}, bf16[8,4,64,768]{3,2,1,0:T(8,128)(2,1)}, bf16[8,4,64,1536]{3,2,1,0:T(8,128)(2,1)}, f32[8,8,256]{2,1,0...) custom-call(s32[1,4]{1,0:T(1,128)} %lengths_ref.1, ...), custom_call_target="tpu_custom_call" | custom-call | tf_op jit(solution)/shard_map/mixer_forward/pallas_call | solution.py:556
  169.4 68.6 %all-gather.4.cloned.1.call-done = bf16[1024,2048]{1,0:T(8,128)(2,1)} async-done(((bf16[128,2048]{1,0:T(8,128)(2,1)}), bf16[1024,2048]{1,0:T(8,128)(2,1)}) %all-gather.4.cloned.1.call-update) | async-done | bytes 4194320 | tf_op jit(solution)/shard_map/all_gather | solution.py:670
  238.0 8.4 fusion.12
  246.3 7.1 fusion.16
  253.4 58.9 %all-gather.6.cloned.1.call-done = bf16[1024,2048]{1,0:T(8,128)(2,1)} async-done(((bf16[128,2048]{1,0:T(8,128)(2,1)}), bf16[1024,2048]{1,0:T(8,128)(2,1)}) %all-gather.6.cloned.1.call-update) | async-done | bytes 4194320 | tf_op jit(solution)/shard_map/all_gather | solution.py:670
  312.3 10.3 multiply_convert_fusion
  322.7 7.0 fusion.14
  330.2 6.9 add_convert_fusion.1
  337.2 6.8 convolution_convert_fusion
  346.4 77.1 %reduce-scatter.9.cloned.1.call-done = bf16[128,2048]{1,0:T(8,128)(2,1)} async-done(((bf16[1024,2048]{1,0:T(8,128)(2,1)}), bf16[128,2048]{1,0:T(8,128)(2,1)}) %reduce-scatter.9.cloned.1.call-update) | async-done | bytes 524304 | tf_op jit(solution)/shard_map/reduce_scatter | solution.py:673
  423.5 1.4 fusion.42
  424.8 90.8 %reduce-scatter.7.cloned.1.call-done = bf16[128,2048]{1,0:T(8,128)(2,1)} async-done(((bf16[1024,2048]{1,0:T(8,128)(2,1)}), bf16[128,2048]{1,0:T(8,128)(2,1)}) %reduce-scatter.7.cloned.1.call-update) | async-done | bytes 524304 | tf_op jit(solution)/shard_map/reduce_scatter | solution.py:673
  515.7 3.0 fusion.58
  518.7 7.9 convolution_convert_fusion.2
  526.6 4.5 all-to-all-start.3
  531.1 1.8 slice_convert_fusion.pos_ref
  532.9 5.8 fusion.60
  539.2 4.9 convolution_convert_fusion.3
  544.1 105.2 %all-gather.8.cloned.1.call-done = bf16[1024,2048]{1,0:T(8,128)(2,1)} async-done(((bf16[128,2048]{1,0:T(8,128)(2,1)}), bf16[1024,2048]{1,0:T(8,128)(2,1)}) %all-gather.8.cloned.1.call-update) | async-done | bytes 4194320 | tf_op jit(solution)/shard_map/all_gather | solution.py:670
  649.3 5.1 fusion.67.gm_ref
  654.4 13.8 %mixer_backward.1 = (bf16[1024,320]{1,0:T(8,128)(2,1)S(1)}, bf16[1024,320]{1,0:T(8,128)(2,1)S(1)}, f32[8,320]{1,0:T(8,128)S(1)}, bf16[320,160]{1,0:T(8,128)(2,1)}, bf16[320,160]{1,0:T(8,128)(2,1)}) custom-call(s32[1024,1]{1,0:T(8,128)S(1)} %copy-done.5, f32[1024,320]{1,0:T(8,128)S(1)} %fusion.67.gm_ref, f32[1024,320]{1,0:T(8,128)S(1)} %bitcast.69, ...), custom_call_target="tpu_custom_call" | custom-call | tf_op jit(solution)/shard_map/mixer_backward/pallas_call | solution.py:738
  669.9 4.6 all-to-all-start.2
  674.8 3.9 fusion.25
  678.7 4.5 add_convert_fusion
  683.2 3.7 fusion.18
  688.1 91.4 %all-to-all-done.2 = bf16[8,256,768]{2,1,0:T(8,128)(2,1)} async-done(((bf16[8,256,768]{2,1,0:T(8,128)(2,1)}), bf16[8,256,768]{2,1,0:T(8,128)(2,1)}, u32[]{:S(2)}, u32[]{:S(2)}) %all-to-all-start.2) | async-done | bytes 3145760 | tf_op jit(solution)/shard_map/all_to_all | solution.py:760
  779.5 3.6 all-to-all-start
  783.1 3.7 fusion.21
  788.0 36.2 %all-to-all-done = bf16[8,256,320]{1,2,0:T(8,128)(2,1)S(1)} async-done(((bf16[8,256,320]{1,2,0:T(8,128)(2,1)}), bf16[8,256,320]{1,2,0:T(8,128)(2,1)S(1)}, u32[]{:S(2)}, u32[]{:S(2)}) %all-to-all-start) | async-done | bytes 1310752 | tf_op jit(solution)/shard_map/all_to_all | solution.py:760
  824.2 4.3 all-to-all-start.1
  828.6 7.1 convolution_convert_fusion.1
  835.7 3.9 copy.82
  839.6 4.0 copy.81
  843.7 1.5 fusion.44
  846.6 4.8 convolution_convert_fusion.4
  851.4 9.2 all-to-all-done.1
  861.9 1.2 fusion.36
  863.1 46.2 %reduce-scatter.13.cloned.1.call-done = bf16[256,2]{1,0:T(8,128)(2,1)} async-done(((bf16[2048,2]{1,0:T(8,128)(2,1)}), bf16[256,2]{1,0:T(8,128)(2,1)}) %reduce-scatter.13.cloned.1.call-update) | async-done | bytes 1040
  910.2 5.8 all-reduce.8
  917.8 236.1 %all-reduce.12.cloned.1.call-done = (bf16[256,2560]{0,1:T(8,128)(2,1)}, bf16[256,2560]{0,1:T(8,128)(2,1)}, bf16[320,160]{1,0:T(8,128)(2,1)}, bf16[320,160]{1,0:T...) async-done(((bf16[256,2560]{0,1:T(8,128)(2,1)}, bf16[256,2560]{0,1:T(8,128)(2,1)}, ...) | async-done | bytes 13574160 | tf_op jit(solution)/shard_map/psum | solution.py:765
  1153.9 1.7 copy.70
  1155.6 1.7 copy.71
  1157.3 2.8 copy.68
  1160.1 3.0 copy.69
  1163.1 3.1 convert_element_type.153
  1166.2 3.4 convert_element_type.155
  1169.7 3.4 convert_element_type.157
  1173.1 3.6 convert_element_type.159
  (117 shorter events, 25.0 us)
Async XLA Ops:
  7.2 230.8 %all-gather.4.cloned.1.call-start = ((), (), s32[]{:S(2)}) async-start(), calls=%async_computation.8 | async-start | bytes 4718592 | tf_op jit(solution)/shard_map/all_gather | solution.py:670
  16.7 0.7 copy-start.3
  17.4 148.0 %copy-start.21 = (s32[1,4]{1,0:T(1,128)S(1)}, s32[1,4]{1,0:T(1,128)}, u32[]{:S(2)}) copy-start(s32[1,4]{1,0:T(1,128)} %lengths_ref.1) | copy-start | bytes 52
  17.4 150.5 %copy-start.11 = (bf16[128,2048]{1,0:T(8,128)(2,1)S(1)}, bf16[128,2048]{1,0:T(8,128)(2,1)}, u32[]{:S(2)}) copy-start(bf16[128,2048]{1,0:T(8,128)(2,1)} %tokens_ref.1) | copy-start | bytes 1572868
  17.4 150.5 %copy-start.19 = (bf16[128,2048]{1,0:T(8,128)(2,1)S(1)}, bf16[128,2048]{1,0:T(8,128)(2,1)}, u32[]{:S(2)}) copy-start(bf16[128,2048]{1,0:T(8,128)(2,1)} %param.20) | copy-start | bytes 1572868
  165.4 147.0 %all-gather.6.cloned.1.call-start = ((), (), s32[]{:S(2)}) async-start(), calls=%async_computation.10 | async-start | bytes 4718592 | tf_op jit(solution)/shard_map/all_gather | solution.py:670
  169.1 254.4 %reduce-scatter.9.cloned.1.call-start = ((), (), s32[]{:S(2)}) async-start(), calls=%async_computation.11 | async-start | bytes 4718592 | tf_op jit(solution)/shard_map/reduce_scatter | solution.py:673
  238.0 8.4 copy-start.22
  322.7 7.1 copy-start.27
  322.7 7.1 copy-start.29
  322.7 14.5 %copy-start.25 = (bf16[1024,768]{1,0:T(8,128)(2,1)}, bf16[1024,768]{1,0:T(8,128)(2,1)S(1)}, u32[]{:S(2)}) copy-start(bf16[1024,768]{1,0:T(8,128)(2,1)S(1)} %get-tuple-element.121) | copy-start | bytes 4718596
  337.2 178.5 %reduce-scatter.7.cloned.1.call-start = ((), (), s32[]{:S(2)}) async-start(), calls=%async_computation.9 | async-start | bytes 4718592 | tf_op jit(solution)/shard_map/reduce_scatter | solution.py:673
  344.1 1.2 copy-start.10
  344.1 305.2 %all-gather.8.cloned.1.call-start = ((), (), s32[]{:S(2)}) async-start(), calls=%async_computation.12 | async-start | bytes 4718592 | tf_op jit(solution)/shard_map/all_gather | solution.py:670
  526.6 143.4 %all-to-all-start.3 = ((bf16[8,256,768]{2,1,0:T(8,128)(2,1)}), bf16[8,256,768]{2,1,0:T(8,128)(2,1)}, u32[]{:S(2)}, u32[]{:S(2)}) async-start(bf16[8,256,768]{2,1,0:T(8,128)(2,1)} %bitcast.21), calls=%async_computation.6 | async-start | bytes 6291456 | tf_op jit(solution)/shard_map/all_to_all | solution.py:760
  532.9 5.8 copy-start.23
  532.9 6.3 copy-start.28
  649.3 5.1 copy-start
  649.3 5.1 copy-start.1
  649.3 5.1 copy-start.2
  649.3 5.1 copy-start.4
  649.3 5.1 copy-start.5
  668.2 0.9 copy-start.6
  669.1 0.9 copy-start.8
  669.9 4.8 copy-start.7
  669.9 109.6 %all-to-all-start.2 = ((bf16[8,256,768]{2,1,0:T(8,128)(2,1)}), bf16[8,256,768]{2,1,0:T(8,128)(2,1)}, u32[]{:S(2)}, u32[]{:S(2)}) async-start(bf16[8,256,768]{2,1,0:T(8,128)(2,1)} %bitcast.75), calls=%async_computation.5 | async-start | bytes 6291456 | tf_op jit(solution)/shard_map/all_to_all | solution.py:760
  674.5 169.1 %reduce-scatter.11.cloned.1.call-start = ((), (), s32[]{:S(2)}) async-start(), calls=%async_computation.13 | async-start | bytes 4718592 | tf_op jit(solution)/shard_map/reduce_scatter | solution.py:673
  674.8 4.0 copy-start.9
  674.8 4.0 copy-start.15
  779.5 44.7 %all-to-all-start = ((bf16[8,256,320]{1,2,0:T(8,128)(2,1)}), bf16[8,256,320]{1,2,0:T(8,128)(2,1)S(1)}, u32[]{:S(2)}, u32[]{:S(2)}) async-start(bf16[8,256,320]{1,2,0:T(8,128)(2,1)} %bitcast.59), calls=%async_computation.3 | async-start | bytes 2621440 | tf_op jit(solution)/shard_map/all_to_all | solution.py:760
  786.8 41.7 %copy-start.26 = (bf16[1024,768]{1,0:T(8,128)(2,1)S(1)}, bf16[1024,768]{1,0:T(8,128)(2,1)}, u32[]{:S(2)}) copy-start(bf16[1024,768]{1,0:T(8,128)(2,1)} %copy-done.25) | copy-start | bytes 4718596
  824.2 11.4 copy-start.13
  824.2 36.3 %all-to-all-start.1 = ((bf16[8,256,320]{1,2,0:T(8,128)(2,1)}), bf16[8,256,320]{1,2,0:T(8,128)(2,1)}, u32[]{:S(2)}, u32[]{:S(2)}) async-start(bf16[8,256,320]{1,2,0:T(8,128)(2,1)} %bitcast.58), calls=%async_computation.4 | async-start | bytes 2621440 | tf_op jit(solution)/shard_map/all_to_all | solution.py:760
  828.5 80.8 %reduce-scatter.13.cloned.1.call-start = ((), (), s32[]{:S(2)}) async-start(), calls=%async_computation.14 | async-start | bytes 589824
  839.6 4.1 copy-start.12
  839.6 7.0 copy-start.24
  846.3 307.6 %all-reduce.12.cloned.1.call-start = ((), (), s32[]{:S(2)}) async-start(), calls=%async_computation.15 | async-start | bytes 27394048 | tf_op jit(solution)/shard_map/psum | solution.py:765
  860.6 1.2 copy-start.14
  860.6 1.4 copy-start.20
  1160.1 6.1 copy-start.18
  1166.2 3.4 copy-start.17
  1169.7 3.5 copy-start.16
Sparse Core Ops, SparseCore 0:
  165.5 72.4 all-gather.3
  240.6 71.6 all-gather.5
  337.3 86.1 reduce-scatter.8
  428.0 87.6 reduce-scatter.6
  518.8 130.4 all-gather.7
  683.3 149.8 reduce-scatter.10
  846.4 62.8 reduce-scatter.12
  913.6 240.1 all-reduce.11

commit v3 on v2

--- a/solution.py
+++ b/solution.py
@@ -282,85 +282,102 @@
 
 class Exchange:
     @classmethod
-    def scratch(cls, shards, sources):
+    def scratch(cls, blocks, count):
         dma = pltpu.SemaphoreType.DMA
-        return [dma((sources, shards)), dma((sources, shards)), dma((3, shards)), dma((3, shards))]
-
-    def __init__(self, sources, full, spans, sems):
-        self.sources, self.full, self.spans = sources, full, spans
+        return [dma((count, blocks)), dma((count, blocks)), dma((3, count, blocks)), dma((3, count, blocks))]
+
+    def __init__(self, sources, views, blocks, sems):
+        self.sources, self.views, self.blocks = sources, views, blocks
         self.send_first, self.recv_first, self.send, self.recv = sems
         self.group, self.shard, _, _ = place()
-        self.shards = full.shape[0]
+        self.home = self.shard if blocks > 1 else 0
         self.core_mate, self.y_mate = mates()
+        self.count = len(sources)
 
     def first(self, j, to, origin):
         return pltpu.make_async_remote_copy(
-            src_ref=self.sources[j](to), dst_ref=self.full.at[origin, self.group, :, self.spans[j]],
+            src_ref=self.sources[j](to), dst_ref=self.views[j](origin, self.group),
             send_sem=self.send_first.at[j, to], recv_sem=self.recv_first.at[j, origin],
             device_id=(self.group, to), device_id_type=MESH_ID,
         )
 
     def own(self, j):
         return pltpu.make_async_copy(
-            self.sources[j](self.shard), self.full.at[self.shard, self.group, :, self.spans[j]],
-            self.recv_first.at[j, self.shard],
+            self.sources[j](self.home), self.views[j](self.home, self.group), self.recv_first.at[j, self.home]
         )
 
-    def pass_on(self, origin, quarter, mate, way):
-        piece = self.full.at[origin, quarter]
+    def pass_on(self, j, origin, quarter, mate, way):
+        piece = self.views[j](origin, quarter)
         return pltpu.make_async_remote_copy(
-            src_ref=piece, dst_ref=piece, send_sem=self.send.at[way, origin], recv_sem=self.recv.at[way, origin],
+            src_ref=piece, dst_ref=piece, send_sem=self.send.at[way, j, origin], recv_sem=self.recv.at[way, j, origin],
             device_id=(mate, self.shard), device_id_type=MESH_ID,
         )
 
+    def others(self, body):
+        if self.blocks > 1:
+            pl.loop(1, self.blocks)(lambda i: body((self.home + i) % self.blocks))
+
     def start(self):
-        for j in range(len(self.sources)):
+        for j in range(self.count):
             self.own(j).start()
 
-        @pl.loop(1, self.shards)
-        def _(i):
-            to = (self.shard + i) % self.shards
-            for j in range(len(self.sources)):
-                self.first(j, to, self.shard).start()
+        def send(to):
+            for j in range(self.count):
+                self.first(j, to, self.home).start()
+
+        self.others(send)
+
+    def both(self, j, origin):
+        self.pass_on(j, origin, self.group, self.y_mate, 1).start()
+        self.pass_on(j, origin, self.group, self.core_mate, 0).start()
 
     def spread(self):
-        for j in range(len(self.sources)):
+        for j in range(self.count):
             self.own(j).wait()
-        self.pass_on(self.shard, self.group, self.core_mate, 0).start()
-        self.pass_on(self.shard, self.group, self.y_mate, 1).start()
-
-        @pl.loop(1, self.shards)
-        def _(i):
-            origin = (self.shard + self.shards - i) % self.shards
-            for j in range(len(self.sources)):
+            self.both(j, self.home)
+
+        def forward(origin):
+            for j in range(self.count):
                 self.first(j, origin, origin).wait_recv()
-            self.pass_on(origin, self.group, self.core_mate, 0).start()
-            self.pass_on(origin, self.group, self.y_mate, 1).start()
+                self.both(j, origin)
+
+        self.others(forward)
+
+    def each(self, body):
+        for j in range(self.count):
+            body(j, self.home)
+
+        def rest(origin):
+            for j in range(self.count):
+                body(j, origin)
+
+        self.others(rest)
 
     def relay(self):
-        @pl.loop(0, self.shards)
-        def _(i):
-            origin = (self.shard + self.shards - i) % self.shards
-            self.pass_on(origin, self.y_mate, self.core_mate, 1).wait_recv()
-            self.pass_on(origin, self.y_mate, self.core_mate, 2).start()
+        def forward(j, origin):
+            self.pass_on(j, origin, self.y_mate, self.core_mate, 1).wait_recv()
+            self.pass_on(j, origin, self.y_mate, self.core_mate, 2).start()
+
+        self.each(forward)
 
     def arrive(self):
-        @pl.loop(0, self.shards)
-        def _(origin):
-            self.pass_on(origin, self.group, self.core_mate, 0).wait_recv()
-            self.pass_on(origin, self.group, self.core_mate, 2).wait_recv()
+        def wait(j, origin):
+            self.pass_on(j, origin, self.group, self.core_mate, 0).wait_recv()
+            self.pass_on(j, origin, self.group, self.core_mate, 2).wait_recv()
+
+        self.each(wait)
 
     def finish(self):
-        @pl.loop(1, self.shards)
-        def _(i):
-            to = (self.shard + i) % self.shards
-            for j in range(len(self.sources)):
-                self.first(j, to, self.shard).wait_send()
-
-        @pl.loop(0, self.shards)
-        def _(origin):
+        def sent(to):
+            for j in range(self.count):
+                self.first(j, to, self.home).wait_send()
+
+        def passed(j, origin):
             for way in range(3):
-                self.pass_on(origin, self.group, self.core_mate, way).wait_send()
+                self.pass_on(j, origin, self.group, self.core_mate, way).wait_send()
+
+        self.others(sent)
+        self.each(passed)
 
 
 def mates():
@@ -435,7 +452,9 @@
             piece = raw[i, :, to * chans : (to + 1) * chans].astype(F32)
             piece = jnp.concatenate([piece, jnp.zeros((quarter_rows, padded - chans), F32)], axis=1)
             quarter[to, :, i * padded : (i + 1) * padded] = piece.astype(BF16)
-    exchange = Exchange([lambda to: quarter.at[to]], weights, [slice(None)], (ex_a, ex_b, ex_c, ex_d))
+    exchange = Exchange(
+        [lambda to: quarter.at[to]], [lambda origin, q: weights.at[origin, q]], shards, (ex_a, ex_b, ex_c, ex_d)
+    )
     exchange.start()
     hidden = mlp_up_ref.shape[1] // shards
 
@@ -443,7 +462,9 @@
         return lambda to: ref.at[pl.ds(group * quarter_rows, quarter_rows), pl.ds(to * hidden, hidden)]
 
     mlp_exchange = Exchange(
-        [part_of(mlp_gate_ref), part_of(mlp_up_ref)], mlp_out, [slice(0, hidden), slice(hidden, 2 * hidden)], (mx_a, mx_b, mx_c, mx_d)
+        [part_of(mlp_gate_ref), part_of(mlp_up_ref)],
+        [lambda origin, q: mlp_out.at[origin, q, :, 0:hidden], lambda origin, q: mlp_out.at[origin, q, :, hidden : 2 * hidden]],
+        shards, (mx_a, mx_b, mx_c, mx_d),
     )
     pos, live = positions_in_run([lengths_ref[0, i] for i in range(3)], rows)
     masked[...] = tokens_ref[...].astype(F32) * live
@@ -578,71 +599,424 @@
     )(lengths, tokens, gains, vec, gates, out_proj, gate_in, linear_in, mlp_gate, mlp_up)
 
 
-def mixer_backward_kernel(pos_ref, gm_ref, gate_ref, linear_ref, rate_ref, input_ref, state_ref,
-                          ck_ref, vec_ref, rw_ref, iw_ref,
-                          gg_ref, gl_ref, small_ref, rate_out_ref, input_out_ref, tr_ref, ti_ref):
-    @pl.when(pl.program_id(0) == 0)
-    def _():
-        small_ref[...] = jnp.zeros_like(small_ref)
-        tr_ref[...] = jnp.zeros_like(tr_ref)
-        ti_ref[...] = jnp.zeros_like(ti_ref)
-
-    pos = pos_ref[...]
-    rows = pos.shape[0]
+class CoreSum:
+    @classmethod
+    def scratch(cls, count):
+        return [pltpu.SemaphoreType.DMA((count, 2))] * 2
+
+    def __init__(self, terms, arrived, sums, sems):
+        self.terms, self.arrived, self.sums = terms, arrived, sums
+        self.send, self.recv = sems
+        group, self.shard, _, _ = place()
+        self.core, self.y = group % 2, group // 2
+        self.core_mate, _ = mates()
+
+    def copy(self, j, half):
+        return pltpu.make_async_remote_copy(
+            src_ref=self.terms[j].at[2 * half + 1 - self.core], dst_ref=self.arrived[j].at[half],
+            send_sem=self.send.at[j, half], recv_sem=self.recv.at[j, half],
+            device_id=(self.core_mate, self.shard), device_id_type=MESH_ID,
+        )
+
+    def start(self):
+        for half in (1 - self.y, self.y):
+            for j in range(len(self.terms)):
+                self.copy(j, half).start()
+
+    def add(self, half):
+        for j in range(len(self.terms)):
+            self.copy(j, half).wait_recv()
+            own = self.sums[j](half)
+
+            @pl.loop(0, self.arrived[j].shape[1])
+            def _(i, j=j, own=own):
+                own[i] = (own[i].astype(F32) + self.arrived[j][half, i].astype(F32)).astype(BF16)
+
+    def finish(self):
+        for half in (0, 1):
+            for j in range(len(self.terms)):
+                self.copy(j, half).wait_send()
+
+
+class LineSum:
+    @classmethod
+    def scratch(cls, count):
+        return [pltpu.SemaphoreType.DMA((count,))] * 2
+
+    def __init__(self, halves, arrived, sums, sems):
+        self.halves, self.arrived, self.sums = halves, arrived, sums
+        self.send, self.recv = sems
+        group, self.shard, _, _ = place()
+        self.y = group // 2
+        _, self.y_mate = mates()
+
+    def copy(self, j):
+        return pltpu.make_async_remote_copy(
+            src_ref=self.halves[j].at[1 - self.y], dst_ref=self.arrived[j],
+            send_sem=self.send.at[j], recv_sem=self.recv.at[j],
+            device_id=(self.y_mate, self.shard), device_id_type=MESH_ID,
+        )
+
+    def start(self):
+        for j in range(len(self.halves)):
+            self.copy(j).start()
+
+    def add(self):
+        for j in range(len(self.halves)):
+            self.copy(j).wait_recv()
+            own = self.sums[j]
+
+            @pl.loop(0, self.arrived[j].shape[0])
+            def _(i, j=j, own=own):
+                own[i] = (own[i].astype(F32) + self.arrived[j][i].astype(F32)).astype(BF16)
+
+    def finish(self):
+        for j in range(len(self.halves)):
+            self.copy(j).wait_send()
+
+
+def split_gains(ref, row, values):
+    size = ref.shape[2]
+    for i in range(ref.shape[0]):
+        ref[i, row : row + 1] = values[:, i * size : (i + 1) * size]
+
+
+def norm_backward(values, gain, grad):
+    scale = rms_scale(values)
+    e = grad * gain
+    back = scale * e - values * (scale * scale * scale) * jnp.mean(values * e, axis=1, keepdims=True)
+    return back, jnp.sum(grad * values * scale, axis=0, keepdims=True)
+
+
+def mlp_kernel(
+    lengths_ref, normed_ref, cotangent_ref, middle_ref, gains_ref, weights_ref, down_ref,
+    mixed_out, half_gu_out, half_down_out, g_middle_ref, gain_ref,
+    normed, g_low, weights, down, act, slope, hidden, grads, parts, term_gu, term_down, core_gu, core_down,
+    a_send, a_recv, b_send, b_recv, core_send, core_recv, load_sem, part_sem, out_sem, *scatter_scratch,
+):
+    _, shard, z, x = place()
+    group = lax.axis_index("group")
+    core_mate, _ = mates()
+    rows, width = normed_ref.shape
+    size = hidden.shape[2]
+    loads = [
+        pltpu.make_async_copy(weights_ref, weights, load_sem.at[0]),
+        pltpu.make_async_copy(down_ref, down, load_sem.at[1]),
+    ]
+    for copy in loads:
+        copy.start()
+    gather = Gather(normed, (a_send, a_recv))
+    gather_g = Gather(g_low, (b_send, b_recv))
+    scatter = Scatter(parts, scatter_scratch)
+    core_sum = CoreSum(
+        [term_gu, term_down], [core_gu, core_down],
+        [lambda half: term_gu.at[2 * half + group % 2], lambda half: term_down.at[2 * half + group % 2]],
+        (core_send, core_recv),
+    )
+    greet(line_peers() + [((core_mate, shard), True)])
+    normed[shard] = normed_ref[...]
+    gather.start()
+    _, live = positions_in_run([lengths_ref[0, i] for i in range(3)], rows)
+    g_low[shard] = (cotangent_ref[...].astype(F32) * live).astype(BF16)
+    gather.step(1)
+    gather.step(2)
+    for copy in loads:
+        copy.wait()
+
+    def part_copy(origin):
+        pair = pl.ds(origin * N_X, N_X)
+        return pltpu.make_async_copy(parts.at[pair], mixed_out.at[pair], part_sem.at[origin])
+
+    @pl.loop(0, N_Z)
+    def _(i):
+        @pl.when(i == 1)
+        def _():
+            gather.step(3)
+            gather_g.start()
+
+        origin = nearest(z, i)
+        gather.wait_across(origin)
+        pair = pl.ds(origin * N_X, N_X)
+        both = mm(normed[pair].reshape(N_X * rows, width), weights[...].reshape(width, 2 * size))
+        value, inclined = gelu_parts(both[:, :size])
+        up = both[:, size:]
+        act[origin] = value
+        slope[origin] = up * inclined
+        hidden[origin] = (value * up).astype(BF16)
+        parts[pair] = mm(hidden[origin], down[...]).astype(BF16).reshape(N_X, rows, width)
+        part_copy(origin).start()
+
+    gather_g.step(1)
+    gather_g.step(2)
+
+    @pl.loop(0, N_Z)
+    def _(i):
+        @pl.when(i == 1)
+        def _():
+            gather_g.step(3)
+
+        origin = nearest(z, i)
+        gather_g.wait_across(origin)
+        pair = pl.ds(origin * N_X, N_X)
+        g_hidden = mm_nt(g_low[pair].reshape(N_X * rows, width), down[...])
+        grads[origin, :, :size] = (g_hidden * slope[origin]).astype(BF16)
+        grads[origin, :, size:] = (g_hidden * act[origin]).astype(BF16)
+        part_copy(origin).wait()
+        back = mm_nt(grads[origin], weights[...].reshape(width, 2 * size))
+        parts[pair] = back.astype(BF16).reshape(N_X, rows, width)
+
+    for i in range(N_Z):
+        scatter.start(i)
+    tile = normed.shape[2] // (N_Z * N_X)
+    total = N_Z * N_X * rows
+
+    @pl.loop(0, size // tile)
+    def _(i):
+        left = hidden[:, :, pl.ds(i * tile, tile)].reshape(total, tile)
+        term = mm_tn(left, g_low[...].reshape(total, width)).astype(BF16)
+        step = term_down.shape[2]
+        for j in range(tile // step):
+            chunk = i * (tile // step) + j
+            term_down[chunk // term_down.shape[1], chunk % term_down.shape[1]] = term[j * step : (j + 1) * step]
+
+    def gu_terms(first, last):
+        @pl.loop(first, last)
+        def _(i):
+            left = normed[:, :, pl.ds(i * tile, tile)].reshape(total, tile)
+            term = mm_tn(left, grads[...].reshape(total, 2 * size)).astype(BF16)
+            term_gu[:, i] = term.reshape(term_gu.shape[0], term_gu.shape[2], 2 * size)
+
+    scatter.step(0)
+    gu_terms(0, N_Z)
+    scatter.step(1)
+    gu_terms(N_Z, 2 * N_Z)
+    core_sum.start()
+    scatter.step(2)
+    outs = []
+    y = group // 2
+    for half in (1 - y, y):
+        core_sum.add(half)
+        for j, (term, out) in enumerate(((term_gu, half_gu_out), (term_down, half_down_out))):
+            outs.append(pltpu.make_async_copy(term.at[2 * half + group % 2], out.at[half], out_sem.at[j, half]))
+            outs[-1].start()
+    scatter.last(g_middle_ref)
+    gain = jnp.concatenate([gains_ref[i] for i in range(N_Z * N_X)], axis=1)[1:2]
+    back, gain_term = norm_backward(middle_ref[...], gain, g_middle_ref[...])
+    g_middle_ref[...] = g_low[shard].astype(F32) + back
+    gain_ref[...] = jnp.zeros_like(gain_ref)
+    split_gains(gain_ref, 1, gain_term)
+    gather.finish()
+    gather_g.finish()
+    core_sum.finish()
+    scatter.finish()
+    for copy in outs:
+        copy.wait()
+
+
+def mlp_call(lengths, normed, cotangent, middle, gains, weights, down):
+    rows, width = normed.shape
+    shards, groups, quarter_rows, both = weights.shape
+    size = down.shape[0]
+    dma = pltpu.SemaphoreType.DMA
+    shape = jax.ShapeDtypeStruct
+    down_term = (size // groups // 64, 64, width)
+    gu_term = (shards, quarter_rows, both)
+    pairs = (N_Z, N_X * rows)
+    return pl.pallas_call(
+        mlp_kernel,
+        out_shape=[
+            shape((shards, rows, width), BF16),
+            shape((2,) + gu_term, BF16),
+            shape((2,) + down_term, BF16),
+            shape((rows, width), F32),
+            shape(gains.shape, F32),
+        ],
+        in_specs=[pl.BlockSpec(memory_space=pltpu.SMEM)] + [vmem_spec()] * 4 + [any_spec()] * 2,
+        out_specs=[any_spec()] * 3 + [vmem_spec()] * 2,
+        scratch_shapes=[
+            pltpu.VMEM((shards, rows, width), BF16),
+            pltpu.VMEM((shards, rows, width), BF16),
+            pltpu.VMEM(weights.shape, BF16),
+            pltpu.VMEM(down.shape, BF16),
+            pltpu.VMEM(pairs + (size,), F32),
+            pltpu.VMEM(pairs + (size,), F32),
+            pltpu.VMEM(pairs + (size,), BF16),
+            pltpu.VMEM(pairs + (both,), BF16),
+            pltpu.VMEM((shards, rows, width), BF16),
+            pltpu.VMEM((groups,) + gu_term, BF16),
+            pltpu.VMEM((groups,) + down_term, BF16),
+            pltpu.VMEM((2,) + gu_term, BF16),
+            pltpu.VMEM((2,) + down_term, BF16),
+        ]
+        + Gather.scratch()
+        + Gather.scratch()
+        + CoreSum.scratch(2)
+        + [dma((2,)), dma((N_Z,)), dma((2, 2))]
+        + Scatter.scratch(rows, width),
+        compiler_params=pltpu.CompilerParams(collective_id=2, has_side_effects=True, vmem_limit_bytes=VMEM_LIMIT),
+        name="mlp",
+    )(lengths, normed, cotangent, middle, gains, weights, down)
+
+
+def mixer_backward(g_merged, saved, pos, vec, gates):
+    gate, linear, rate_pre, input_pre, state = saved
+    width = linear.shape[1]
     masks = [(pos >= k).astype(F32) for k in (1, 2, 3)]
-    index = lax.broadcasted_iota(jnp.int32, pos.shape, 0)
-    later = [
-        jnp.where(index < rows - k, roll_rows(masks[k - 1], -k), 0.0) for k in (1, 2, 3)
-    ]
-    linear = linear_ref[...]
-    kernel = ck_ref[...]
-    conv = conv_rows(linear, kernel, vec_ref[0:1], masks)
-    low = conv.astype(BF16)
-    input_gate = sigmoid(input_ref[...])
-    decay = vec_ref[3:4]
-    rate, a, weight_in = decay_terms(rate_ref[...], decay)
-    state = state_ref[...]
-    g_merged = gm_ref[...]
-    act, slope = gelu_parts(gate_ref[...])
-    gg_ref[...] = (g_merged * state * slope).astype(BF16)
+    later = [roll_rows(jnp.broadcast_to(masks[k - 1], linear.shape), -k) for k in (1, 2, 3)]
+    conv = conv_rows(linear, vec[0:4], vec[4:5], masks)
+    input_gate = sigmoid(input_pre)
+    decay = vec[7:8]
+    rate, a, weight_in = decay_terms(rate_pre, decay)
+    act, slope = gelu_parts(gate)
+    g_gate = (g_merged * state * slope).astype(BF16)
     lam = g_merged * act
     mult = roll_rows(a, -1) * later[0]
     step = 1
-    while step < rows:
+    while step < CAP:
         lam = lam + mult * roll_rows(lam, -step)
-        if 2 * step < rows:
+        if 2 * step < CAP:
             mult = mult * roll_rows(mult, -step)
         step *= 2
     g_a = lam * (roll_rows(state, 1) * masks[0])
-    opened = input_gate * conv
-    g_keep = g_a * a - lam * opened * (a * a) / weight_in
-    slow = RATE_SCALE * rate
+    g_keep = g_a * a - lam * (input_gate * conv) * (a * a) / weight_in
     g_rate = (g_keep * (-RATE_SCALE * softplus_neg(decay)) * (rate * (1.0 - rate))).astype(BF16)
-    g_decay = g_keep * slow * sigmoid(-decay)
+    g_decay = g_keep * (RATE_SCALE * rate) * sigmoid(-decay)
     flow = lam * weight_in
     g_inp = (flow * conv * (input_gate * (1.0 - input_gate))).astype(BF16)
-    g_conv = flow * input_gate + mm_nt(g_rate, rw_ref[...]) + mm_nt(g_inp, iw_ref[...])
-    g_linear = g_conv * kernel[0:1]
+    g_conv = flow * input_gate + mm_nt(jnp.concatenate([g_rate, g_inp], axis=1), gates)
+    g_linear = g_conv * vec[0:1]
     sums = [jnp.sum(g_conv * linear, axis=0, keepdims=True)]
     for k in (1, 2, 3):
-        g_linear = g_linear + kernel[k : k + 1] * (roll_rows(g_conv, -k) * later[k - 1])
+        g_linear = g_linear + vec[k : k + 1] * (roll_rows(g_conv, -k) * later[k - 1])
         sums.append(jnp.sum(g_conv * (roll_rows(linear, k) * masks[k - 1]), axis=0, keepdims=True))
-    gl_ref[...] = g_linear.astype(BF16)
-    sums.append(jnp.sum(g_conv, axis=0, keepdims=True))
-    sums.append(jnp.sum(g_rate.astype(F32), axis=0, keepdims=True))
-    sums.append(jnp.sum(g_inp.astype(F32), axis=0, keepdims=True))
-    sums.append(jnp.sum(g_decay, axis=0, keepdims=True))
-    small_ref[...] += jnp.concatenate(sums, axis=0)
-    tr_ref[...] += mm_tn(low, g_rate)
-    ti_ref[...] += mm_tn(low, g_inp)
-
-    @pl.when(pl.program_id(0) == pl.num_programs(0) - 1)
-    def _():
-        size = rate_out_ref.shape[1]
-        for h in range(rate_out_ref.shape[0] // size):
-            part = slice(h * size, (h + 1) * size)
-            rate_out_ref[part] = tr_ref[part, part].astype(BF16)
-            input_out_ref[part] = ti_ref[part, part].astype(BF16)
+    for value in (g_conv, g_rate.astype(F32), g_inp.astype(F32), g_decay):
+        sums.append(jnp.sum(value, axis=0, keepdims=True))
+    return g_gate, g_linear.astype(BF16), jnp.concatenate(sums, axis=0), conv.astype(BF16), g_rate, g_inp
+
+
+def backward_kernel(
+    lengths_ref, tokens_ref, g_middle_ref, gains_ref, gain_in_ref, vec_ref, gates_ref, out_proj_ref,
+    half_gu_ref, half_down_ref, weights_ref, saved_ref, merged_ref, gathered_ref,
+    grad_gate_out, grad_up_out, grad_down_out, term_gl_out, term_out_out, grad_tokens_ref, gain_ref, small_ref, term_bd_ref,
+    g_mix, normed, weights, saved, merged, grads, parts, term_gl, term_out, total_bd, g_normed,
+    sum_gu, sum_down, line_gu, line_down,
+    a_send, a_recv, line_send, line_recv, ex_a, ex_b, ex_c, ex_d, dn_a, dn_b, dn_c, dn_d, load_sem, out_sem, *scatter_scratch,
+):
+    group, shard, z, x = place()
+    y = group // 2
+    shards = N_Z * N_X
+    rows, width = tokens_ref.shape
+    padded = vec_ref.shape[1]
+    total = shards * rows
+    chans = out_proj_ref.shape[0]
+    loads = [
+        pltpu.make_async_copy(source, target, load_sem.at[i])
+        for i, (source, target) in enumerate((
+            (half_gu_ref.at[y], sum_gu), (half_down_ref.at[y], sum_down),
+            (saved_ref, saved), (weights_ref, weights), (gathered_ref, normed), (merged_ref, merged),
+        ))
+    ]
+    for copy in loads:
+        copy.start()
+    gather = Gather(g_mix, (a_send, a_recv))
+    scatter = Scatter(parts, scatter_scratch)
+    line_sum = LineSum([half_gu_ref, half_down_ref], [line_gu, line_down], [sum_gu, sum_down], (line_send, line_recv))
+    half = sum_gu.shape[2] // 2
+    quarter_rows = sum_gu.shape[1]
+
+    def columns(ref):
+        return lambda origin, quarter: ref.at[pl.ds(quarter * quarter_rows, quarter_rows), pl.ds(origin * half, half)]
+
+    exchange = Exchange(
+        [lambda to: sum_gu.at[to, :, 0:half], lambda to: sum_gu.at[to, :, half : 2 * half]],
+        [columns(grad_gate_out), columns(grad_up_out)], shards, (ex_a, ex_b, ex_c, ex_d),
+    )
+    down_exchange = Exchange(
+        [lambda to: sum_down], [lambda origin, quarter: grad_down_out.at[quarter]], 1, (dn_a, dn_b, dn_c, dn_d)
+    )
+    greet(all_peers())
+    line_sum.start()
+    g_mix[shard] = g_middle_ref[...].astype(BF16)
+    gather.start()
+    small_ref[...] = jnp.zeros_like(small_ref)
+    total_bd[...] = jnp.zeros_like(total_bd)
+    gather.step(1)
+    gather.step(2)
+    for copy in loads:
+        copy.wait()
+
+    @pl.loop(0, N_Z)
+    def _(i):
+        @pl.when(i == 1)
+        def _():
+            gather.step(3)
+
+        origin = nearest(z, i)
+        gather.wait_across(origin)
+        pair = pl.ds(origin * N_X, N_X)
+        g_merged = mm_nt(g_mix[pair].reshape(N_X * rows, width), out_proj_ref[...])
+        g_merged = jnp.concatenate([g_merged, jnp.zeros((N_X * rows, padded - chans), F32)], axis=1)
+        where = normed[pair, :, width:].reshape(N_X * rows, normed.shape[2] - width)[:, :1].astype(F32)
+        g_gate, g_linear, sums, low, g_rate, g_inp = mixer_backward(
+            g_merged, [saved[origin, j] for j in range(5)], where, vec_ref[...], gates_ref[...]
+        )
+        grads[origin, :, :padded] = g_gate
+        grads[origin, :, padded:] = g_linear
+        small_ref[...] += sums
+        total_bd[0] += mm_tn(low, g_rate)
+        total_bd[1] += mm_tn(low, g_inp)
+        back = mm_nt(grads[origin], weights[...].reshape(width, 2 * padded))
+        parts[pair] = back.astype(BF16).reshape(N_X, rows, width)
+
+    for i in range(N_Z):
+        scatter.start(i)
+    line_sum.add()
+    exchange.start()
+    down_exchange.start()
+    tile = width // shards
+
+    @pl.loop(0, shards)
+    def _(i):
+        left = normed[:, :, pl.ds(i * tile, tile)].reshape(total, tile)
+        term = mm_tn(left, grads[...].reshape(total, 2 * padded)).astype(BF16)
+        term_gl[:, i] = term.reshape(term_gl.shape[0], term_gl.shape[2], 2 * padded)
+
+    scatter.step(0)
+    down_exchange.spread()
+    exchange.spread()
+    term = mm_tn(merged[...].reshape(total, padded), g_mix[...].reshape(total, width))
+    term_out[...] = term[:chans].astype(BF16).reshape(term_out.shape)
+    outs = [
+        pltpu.make_async_copy(term_gl, term_gl_out, out_sem.at[0]),
+        pltpu.make_async_copy(term_out, term_out_out, out_sem.at[1]),
+    ]
+    for copy in outs:
+        copy.start()
+    scatter.step(1)
+    size = term_bd_ref.shape[1] // 2
+    for h in range(chans // size):
+        part = slice(h * size, (h + 1) * size)
+        both = jnp.concatenate([total_bd[0, part, part], total_bd[1, part, part]], axis=1)
+        term_bd_ref[part] = both.astype(BF16)
+    scatter.step(2)
+    down_exchange.relay()
+    exchange.relay()
+    scatter.last(g_normed)
+    _, live = positions_in_run([lengths_ref[0, i] for i in range(3)], rows)
+    masked = tokens_ref[...].astype(F32) * live
+    gain = jnp.concatenate([gains_ref[i] for i in range(shards)], axis=1)[0:1]
+    back, gain_term = norm_backward(masked, gain, g_normed[...])
+    grad_tokens_ref[...] = ((g_middle_ref[...] + back) * live).astype(BF16)
+    gain_ref[...] = gain_in_ref[...]
+    split_gains(gain_ref, 0, gain_term)
+    gather.finish()
+    line_sum.finish()
+    for one in (down_exchange, exchange):
+        one.arrive()
+        one.finish()
+    scatter.finish()
+    for copy in outs:
+        copy.wait()
 
 
 def block_diagonal(weight):
@@ -656,120 +1030,228 @@
     return jnp.concatenate(parts, axis=0)
 
 
+def backward_call(
+    head, lengths, tokens, g_middle, gains, gain_terms, vec, gates, out_proj, half_gu, half_down, weights, saved, merged, gathered
+):
+    rows, width = tokens.shape
+    shards, groups = N_Z * N_X, weights.shape[1]
+    quarter_rows, both = half_gu.shape[2:]
+    padded = vec.shape[1]
+    chans = out_proj.shape[0]
+    dma = pltpu.SemaphoreType.DMA
+    shape = jax.ShapeDtypeStruct
+    gl_term = (groups, shards, quarter_rows, 2 * padded)
+    out_term = (groups, chans // groups // 16, 16, width)
+    return pl.pallas_call(
+        backward_kernel,
+        out_shape=[
+            shape((groups * quarter_rows, shards * both // 2), BF16),
+            shape((groups * quarter_rows, shards * both // 2), BF16),
+            shape((groups,) + half_down.shape[1:], BF16),
+            shape(gl_term, BF16),
+            shape(out_term, BF16),
+            shape((rows, width), BF16),
+            shape(gains.shape, F32),
+            shape(vec.shape, F32),
+            shape((chans, 2 * head), BF16),
+        ],
+        in_specs=[pl.BlockSpec(memory_space=pltpu.SMEM)] + [vmem_spec()] * 7 + [any_spec()] * 6,
+        out_specs=[any_spec()] * 5 + [vmem_spec()] * 4,
+        scratch_shapes=[
+            pltpu.VMEM((shards, rows, width), BF16),
+            pltpu.VMEM(gathered.shape, BF16),
+            pltpu.VMEM(weights.shape, BF16),
+            pltpu.VMEM(saved.shape, F32),
+            pltpu.VMEM(merged.shape, BF16),
+            pltpu.VMEM((N_Z, N_X * rows, 2 * padded), BF16),
+            pltpu.VMEM((shards, rows, width), BF16),
+            pltpu.VMEM(gl_term, BF16),
+            pltpu.VMEM(out_term, BF16),
+            pltpu.VMEM((2, padded, padded), F32),
+            pltpu.VMEM((rows, width), F32),
+        ]
+        + [pltpu.VMEM(half.shape[1:], BF16) for half in (half_gu, half_down)] * 2
+        + Gather.scratch()
+        + LineSum.scratch(2)
+        + Exchange.scratch(shards, 2)
+        + Exchange.scratch(1, 1)
+        + [dma((6,)), dma((2,))]
+        + Scatter.scratch(rows, width),
+        compiler_params=pltpu.CompilerParams(collective_id=3, has_side_effects=True, vmem_limit_bytes=VMEM_LIMIT),
+        name="mixer_backward",
+    )(lengths, tokens, g_middle, gains, gain_terms, vec, gates, out_proj, half_gu, half_down, weights, saved, merged, gathered)
+
+
+def final_kernel(
+    lengths_ref, middle_ref, small_ref, gain_ref, parts_ref, term_gl_ref, term_out_ref, term_bd_ref,
+    gl_out, out_out, bd_out, mixed_ref, small_out_ref,
+    sum_gl, sum_out, sum_bd, core_gl, core_out, core_bd, line_gl, line_out, line_bd, gains, packed, packs, result,
+    core_send, core_recv, line_send, line_recv, ex_a, ex_b, ex_c, ex_d, sp_a, sp_b, sp_c, sp_d, sq_a, sq_b, sq_c, sq_d,
+    gain_send, gain_recv, pack_send, pack_recv, load_sem, *scatter_scratch,
+):
+    group, shard, z, x = place()
+    y, core = group // 2, group % 2
+    shards = N_Z * N_X
+    rows, width = middle_ref.shape
+    core_mate, y_mate = mates()
+    terms = [term_gl_ref, term_out_ref, term_bd_ref]
+    sums = [sum_gl, sum_out, sum_bd]
+    loads = [
+        pltpu.make_async_copy(term.at[2 * half + core], total.at[half], load_sem.at[j, half])
+        for j, (term, total) in enumerate(zip(terms, sums)) for half in (0, 1)
+    ]
+    for copy in loads:
+        copy.start()
+    core_sum = CoreSum(
+        terms, [core_gl, core_out, core_bd], [lambda half, total=total: total.at[half] for total in sums], (core_send, core_recv)
+    )
+    line_sum = LineSum(sums, [line_gl, line_out, line_bd], [total.at[y] for total in sums], (line_send, line_recv))
+    scatter = Scatter(parts_ref, scatter_scratch)
+    exchanges = [
+        Exchange(
+            [lambda to: sum_gl.at[y, to]], [lambda origin, quarter: gl_out.at[origin, quarter]], shards, (ex_a, ex_b, ex_c, ex_d)
+        ),
+        Exchange([lambda to: sum_out.at[y]], [lambda origin, quarter: out_out.at[quarter]], 1, (sp_a, sp_b, sp_c, sp_d)),
+        Exchange([lambda to: sum_bd.at[y]], [lambda origin, quarter: bd_out.at[quarter]], 1, (sq_a, sq_b, sq_c, sq_d)),
+    ]
+
+    def gain_copy(to, origin):
+        return pltpu.make_async_remote_copy(
+            src_ref=gain_ref.at[to], dst_ref=gains.at[origin], send_sem=gain_send.at[to], recv_sem=gain_recv.at[origin],
+            device_id=(group, to), device_id_type=MESH_ID,
+        )
+
+    def pack_copy(i):
+        return pltpu.make_async_remote_copy(
+            src_ref=packed, dst_ref=packs.at[i], send_sem=pack_send.at[i], recv_sem=pack_recv.at[i],
+            device_id=((core_mate, y_mate, 3 - group)[i], shard), device_id_type=MESH_ID,
+        )
+
+    greet(all_peers() + [((3 - group, shard), True)])
+    core_sum.start()
+    for i in range(1, shards):
+        gain_copy((shard + i) % shards, shard).start()
+    for i in range(N_Z):
+        scatter.start(i)
+    for copy in loads:
+        copy.wait()
+    core_sum.add(1 - y)
+    line_sum.start()
+    core_sum.add(y)
+    total = gain_ref[shard]
+    for i in range(1, shards):
+        origin = (shard + i) % shards
+        gain_copy(origin, origin).wait_recv()
+        total = total + gains[origin]
+    packed[0:8] = small_ref[...]
+    packed[8:16] = jnp.concatenate([total, jnp.zeros((8, packed.shape[1] - total.shape[1]), F32)], axis=1)
+    for i in range(3):
+        pack_copy(i).start()
+    scatter.step(0)
+    scatter.step(1)
+    line_sum.add()
+    for one in exchanges:
+        one.start()
+    for one in exchanges[1:]:
+        one.spread()
+    scatter.step(2)
+    exchanges[0].spread()
+    scatter.last(result)
+    _, live = positions_in_run([lengths_ref[0, i] for i in range(3)], rows)
+    mixed_ref[...] = ((middle_ref[...] + result[...]) * live).astype(BF16)
+    total = packed[...]
+    for i in range(3):
+        pack_copy(i).wait_recv()
+        total = total + packs[i]
+    small_out_ref[...] = total
+    for one in exchanges[1:] + exchanges[:1]:
+        one.relay()
+    for i in range(1, shards):
+        gain_copy((shard + i) % shards, shard).wait_send()
+    for i in range(3):
+        pack_copy(i).wait_send()
+    core_sum.finish()
+    line_sum.finish()
+    scatter.finish()
+    for one in exchanges:
+        one.arrive()
+        one.finish()
+
+
+def final_call(lengths, middle, small, gain_terms, parts, term_gl, term_out, term_bd):
+    rows, width = middle.shape
+    shards = N_Z * N_X
+    terms = (term_gl, term_out, term_bd)
+    dma = pltpu.SemaphoreType.DMA
+    shape = jax.ShapeDtypeStruct
+    groups = term_gl.shape[0]
+    packed = (16, small.shape[1])
+    return pl.pallas_call(
+        final_kernel,
+        out_shape=[
+            shape((shards, groups) + term_gl.shape[2:], BF16),
+            shape(term_out.shape, BF16),
+            shape(term_bd.shape, BF16),
+            shape((rows, width), BF16),
+            shape(packed, F32),
+        ],
+        in_specs=[pl.BlockSpec(memory_space=pltpu.SMEM)] + [vmem_spec()] * 4 + [any_spec()] * 3,
+        out_specs=[any_spec()] * 3 + [vmem_spec()] * 2,
+        scratch_shapes=[pltpu.VMEM((2,) + term.shape[1:], BF16) for term in terms] * 2
+        + [pltpu.VMEM(term.shape[1:], BF16) for term in terms]
+        + [
+            pltpu.VMEM(gain_terms.shape, F32),
+            pltpu.VMEM(packed, F32),
+            pltpu.VMEM((3,) + packed, F32),
+            pltpu.VMEM((rows, width), F32),
+        ]
+        + CoreSum.scratch(3)
+        + LineSum.scratch(3)
+        + Exchange.scratch(shards, 1)
+        + Exchange.scratch(1, 1) * 2
+        + [dma((shards,)), dma((shards,)), dma((3,)), dma((3,)), dma((3, 2))]
+        + Scatter.scratch(rows, width),
+        compiler_params=pltpu.CompilerParams(collective_id=4, has_side_effects=True, vmem_limit_bytes=VMEM_LIMIT),
+        name="last_sums",
+    )(lengths, middle, small, gain_terms, parts, term_gl, term_out, term_bd)
+
+
 def per_device_split(
     tokens, lengths, cotangent, norm1_gain, gate_in, linear_in, conv_kernel, conv_bias, rate_weight,
     rate_bias, input_weight, input_bias, decay_param, out_proj, norm2_gain, mlp_gate, mlp_up, mlp_down,
 ):
-    rows, width = tokens.shape
-    n_shard = lax.axis_size("shard")
-    size = rate_weight.shape[1]
-    chans = rate_weight.shape[0]
-    total_rows = rows * n_shard
-
-    def gather(x):
-        return lax.all_gather(x, "shard", axis=0, tiled=True)
-
-    def scatter(x):
-        return lax.psum_scatter(x.astype(BF16), "shard", scatter_dimension=0, tiled=True).astype(F32)
-
-    def columns(w):
-        return lax.all_to_all(w, "shard", split_axis=1, concat_axis=0, tiled=True)
-
-    pos, live = positions_in_run(lengths[0], rows)
+    width = tokens.shape[1]
+    chans, size = rate_weight.shape
     padded = -(-chans // 128) * 128
-    masked = tokens.astype(F32) * live
-    scale1 = lax.rsqrt(jnp.mean(masked * masked, axis=1, keepdims=True) + EPSILON)
     own_gains = jnp.pad(jnp.stack([norm1_gain, norm2_gain]).astype(F32), ((0, 6), (0, 0)))
-    rate_bd, input_bd = block_diagonal(rate_weight), block_diagonal(input_weight)
     fill = ((0, padded - chans), (0, padded - chans))
-    gates = jnp.concatenate([jnp.pad(rate_bd, fill), jnp.pad(input_bd, fill)], axis=1)
+    gates = jnp.concatenate(
+        [jnp.pad(block_diagonal(rate_weight), fill), jnp.pad(block_diagonal(input_weight), fill)], axis=1
+    )
     vec = jnp.concatenate([conv_kernel, jnp.stack([conv_bias, rate_bias, input_bias, decay_param])]).astype(F32)
-    vec8 = jnp.pad(vec, ((0, 0), (0, padded - chans)))
-    got, gl_w, mlp_w, gains, saved, merged, middle, normed_two_own = forward_call(
-        lengths, tokens, own_gains, vec8, gates, out_proj, gate_in, linear_in, mlp_gate, mlp_up
-    )
-    gains = gains.transpose(1, 0, 2).reshape(8, width)
-    got = got.reshape(total_rows, -1)
-    normed_all = got[:, :width]
-    pos_all = got[:, width : width + 1].astype(jnp.int32)
-    gl_w = gl_w.reshape(width, -1)
-    gate_w, linear_w = gl_w[:, :chans], gl_w[:, padded : padded + chans]
-    mlp_w = mlp_w.reshape(width, -1)
-    mg_w, mu_w = mlp_w[:, : mlp_w.shape[1] // 2], mlp_w[:, mlp_w.shape[1] // 2 :]
-    gate_pre, linear_pre, rate_pre, input_pre, state = [
-        saved[:, j].reshape(total_rows, padded)[:, :chans] for j in range(5)
-    ]
-    merged = merged.reshape(total_rows, padded)[:, :chans]
-    vec, ck = vec[4:], vec[:4]
-    row_spec = pl.BlockSpec((rows, chans), lambda i: (i, 0))
-    pos_spec = pl.BlockSpec((rows, 1), lambda i: (i, 0))
-
-    def whole(a):
-        return pl.BlockSpec(a.shape, lambda i: (0,) * a.ndim)
-
-    b_shape = jax.ShapeDtypeStruct((total_rows, chans), BF16)
-    scale2 = lax.rsqrt(jnp.mean(middle * middle, axis=1, keepdims=True) + EPSILON)
-    normed_two = gather(normed_two_own)
-    g_out = cotangent.astype(F32) * live
-    g_low = gather(g_out.astype(BF16))
-    gate_mlp = mm(normed_two, mg_w)
-    up_mlp = mm(normed_two, mu_w)
-    act, slope = gelu_parts(gate_mlp)
-    hidden = (act * up_mlp).astype(BF16)
-    mixed = ((middle + scatter(mm(hidden, mlp_down))) * live).astype(BF16)
-    term_down = mm_tn(hidden, g_low).astype(BF16)
-    g_hidden = mm_nt(g_low, mlp_down)
-    g_gate_mlp = (g_hidden * up_mlp * slope).astype(BF16)
-    g_up = (g_hidden * act).astype(BF16)
-    term_mg = mm_tn(normed_two, g_gate_mlp).astype(BF16)
-    term_mu = mm_tn(normed_two, g_up).astype(BF16)
-    g_normed_two = scatter(mm_nt(g_gate_mlp, mg_w) + mm_nt(g_up, mu_w))
-    e2 = g_normed_two * gains[1:2]
-    g_middle = (
-        g_out + scale2 * e2
-        - middle * (scale2 * scale2 * scale2) * jnp.mean(middle * e2, axis=1, keepdims=True)
-    )
-    gain2_term = jnp.sum(g_normed_two * middle * scale2, axis=0)
-    g_mix = gather(g_middle.astype(BF16))
-    term_out = mm_tn(merged, g_mix).astype(BF16)
-    g_merged = mm_nt(g_mix, out_proj)
-    small_shape = jax.ShapeDtypeStruct((8, chans), F32)
-    bd_shape = jax.ShapeDtypeStruct((chans, size), BF16)
-    g_gate, g_linear, small, tr, ti = pl.pallas_call(
-        mixer_backward_kernel,
-        grid=(n_shard,),
-        in_specs=[pos_spec] + [row_spec] * 6 + [whole(ck), whole(vec), whole(rate_bd), whole(input_bd)],
-        out_specs=[row_spec] * 2 + [whole(small_shape), whole(bd_shape), whole(bd_shape)],
-        out_shape=[b_shape, b_shape, small_shape, bd_shape, bd_shape],
-        scratch_shapes=[pltpu.VMEM((chans, chans), F32)] * 2,
-        compiler_params=pltpu.CompilerParams(vmem_limit_bytes=32 * 2**20),
-        name="mixer_backward",
-    )(pos_all, g_merged, gate_pre, linear_pre, rate_pre, input_pre, state, ck, vec, rate_bd, input_bd)
-    term_gi = mm_tn(normed_all, g_gate).astype(BF16)
-    term_li = mm_tn(normed_all, g_linear).astype(BF16)
-    g_normed = scatter(mm_nt(g_gate, gate_w) + mm_nt(g_linear, linear_w))
-    e1 = g_normed * gains[0:1]
-    g_masked = (
-        scale1 * e1
-        - masked * (scale1 * scale1 * scale1) * jnp.mean(masked * e1, axis=1, keepdims=True)
-    )
-    gain1_term = jnp.sum(g_normed * masked * scale1, axis=0)
-    grad_tokens = ((g_middle + g_masked) * live).astype(BF16)
-
-    def back_columns(t):
-        return lax.all_to_all(t, "shard", split_axis=0, concat_axis=1, tiled=True)
-
-    gain_terms = lax.psum_scatter(
-        jnp.stack([gain1_term, gain2_term]).astype(BF16), "shard", scatter_dimension=1, tiled=True
-    )
-    sums = lax.psum(
-        (gain_terms, back_columns(term_gi), back_columns(term_li), small.astype(BF16), tr, ti, term_out,
-         back_columns(term_mg), back_columns(term_mu), term_down), "group",
-    )
-    gain_s, gi_s, li_s, small_s, tr_s, ti_s, out_s, mg_s, mu_s, down_s = [s.astype(F32) for s in sums]
+    vec = jnp.pad(vec, ((0, 0), (0, padded - chans)))
+    gathered, weights, mlp_weights, gains, saved, merged, middle, normed_two = forward_call(
+        lengths, tokens, own_gains, vec, gates, out_proj, gate_in, linear_in, mlp_gate, mlp_up
+    )
+    parts, half_gu, half_down, g_middle, gain_terms = mlp_call(
+        lengths, normed_two, cotangent, middle, gains, mlp_weights, mlp_down
+    )
+    grad_gate, grad_up, grad_down, term_gl, term_out, grad_tokens, gain_terms, small, term_bd = backward_call(
+        size, lengths, tokens, g_middle, gains, gain_terms, vec, gates, out_proj, half_gu, half_down, weights, saved, merged, gathered
+    )
+    groups = term_gl.shape[0]
+    gl, grad_out, bd, mixed, small = final_call(
+        lengths, middle, small, gain_terms, parts, term_gl, term_out, term_bd.reshape(groups, -1, 16, 2 * size)
+    )
+    gl = gl.transpose(1, 2, 0, 3).reshape(gate_in.shape[0], -1, 2 * padded)
+    grad_gate_in = gl[:, :, :chans].astype(F32).reshape(gate_in.shape)
+    grad_linear_in = gl[:, :, padded : padded + chans].astype(F32).reshape(gate_in.shape)
+    bd = bd.reshape(chans, 2 * size).astype(F32)
+    own = norm1_gain.shape[0]
     return (
-        mixed, grad_tokens, gain_s[0], gi_s, li_s, small_s[0:4], small_s[4], tr_s, small_s[5], ti_s,
-        small_s[6], small_s[7], out_s, gain_s[1], mg_s, mu_s, down_s,
+        mixed, grad_tokens, small[8, :own], grad_gate_in, grad_linear_in, small[0:4, :chans], small[4, :chans], bd[:, :size],
+        small[5, :chans], bd[:, size:], small[6, :chans], small[7, :chans], grad_out.reshape(out_proj.shape).astype(F32),
+        small[9, :own], grad_gate.astype(F32), grad_up.astype(F32), grad_down.reshape(mlp_down.shape).astype(F32),
     )
 
 

time: 1190 us -> 574 us (0.48)
  waiting for transfers between devices: 820 us -> 0 us
  Pallas kernels: 162 us -> 529 us
  matrix products: 92.2 us -> 0 us
  local copies, waits for them, and re-layouts: 44 us -> 24.2 us
  starting transfers between devices: 17.8 us -> 0 us
  between operations: 17.2 us -> 0.78 us
    pallas_call x1 -> x3, Pallas kernels: 13.8 us -> 380 us  [the longest x1 152 us: backward_call(): pl.pallas_call(backward_kernel, out_shape=[shape((groups * quarter_rows,...]
    psum x1 -> x0, waiting for transfers between devices: 236 us -> none  [per_device_split(): lax.psum((gain_terms, back_columns(term_gi), back_columns(term_li), small...]
    all_gather x3 -> x0, waiting for transfers between devices: 233 us -> none  [gather(): return lax.all_gather(x, 'shard', axis=0, tiled=True)]
    reduce_scatter x3 -> x0, waiting for transfers between devices: 168 us -> none  [scatter(): lax.psum_scatter(x.astype(BF16), 'shard', scatter_dimension=0, tiled=True)]
    all_to_all x4 -> x0, waiting for transfers between devices: 137 us -> none  [back_columns(): return lax.all_to_all(t, 'shard', split_axis=0, concat_axis=1, tiled=True)]
    dot_general x15 -> x0, matrix products: 92.2 us -> none  [the longest x6 37.7 us: mm_nt(): lax.dot_general(a, b, (((1,), (1,)), ((), ())), preferred_element_type=F32)]
    unnamed x9 -> x0, waiting for transfers between devices: 46.3 us -> none
    all_to_all x4 -> x0, starting transfers between devices: 16.9 us -> none  [back_columns(): return lax.all_to_all(t, 'shard', split_axis=0, concat_axis=1, tiled=True)]
  transfers between devices with their start and end apart: 12 -> 0, of which waited for: 10 -> 0; matrix products, arithmetic and copies ran while one was open for 8% -> 0% of each run, Pallas kernels for 1% -> 0%
where the time goes in v3:
time: 574 us; the launch traced here: 573 us
  Pallas kernels  529 us (92%)
  local copies, waits for them, and re-layouts  24.2 us (4%)
  other arithmetic  19.2 us (3%)
    pallas_call x1, Pallas kernels, backward_call(): pl.pallas_call(backward_kernel, out_shape=[shape((groups * quarter_rows,...  152 us
    pallas_call x1, Pallas kernels, forward_call(): pl.pallas_call(forward_kernel, out_shape=out_shape, in_specs=[pl.BlockSpe...  148 us
    pallas_call x1, Pallas kernels, mlp_call(): pl.pallas_call(mlp_kernel, out_shape=[shape((shards, rows, width), BF16),...  148 us
    pallas_call x1, Pallas kernels, final_call(): pl.pallas_call(final_kernel, out_shape=[shape((shards, groups) + term_gl....  80.5 us
    unnamed x26, local copies, waits for them, and re-layouts  12 us

profile of v3, /device:TPU:0, one launch (start us, length us, event | category | flops | bytes accessed | tf_op | source)
XLA Modules:
  0.0 573.0 jit_solution(15213182122267829532)
XLA Ops:
  0.7 0.7 stack.21
  1.3 0.7 stack.22
  2.0 0.7 stack.24
  2.7 0.7 stack.25
  3.3 0.7 stack.26
  4.0 0.7 stack.27
  4.7 0.7 concatenate.12
  5.4 0.6 pad_convert_fusion.vec_ref
  6.0 0.6 fusion.12.gains_ref
  6.6 1.1 fusion.15
  7.7 0.1 copy.53
  7.8 0.1 copy.54
  7.9 1.1 fusion.16
  9.0 0.1 copy.55
  9.1 0.1 copy.56
  9.2 0.1 fusion.7
  9.3 0.9 fusion.2.gates_ref
  10.2 148.4 %mixer_forward.1 = (bf16[8,128,2176]{2,1,0:T(8,128)(2,1)}, bf16[8,4,64,768]{3,2,1,0:T(8,128)(2,1)}, bf16[8,4,64,1536]{3,2,1,0:T(8,128)(2,1)}, f32[8,8,256]{2,1,0...) custom-call(s32[1,4]{1,0:T(1,128)} %lengths_ref.7, ...), custom_call_target="tpu_custom_call" | custom-call | tf_op jit(solution)/shard_map/mixer_forward/pallas_call | solution.py:577
  158.6 147.9 %mlp.1 = (bf16[8,128,2048]{2,1,0:T(8,128)(2,1)}, bf16[2,8,64,1536]{3,2,1,0:T(8,128)(2,1)}, bf16[2,3,64,2048]{3,2,1,0:T(8,128)(2,1)}, f32[128,2048]{1,0:T(8,128)}, f32[8,8,256]{2,1,0:T(8,128)}) custom-call(s32[1,4]{1,0:T(1,128)} %lengths_ref.7, bf16[128,2048]{1,0:T(8,128)(2,1)} %get-tuple-element.45.normed_ref, bf16[128,2048]{1,0:T(8,128)(2,1)} %cotangent_ref.1, ...), custom_call_target="tpu_custom_call" | custom-call | tf_op jit(solution)/shard_map/mlp/pallas_call | solution.py:825
  306.5 152.0 %mixer_backward.1 = (bf16[256,6144]{1,0:T(8,128)(2,1)}, bf16[256,6144]{1,0:T(8,128)(2,1)}, bf16[4,3,64,2048]{3,2,1,0:T(8,128)(2,1)}, bf16[4,8,64,768]{3,2,1,0:T(...) custom-call(s32[1,4]{1,0:T(1,128)} %lengths_ref.7, ...), custom_call_target="tpu_custom_call" | custom-call | tf_op jit(solution)/shard_map/mixer_backward/pallas_call | solution.py:1045
  458.5 80.5 %last_sums.1 = (bf16[8,4,64,768]{3,2,1,0:T(8,128)(2,1)}, bf16[4,5,16,2048]{3,2,1,0:T(8,128)(2,1)}, bf16[4,5,16,320]{3,2,1,0:T(8,128)(2,1)}, bf16[128,2048]{1,0:T(8,128)(2,1)}, f32[16,384]{1,0:T(8,128)}) custom-call(s32[1,4]{1,0:T(1,128)} %lengths_ref.7, f32[128,2048]{1,0:T(8,128)} %get-tuple-element.44.middle_ref, f32[8,384]{1,0:T(8,128)} %get-tuple-element.56.small_ref, ...), custom_call_target="tpu_custom_call" | custom-call | tf_op jit(solution)/shard_map/last_sums/pallas_call | solution.py:1189
  539.0 3.4 fusion.13
  542.5 1.6 copy.58
  544.0 0.0 copy-done.6
  544.1 0.6 fusion.17
  544.6 0.6 slice.52
  545.2 0.6 slice_reduce_fusion
  545.8 0.0 copy-done.5
  545.8 0.1 bitcast_convert_fusion.4
  545.9 0.2 fusion.14
  546.0 0.8 copy.60
  546.9 0.8 copy.59
  547.7 1.5 bitcast_convert_fusion.2
  549.2 2.1 copy.52
  551.3 2.5 copy.57
  553.9 1.5 bitcast_convert_fusion.3
  555.4 2.1 copy.51
  557.5 3.3 bitcast_convert_fusion.1
  560.7 0.0 copy-done.2
  560.7 3.4 convert_element_type.45
  564.2 0.0 copy-done.1
  564.2 3.4 convert_element_type.46
  567.6 0.0 copy-done
  567.7 3.8 bitcast_convert_fusion
  571.4 0.0 copy-done.4
  571.4 0.8 copy.63
  572.2 0.0 copy-done.3
  572.2 0.8 copy.64
  (7 shorter events, 0.0 us)
Async XLA Ops:
  542.5 1.6 copy-start.6
  542.5 3.4 copy-start.5
  557.5 3.3 copy-start.2
  560.7 3.5 copy-start.1
  564.2 3.5 copy-start
  567.6 3.8 copy-start.4
  567.7 4.6 copy-start.3

commit v4 on v3

--- a/solution.py
+++ b/solution.py
@@ -192,15 +192,19 @@
         return [
             pltpu.VMEM((N_Z, rows, width), BF16),
             pltpu.VMEM((N_Z + 1, rows, width), BF16),
-            pltpu.VMEM((N_Z, rows, width), BF16),
             dma((2, N_Z, cls.CHUNKS)), dma((N_Z, cls.CHUNKS)), dma((N_Z + 1, cls.CHUNKS)),
         ]
 
-    def __init__(self, parts, scratch):
-        self.parts = parts
-        self.across, self.along, self.held, self.send, self.recv_x, self.recv_z = scratch
+    def __init__(self, away, own, scratch):
+        self.away, self.own = away, own
+        self.across, self.along, self.send, self.recv_x, self.recv_z = scratch
         self.group, self.shard, self.z, self.x = place()
-        self.rows = parts.shape[1] // self.CHUNKS
+        self.rows = self.across.shape[1] // self.CHUNKS
+
+    @classmethod
+    def of(cls, parts, scratch):
+        _, _, _, x = place()
+        return cls(lambda k: parts.at[k * N_X + 1 - x], lambda k: parts.at[k * N_X + x], scratch)
 
     def dest(self, i):
         low = jnp.minimum(self.z, N_Z - 1 - self.z)
@@ -212,15 +216,14 @@
 
     def copy_x(self, dest, c):
         return pltpu.make_async_remote_copy(
-            src_ref=self.parts.at[dest * N_X + 1 - self.x, self.span(c)],
-            dst_ref=self.across.at[dest, self.span(c)],
+            src_ref=self.away(dest).at[self.span(c)], dst_ref=self.across.at[dest, self.span(c)],
             send_sem=self.send.at[0, dest, c], recv_sem=self.recv_x.at[dest, c],
             device_id=(self.group, self.z * N_X + 1 - self.x), device_id_type=MESH_ID,
         )
 
     def copy_z(self, dest, slot, c, step):
         return pltpu.make_async_remote_copy(
-            src_ref=self.held.at[dest, self.span(c)], dst_ref=self.along.at[slot, self.span(c)],
+            src_ref=self.own(dest).at[self.span(c)], dst_ref=self.along.at[slot, self.span(c)],
             send_sem=self.send.at[1, dest, c], recv_sem=self.recv_z.at[slot, c],
             device_id=(self.group, (self.z + step) * N_X + self.x), device_id_type=MESH_ID,
         )
@@ -233,21 +236,23 @@
         self.copy_z(0, slot, c, 0).wait_recv()
         return self.along[slot, self.span(c)].astype(F32)
 
+    def half(self, dest, c):
+        return self.own(dest)[self.span(c)].astype(F32) + self.across[dest, self.span(c)].astype(F32)
+
     def step(self, i):
         dest = self.dest(i)
+        own = self.own(dest)
         for c in range(self.CHUNKS):
             self.copy_x(dest, c).wait_recv()
-            own = dest * N_X + self.x
-            self.held[dest, self.span(c)] = (
-                self.parts[own, self.span(c)].astype(F32) + self.across[dest, self.span(c)].astype(F32)
-            ).astype(BF16)
-
-            @pl.when(((dest > self.z) & (self.z > 0)) | ((dest < self.z) & (self.z < N_Z - 1)))
+            inner = ((dest > self.z) & (self.z > 0)) | ((dest < self.z) & (self.z < N_Z - 1))
+
+            @pl.when(inner)
             def _(c=c):
-                self.held[dest, self.span(c)] = (
-                    self.parts[own, self.span(c)].astype(F32) + self.across[dest, self.span(c)].astype(F32)
-                    + self.arrived(dest, c)
-                ).astype(BF16)
+                own[self.span(c)] = (self.half(dest, c) + self.arrived(dest, c)).astype(BF16)
+
+            @pl.when(jnp.logical_not(inner))
+            def _(c=c):
+                own[self.span(c)] = self.half(dest, c).astype(BF16)
 
             @pl.when(dest > self.z)
             def _(c=c):
@@ -260,7 +265,7 @@
     def last(self, out):
         for c in range(self.CHUNKS):
             self.copy_x(self.z, c).wait_recv()
-            out[self.span(c)] = self.parts[self.shard, self.span(c)].astype(F32) + self.across[self.z, self.span(c)].astype(F32)
+            out[self.span(c)] = self.half(self.z, c)
 
             @pl.when(self.z > 0)
             def _(c=c):
@@ -306,10 +311,10 @@
             self.sources[j](self.home), self.views[j](self.home, self.group), self.recv_first.at[j, self.home]
         )
 
-    def pass_on(self, j, origin, quarter, mate, way):
+    def pass_on(self, j, origin, quarter, mate, way, source=None):
         piece = self.views[j](origin, quarter)
         return pltpu.make_async_remote_copy(
-            src_ref=piece, dst_ref=piece, send_sem=self.send.at[way, j, origin], recv_sem=self.recv.at[way, j, origin],
+            src_ref=piece if source is None else source, dst_ref=piece, send_sem=self.send.at[way, j, origin], recv_sem=self.recv.at[way, j, origin],
             device_id=(mate, self.shard), device_id_type=MESH_ID,
         )
 
@@ -327,14 +332,13 @@
 
         self.others(send)
 
-    def both(self, j, origin):
-        self.pass_on(j, origin, self.group, self.y_mate, 1).start()
-        self.pass_on(j, origin, self.group, self.core_mate, 0).start()
+    def both(self, j, origin, source=None):
+        self.pass_on(j, origin, self.group, self.y_mate, 1, source).start()
+        self.pass_on(j, origin, self.group, self.core_mate, 0, source).start()
 
     def spread(self):
         for j in range(self.count):
-            self.own(j).wait()
-            self.both(j, self.home)
+            self.both(j, self.home, self.sources[j](self.home))
 
         def forward(origin):
             for j in range(self.count):
@@ -365,6 +369,8 @@
             self.pass_on(j, origin, self.group, self.core_mate, 0).wait_recv()
             self.pass_on(j, origin, self.group, self.core_mate, 2).wait_recv()
 
+        for j in range(self.count):
+            self.own(j).wait()
         self.each(wait)
 
     def finish(self):
@@ -396,7 +402,7 @@
     masks = [(pos >= k).astype(F32) for k in (1, 2, 3)]
     conv = conv_rows(linear, vec[0:4], vec[4:5], masks)
     width = linear.shape[1]
-    both = mm(conv.astype(BF16), gates)
+    both = mm_nt(conv.astype(BF16), gates)
     rate_pre = both[:, :width] + vec[5:6]
     input_pre = both[:, width:] + vec[6:7]
     _, a, weight_in = decay_terms(rate_pre, vec[7:8])
@@ -416,12 +422,14 @@
 
 
 def forward_kernel(
-    lengths_ref, tokens_ref, gains_ref, vec_ref, gates_ref, out_proj_ref, gate_in_ref, linear_in_ref, mlp_gate_ref, mlp_up_ref,
-    gather_out, weights_out, mlp_out, gains_out, saved_out, merged_out, middle_ref, normed_two_ref,
-    buf, weights, quarter, raw, masked, saved, merged, parts,
+    lengths_ref, tokens_ref, cotangent_ref, gain1_ref, gain2_ref, kernel_ref, bias_ref, rate_bias_ref, input_bias_ref, decay_ref, rate_weight_ref,
+    input_weight_ref, out_proj_ref, gate_in_ref, linear_in_ref, mlp_gate_ref, mlp_up_ref,
+    gather_out, weights_out, mlp_out, gains_out, saved_out, merged_out, middle_ref, normed_two_ref, vec_ref, gates_ref, g_low_out,
+    gains_ref, g_low, buf, weights, quarter, raw, masked, saved, merged, parts,
     gather_a, gather_b, ex_a, ex_b, ex_c, ex_d, mx_a, mx_b, mx_c, mx_d, *rest,
 ):
-    scatter_scratch, (gain_send, gain_recv, raw_sem, out_sem, pair_sem) = rest[:-5], rest[-5:]
+    scatter_scratch, rest = rest[:-8], rest[-8:]
+    gain_send, gain_recv, raw_sem, out_sem, pair_sem, g_sem, g_send, g_recv = rest
     group, shard, z, x = place()
     shards = N_Z * N_X
     rows, width = tokens_ref.shape
@@ -434,6 +442,9 @@
     ]
     for copy in fetch:
         copy.start()
+    gains_ref[...] = jnp.zeros_like(gains_ref)
+    gains_ref[0:1] = gain1_ref[...].astype(F32).reshape(1, -1)
+    gains_ref[1:2] = gain2_ref[...].astype(F32).reshape(1, -1)
     greet(all_peers())
 
     def gain_copy(to, origin):
@@ -468,6 +479,10 @@
     )
     pos, live = positions_in_run([lengths_ref[0, i] for i in range(3)], rows)
     masked[...] = tokens_ref[...].astype(F32) * live
+    g_low[...] = (cotangent_ref[...].astype(F32) * live).astype(BF16)
+    g_copy = pltpu.make_async_copy(g_low, g_low_out.at[shard], g_sem)
+    g_copy.start()
+    g_gather = Gather(g_low_out, (g_send, g_recv))
     for i in range(1, shards):
         gain_copy(shard, (shard + i) % shards).wait_recv()
     gains = jnp.concatenate([gains_out[i] for i in range(shards)], axis=1)
@@ -475,13 +490,23 @@
     buf[shard, :, :width] = (masked[...] * rms_scale(masked[...]) * gains[0:1]).astype(BF16)
     buf[shard, :, width:] = jnp.broadcast_to(pos.astype(F32).astype(BF16), (rows, buf.shape[2] - width))
     gather.start()
+    vec_ref[...] = jnp.zeros_like(vec_ref)
+    vec_ref[0:4, :chans] = kernel_ref[...].astype(F32)
+    for i, ref in enumerate((bias_ref, rate_bias_ref, input_bias_ref, decay_ref)):
+        vec_ref[4 + i : 5 + i, :chans] = ref[...].astype(F32).reshape(1, -1)
+    gates_ref[...] = jnp.zeros_like(gates_ref)
+    size = rate_weight_ref.shape[0]
+    for i, ref in enumerate((rate_weight_ref, input_weight_ref)):
+        for h in range(chans // size):
+            part = slice(h * size, (h + 1) * size)
+            gates_ref[i * padded + h * size : i * padded + (h + 1) * size, part] = ref[:, part]
     gather.step(1)
     exchange.spread()
     gather.step(2)
     exchange.relay()
     mlp_exchange.start()
     exchange.arrive()
-    scatter = Scatter(parts, scatter_scratch)
+    scatter = Scatter.of(parts, scatter_scratch)
 
     def pair_copies(origin):
         return [
@@ -494,6 +519,8 @@
         @pl.when(i == 1)
         def _():
             gather.step(3)
+            g_copy.wait()
+            g_gather.start()
 
         origin = nearest(z, i)
         gather.wait_across(origin)
@@ -520,9 +547,12 @@
         scatter.start(i)
     mlp_exchange.spread()
     scatter.step(0)
+    g_gather.step(1)
     mlp_exchange.relay()
     scatter.step(1)
+    g_gather.step(2)
     scatter.step(2)
+    g_gather.step(3)
     scatter.last(middle_ref)
     middle_ref[...] += masked[...]
     normed_two_ref[...] = (middle_ref[...] * rms_scale(middle_ref[...]) * gains[1:2]).astype(BF16)
@@ -530,6 +560,9 @@
         gain_copy((shard + i) % shards, shard).wait_send()
     gather.finish()
     exchange.finish()
+    for origin in range(N_Z):
+        g_gather.wait_across(origin)
+    g_gather.finish()
     mlp_exchange.arrive()
     mlp_exchange.finish()
     scatter.finish()
@@ -556,10 +589,11 @@
     return pl.BlockSpec(memory_space=pltpu.VMEM)
 
 
-def forward_call(lengths, tokens, gains, vec, gates, out_proj, gate_in, linear_in, mlp_gate, mlp_up):
+def forward_call(lengths, tokens, cotangent, small, out_proj, gate_in, linear_in, mlp_gate, mlp_up):
     rows, width = tokens.shape
     shards, groups = lax.axis_size("shard"), lax.axis_size("group")
-    padded = vec.shape[1]
+    padded = -(-out_proj.shape[0] // 128) * 128
+    gains = (8, width // shards)
     quarter_rows = gate_in.shape[0] // groups
     hidden = mlp_up.shape[1] // shards
     dma = pltpu.SemaphoreType.DMA
@@ -568,18 +602,23 @@
         shape((shards, rows, width + 128), BF16),
         shape((shards, groups, quarter_rows, 2 * padded), BF16),
         shape((shards, groups, quarter_rows, 2 * hidden), BF16),
-        shape((shards,) + gains.shape, F32),
+        shape((shards,) + gains, F32),
         shape((N_Z, 5, N_X * rows, padded), F32),
         shape((N_Z, N_X * rows, padded), BF16),
         shape((rows, width), F32),
         shape((rows, width), BF16),
+        shape((8, padded), F32),
+        shape((2 * padded, padded), BF16),
+        shape((shards, rows, width), BF16),
     ]
     return pl.pallas_call(
         forward_kernel,
         out_shape=out_shape,
-        in_specs=[pl.BlockSpec(memory_space=pltpu.SMEM)] + [vmem_spec()] * 5 + [any_spec()] * 4,
-        out_specs=[any_spec()] * 3 + [vmem_spec()] + [any_spec()] * 2 + [vmem_spec()] * 2,
+        in_specs=[pl.BlockSpec(memory_space=pltpu.SMEM)] + [vmem_spec()] * 12 + [any_spec()] * 4,
+        out_specs=[any_spec()] * 3 + [vmem_spec()] + [any_spec()] * 2 + [vmem_spec()] * 4 + [any_spec()],
         scratch_shapes=[
+            pltpu.VMEM(gains, F32),
+            pltpu.VMEM((rows, width), BF16),
             pltpu.VMEM((shards, rows, width + 128), BF16),
             pltpu.VMEM((shards, groups, quarter_rows, 2 * padded), BF16),
             pltpu.VMEM((shards, quarter_rows, 2 * padded), BF16),
@@ -593,10 +632,11 @@
         + Exchange.scratch(shards, 1)
         + Exchange.scratch(shards, 2)
         + Scatter.scratch(rows, width)
-        + [dma((shards,)), dma((shards,)), dma((2,)), dma((2,)), dma((2, N_Z))],
+        + [dma((shards,)), dma((shards,)), dma((2,)), dma((2,)), dma((2, N_Z)), dma]
+        + Gather.scratch(),
         compiler_params=pltpu.CompilerParams(collective_id=1, has_side_effects=True, vmem_limit_bytes=VMEM_LIMIT),
         name="mixer_forward",
-    )(lengths, tokens, gains, vec, gates, out_proj, gate_in, linear_in, mlp_gate, mlp_up)
+    )(lengths, tokens, cotangent, *small, out_proj, gate_in, linear_in, mlp_gate, mlp_up)
 
 
 class CoreSum:
@@ -604,8 +644,8 @@
     def scratch(cls, count):
         return [pltpu.SemaphoreType.DMA((count, 2))] * 2
 
-    def __init__(self, terms, arrived, sums, sems):
-        self.terms, self.arrived, self.sums = terms, arrived, sums
+    def __init__(self, terms, arrived, sems):
+        self.terms, self.arrived = terms, arrived
         self.send, self.recv = sems
         group, self.shard, _, _ = place()
         self.core, self.y = group % 2, group // 2
@@ -613,24 +653,25 @@
 
     def copy(self, j, half):
         return pltpu.make_async_remote_copy(
-            src_ref=self.terms[j].at[2 * half + 1 - self.core], dst_ref=self.arrived[j].at[half],
+            src_ref=self.terms[j](2 * half + 1 - self.core), dst_ref=self.arrived[j].at[half],
             send_sem=self.send.at[j, half], recv_sem=self.recv.at[j, half],
             device_id=(self.core_mate, self.shard), device_id_type=MESH_ID,
         )
 
-    def start(self):
+    def mine(self, j, half):
+        return self.terms[j](2 * half + self.core)
+
+    def start(self, j):
         for half in (1 - self.y, self.y):
-            for j in range(len(self.terms)):
-                self.copy(j, half).start()
-
-    def add(self, half):
-        for j in range(len(self.terms)):
-            self.copy(j, half).wait_recv()
-            own = self.sums[j](half)
-
-            @pl.loop(0, self.arrived[j].shape[1])
-            def _(i, j=j, own=own):
-                own[i] = (own[i].astype(F32) + self.arrived[j][half, i].astype(F32)).astype(BF16)
+            self.copy(j, half).start()
+
+    def add(self, j, half):
+        self.copy(j, half).wait_recv()
+        own = self.mine(j, half)
+
+        @pl.loop(0, self.arrived[j].shape[1])
+        def _(i):
+            own[i] = (own[i].astype(F32) + self.arrived[j][half, i].astype(F32)).astype(BF16)
 
     def finish(self):
         for half in (0, 1):
@@ -643,35 +684,35 @@
     def scratch(cls, count):
         return [pltpu.SemaphoreType.DMA((count,))] * 2
 
-    def __init__(self, halves, arrived, sums, sems):
-        self.halves, self.arrived, self.sums = halves, arrived, sums
+    def __init__(self, core_sum, arrived, sems):
+        self.core_sum, self.arrived = core_sum, arrived
         self.send, self.recv = sems
-        group, self.shard, _, _ = place()
-        self.y = group // 2
+        self.shard, self.y = core_sum.shard, core_sum.y
         _, self.y_mate = mates()
 
     def copy(self, j):
         return pltpu.make_async_remote_copy(
-            src_ref=self.halves[j].at[1 - self.y], dst_ref=self.arrived[j],
+            src_ref=self.core_sum.mine(j, 1 - self.y), dst_ref=self.arrived[j],
             send_sem=self.send.at[j], recv_sem=self.recv.at[j],
             device_id=(self.y_mate, self.shard), device_id_type=MESH_ID,
         )
 
-    def start(self):
-        for j in range(len(self.halves)):
-            self.copy(j).start()
-
-    def add(self):
-        for j in range(len(self.halves)):
-            self.copy(j).wait_recv()
-            own = self.sums[j]
-
-            @pl.loop(0, self.arrived[j].shape[0])
-            def _(i, j=j, own=own):
-                own[i] = (own[i].astype(F32) + self.arrived[j][i].astype(F32)).astype(BF16)
+    def start(self, j):
+        self.core_sum.add(j, 1 - self.y)
+        self.copy(j).start()
+        self.core_sum.add(j, self.y)
+
+    def add(self, j):
+        self.copy(j).wait_recv()
+        own = self.core_sum.mine(j, self.y)
+
+        @pl.loop(0, self.arrived[j].shape[0])
+        def _(i):
+            own[i] = (own[i].astype(F32) + self.arrived[j][i].astype(F32)).astype(BF16)
 
     def finish(self):
-        for j in range(len(self.halves)):
+        self.core_sum.finish()
+        for j in range(len(self.arrived)):
             self.copy(j).wait_send()
 
 
@@ -689,82 +730,75 @@
 
 
 def mlp_kernel(
-    lengths_ref, normed_ref, cotangent_ref, middle_ref, gains_ref, weights_ref, down_ref,
-    mixed_out, half_gu_out, half_down_out, g_middle_ref, gain_ref,
-    normed, g_low, weights, down, act, slope, hidden, grads, parts, term_gu, term_down, core_gu, core_down,
-    a_send, a_recv, b_send, b_recv, core_send, core_recv, load_sem, part_sem, out_sem, *scatter_scratch,
+    lengths_ref, normed_ref, middle_ref, gains_ref, g_low_ref, weights_ref, down_ref,
+    quarter_gu_out, quarter_down_out, mixed_ref, g_middle_ref, gain_ref,
+    normed, g_low, weights, down, hidden, grads, parts, mixed_parts, term_down,
+    core_down, core_first, core_second, line_down, line_first, line_second, *sems,
 ):
-    _, shard, z, x = place()
-    group = lax.axis_index("group")
-    core_mate, _ = mates()
+    sems = list(sems)
+
+    def take(n):
+        taken = tuple(sems[:n])
+        del sems[:n]
+        return taken
+
+    group, shard, z, x = place()
+    core_mate, y_mate = mates()
     rows, width = normed_ref.shape
     size = hidden.shape[2]
+    load_sem, out_sem = take(2)
     loads = [
-        pltpu.make_async_copy(weights_ref, weights, load_sem.at[0]),
-        pltpu.make_async_copy(down_ref, down, load_sem.at[1]),
+        pltpu.make_async_copy(source, target, load_sem.at[i])
+        for i, (source, target) in enumerate(((weights_ref, weights), (down_ref, down), (g_low_ref, g_low)))
     ]
     for copy in loads:
         copy.start()
-    gather = Gather(normed, (a_send, a_recv))
-    gather_g = Gather(g_low, (b_send, b_recv))
-    scatter = Scatter(parts, scatter_scratch)
+    gather = Gather(normed, take(2))
+    scatter = Scatter.of(parts, take(5))
+    mixed_scatter = Scatter.of(mixed_parts, take(5))
+    middle_tile = N_Z * N_X // 2
     core_sum = CoreSum(
-        [term_gu, term_down], [core_gu, core_down],
-        [lambda half: term_gu.at[2 * half + group % 2], lambda half: term_down.at[2 * half + group % 2]],
-        (core_send, core_recv),
-    )
-    greet(line_peers() + [((core_mate, shard), True)])
+        [lambda q: term_down.at[q], lambda q: weights.at[0:middle_tile, q], lambda q: weights.at[middle_tile : 2 * middle_tile, q]],
+        [core_down, core_first, core_second], take(2),
+    )
+    line_sum = LineSum(core_sum, [line_down, line_first, line_second], take(2))
+    greet(line_peers() + [((core_mate, shard), True), ((y_mate, shard), True)])
     normed[shard] = normed_ref[...]
     gather.start()
-    _, live = positions_in_run([lengths_ref[0, i] for i in range(3)], rows)
-    g_low[shard] = (cotangent_ref[...].astype(F32) * live).astype(BF16)
     gather.step(1)
     gather.step(2)
     for copy in loads:
         copy.wait()
-
-    def part_copy(origin):
-        pair = pl.ds(origin * N_X, N_X)
-        return pltpu.make_async_copy(parts.at[pair], mixed_out.at[pair], part_sem.at[origin])
 
     @pl.loop(0, N_Z)
     def _(i):
         @pl.when(i == 1)
         def _():
             gather.step(3)
-            gather_g.start()
+
+        @pl.when(i == N_Z - 1)
+        def _():
+            for k in range(1, N_Z):
+                mixed_scatter.start(k)
 
         origin = nearest(z, i)
         gather.wait_across(origin)
         pair = pl.ds(origin * N_X, N_X)
-        both = mm(normed[pair].reshape(N_X * rows, width), weights[...].reshape(width, 2 * size))
-        value, inclined = gelu_parts(both[:, :size])
-        up = both[:, size:]
-        act[origin] = value
-        slope[origin] = up * inclined
-        hidden[origin] = (value * up).astype(BF16)
-        parts[pair] = mm(hidden[origin], down[...]).astype(BF16).reshape(N_X, rows, width)
-        part_copy(origin).start()
-
-    gather_g.step(1)
-    gather_g.step(2)
-
-    @pl.loop(0, N_Z)
-    def _(i):
-        @pl.when(i == 1)
-        def _():
-            gather_g.step(3)
-
-        origin = nearest(z, i)
-        gather_g.wait_across(origin)
-        pair = pl.ds(origin * N_X, N_X)
-        g_hidden = mm_nt(g_low[pair].reshape(N_X * rows, width), down[...])
-        grads[origin, :, :size] = (g_hidden * slope[origin]).astype(BF16)
-        grads[origin, :, size:] = (g_hidden * act[origin]).astype(BF16)
-        part_copy(origin).wait()
+        left = normed[pair].reshape(N_X * rows, width)
+        g_left = g_low[pair].reshape(N_X * rows, width)
+        for first in range(0, size, size // 2):
+            part, up_part = slice(first, first + size // 2), slice(size + first, size + first + size // 2)
+            act, slope = gelu_parts(mm(left, weights[:, :, :, part].reshape(width, size // 2)))
+            up = mm(left, weights[:, :, :, up_part].reshape(width, size // 2))
+            g_hidden = mm_nt(g_left, down[part])
+            hidden[origin, :, part] = (act * up).astype(BF16)
+            grads[origin, :, part] = (g_hidden * up * slope).astype(BF16)
+            grads[origin, :, up_part] = (g_hidden * act).astype(BF16)
         back = mm_nt(grads[origin], weights[...].reshape(width, 2 * size))
         parts[pair] = back.astype(BF16).reshape(N_X, rows, width)
-
+        mixed_parts[pair] = mm(hidden[origin], down[...]).astype(BF16).reshape(N_X, rows, width)
+
+    mixed_scatter.start(0)
     for i in range(N_Z):
         scatter.start(i)
     tile = normed.shape[2] // (N_Z * N_X)
@@ -779,26 +813,36 @@
             chunk = i * (tile // step) + j
             term_down[chunk // term_down.shape[1], chunk % term_down.shape[1]] = term[j * step : (j + 1) * step]
 
+    core_sum.start(0)
+
     def gu_terms(first, last):
         @pl.loop(first, last)
         def _(i):
             left = normed[:, :, pl.ds(i * tile, tile)].reshape(total, tile)
             term = mm_tn(left, grads[...].reshape(total, 2 * size)).astype(BF16)
-            term_gu[:, i] = term.reshape(term_gu.shape[0], term_gu.shape[2], 2 * size)
-
+            weights[i] = term.reshape(weights.shape[1:])
+
+    gu_terms(0, middle_tile)
+    core_sum.start(1)
+    line_sum.start(0)
+    gu_terms(middle_tile, 2 * middle_tile)
+    core_sum.start(2)
+    line_sum.start(1)
+    mixed_scatter.step(0)
+    line_sum.start(2)
+    mixed_scatter.step(1)
+    mixed_scatter.step(2)
     scatter.step(0)
-    gu_terms(0, N_Z)
+    mixed_scatter.last(g_middle_ref)
+    _, live = positions_in_run([lengths_ref[0, i] for i in range(3)], rows)
+    mixed_ref[...] = ((middle_ref[...] + g_middle_ref[...]) * live).astype(BF16)
     scatter.step(1)
-    gu_terms(N_Z, 2 * N_Z)
-    core_sum.start()
     scatter.step(2)
     outs = []
-    y = group // 2
-    for half in (1 - y, y):
-        core_sum.add(half)
-        for j, (term, out) in enumerate(((term_gu, half_gu_out), (term_down, half_down_out))):
-            outs.append(pltpu.make_async_copy(term.at[2 * half + group % 2], out.at[half], out_sem.at[j, half]))
-            outs[-1].start()
+    for j, out in enumerate((quarter_down_out, quarter_gu_out.at[0:middle_tile], quarter_gu_out.at[middle_tile : 2 * middle_tile])):
+        line_sum.add(j)
+        outs.append(pltpu.make_async_copy(core_sum.mine(j, group // 2), out, out_sem.at[j]))
+        outs[-1].start()
     scatter.last(g_middle_ref)
     gain = jnp.concatenate([gains_ref[i] for i in range(N_Z * N_X)], axis=1)[1:2]
     back, gain_term = norm_backward(middle_ref[...], gain, g_middle_ref[...])
@@ -806,14 +850,14 @@
     gain_ref[...] = jnp.zeros_like(gain_ref)
     split_gains(gain_ref, 1, gain_term)
     gather.finish()
-    gather_g.finish()
-    core_sum.finish()
+    line_sum.finish()
+    mixed_scatter.finish()
     scatter.finish()
     for copy in outs:
         copy.wait()
 
 
-def mlp_call(lengths, normed, cotangent, middle, gains, weights, down):
+def mlp_call(lengths, normed, middle, gains, g_low, weights, down):
     rows, width = normed.shape
     shards, groups, quarter_rows, both = weights.shape
     size = down.shape[0]
@@ -821,41 +865,34 @@
     shape = jax.ShapeDtypeStruct
     down_term = (size // groups // 64, 64, width)
     gu_term = (shards, quarter_rows, both)
+    terms = [down_term] + [(shards // 2, quarter_rows, both)] * 2
     pairs = (N_Z, N_X * rows)
+    scratch = [
+        (shards, rows, width), (shards, rows, width), weights.shape, down.shape, pairs + (size,), pairs + (both,),
+        (shards, rows, width), (shards, rows, width), (groups,) + down_term,
+        *[(2,) + term for term in terms], *terms,
+    ]
     return pl.pallas_call(
         mlp_kernel,
         out_shape=[
-            shape((shards, rows, width), BF16),
-            shape((2,) + gu_term, BF16),
-            shape((2,) + down_term, BF16),
+            shape(gu_term, BF16),
+            shape(down_term, BF16),
+            shape((rows, width), BF16),
             shape((rows, width), F32),
             shape(gains.shape, F32),
         ],
-        in_specs=[pl.BlockSpec(memory_space=pltpu.SMEM)] + [vmem_spec()] * 4 + [any_spec()] * 2,
-        out_specs=[any_spec()] * 3 + [vmem_spec()] * 2,
-        scratch_shapes=[
-            pltpu.VMEM((shards, rows, width), BF16),
-            pltpu.VMEM((shards, rows, width), BF16),
-            pltpu.VMEM(weights.shape, BF16),
-            pltpu.VMEM(down.shape, BF16),
-            pltpu.VMEM(pairs + (size,), F32),
-            pltpu.VMEM(pairs + (size,), F32),
-            pltpu.VMEM(pairs + (size,), BF16),
-            pltpu.VMEM(pairs + (both,), BF16),
-            pltpu.VMEM((shards, rows, width), BF16),
-            pltpu.VMEM((groups,) + gu_term, BF16),
-            pltpu.VMEM((groups,) + down_term, BF16),
-            pltpu.VMEM((2,) + gu_term, BF16),
-            pltpu.VMEM((2,) + down_term, BF16),
-        ]
+        in_specs=[pl.BlockSpec(memory_space=pltpu.SMEM)] + [vmem_spec()] * 3 + [any_spec()] * 3,
+        out_specs=[any_spec()] * 2 + [vmem_spec()] * 3,
+        scratch_shapes=[pltpu.VMEM(dims, BF16) for dims in scratch]
+        + [dma((3,)), dma((3,))]
         + Gather.scratch()
-        + Gather.scratch()
-        + CoreSum.scratch(2)
-        + [dma((2,)), dma((N_Z,)), dma((2, 2))]
-        + Scatter.scratch(rows, width),
+        + Scatter.scratch(rows, width)
+        + Scatter.scratch(rows, width)
+        + CoreSum.scratch(3)
+        + LineSum.scratch(3),
         compiler_params=pltpu.CompilerParams(collective_id=2, has_side_effects=True, vmem_limit_bytes=VMEM_LIMIT),
         name="mlp",
-    )(lengths, normed, cotangent, middle, gains, weights, down)
+    )(lengths, normed, middle, gains, g_low, weights, down)
 
 
 def mixer_backward(g_merged, saved, pos, vec, gates):
@@ -883,7 +920,7 @@
     g_decay = g_keep * (RATE_SCALE * rate) * sigmoid(-decay)
     flow = lam * weight_in
     g_inp = (flow * conv * (input_gate * (1.0 - input_gate))).astype(BF16)
-    g_conv = flow * input_gate + mm_nt(jnp.concatenate([g_rate, g_inp], axis=1), gates)
+    g_conv = flow * input_gate + mm(jnp.concatenate([g_rate, g_inp], axis=1), gates)
     g_linear = g_conv * vec[0:1]
     sums = [jnp.sum(g_conv * linear, axis=0, keepdims=True)]
     for k in (1, 2, 3):
@@ -896,49 +933,79 @@
 
 def backward_kernel(
     lengths_ref, tokens_ref, g_middle_ref, gains_ref, gain_in_ref, vec_ref, gates_ref, out_proj_ref,
-    half_gu_ref, half_down_ref, weights_ref, saved_ref, merged_ref, gathered_ref,
-    grad_gate_out, grad_up_out, grad_down_out, term_gl_out, term_out_out, grad_tokens_ref, gain_ref, small_ref, term_bd_ref,
-    g_mix, normed, weights, saved, merged, grads, parts, term_gl, term_out, total_bd, g_normed,
-    sum_gu, sum_down, line_gu, line_down,
-    a_send, a_recv, line_send, line_recv, ex_a, ex_b, ex_c, ex_d, dn_a, dn_b, dn_c, dn_d, load_sem, out_sem, *scatter_scratch,
+    quarter_gu_ref, quarter_down_ref, weights_ref, saved_ref, merged_ref, gathered_ref,
+    grad_gate_out, grad_up_out, grad_down_out, gl_out, out_out, bd_out, grad_tokens_ref, small_out_ref,
+    g_mix, normed, weights, saved, merged, grads, parts, term_gl, term_out, term_bd, total_bd, total_small, result,
+    core_gl, core_out, core_bd, line_gl, line_out, line_bd,
+    gain_terms, gains_got, packed, packs, *sems,
 ):
+    sems = list(sems)
+
+    def take(n):
+        taken = tuple(sems[:n])
+        del sems[:n]
+        return taken
+
     group, shard, z, x = place()
-    y = group // 2
+    core_mate, y_mate = mates()
     shards = N_Z * N_X
     rows, width = tokens_ref.shape
     padded = vec_ref.shape[1]
     total = shards * rows
     chans = out_proj_ref.shape[0]
+    half = quarter_gu_ref.shape[2] // 2
+    quarter_rows = quarter_gu_ref.shape[1]
+    load_sem, saved_sem, gain_send, gain_recv, pack_send, pack_recv = take(6)
+    gather = Gather(g_mix, take(2))
+    scatter = Scatter.of(parts, take(5))
+    core_sum = CoreSum(
+        [lambda q: term_gl.at[q], lambda q: term_out.at[q], lambda q: term_bd.at[q]], [core_gl, core_out, core_bd], take(2)
+    )
+    line_sum = LineSum(core_sum, [line_gl, line_out, line_bd], take(2))
+
+    def columns(ref):
+        return lambda origin, quarter: ref.at[pl.ds(quarter * quarter_rows, quarter_rows), pl.ds(origin * half, half)]
+
+    gate_exchange = Exchange([lambda to: quarter_gu_ref.at[to, :, 0:half]], [columns(grad_gate_out)], shards, take(4))
+    up_exchange = Exchange([lambda to: quarter_gu_ref.at[to, :, half : 2 * half]], [columns(grad_up_out)], shards, take(4))
+    down_exchange = Exchange([lambda to: quarter_down_ref], [lambda origin, quarter: grad_down_out.at[quarter]], 1, take(4))
+    gl_exchange = Exchange(
+        [lambda to: term_gl.at[group, to]], [lambda origin, quarter: gl_out.at[origin, quarter]], shards, take(4)
+    )
+    out_exchange = Exchange([lambda to: term_out.at[group]], [lambda origin, quarter: out_out.at[quarter]], 1, take(4))
+    bd_exchange = Exchange([lambda to: term_bd.at[group]], [lambda origin, quarter: bd_out.at[quarter]], 1, take(4))
+
+    def gain_copy(to, origin):
+        return pltpu.make_async_remote_copy(
+            src_ref=gain_terms.at[to], dst_ref=gains_got.at[origin], send_sem=gain_send.at[to], recv_sem=gain_recv.at[origin],
+            device_id=(group, to), device_id_type=MESH_ID,
+        )
+
+    def pack_copy(i):
+        return pltpu.make_async_remote_copy(
+            src_ref=packed, dst_ref=packs.at[i], send_sem=pack_send.at[i], recv_sem=pack_recv.at[i],
+            device_id=((core_mate, y_mate, 3 - group)[i], shard), device_id_type=MESH_ID,
+        )
+
+    def saved_copy(i):
+        return pltpu.make_async_copy(saved_ref.at[nearest(z, i)], saved.at[i % 2], saved_sem.at[i % 2])
+
     loads = [
         pltpu.make_async_copy(source, target, load_sem.at[i])
         for i, (source, target) in enumerate((
-            (half_gu_ref.at[y], sum_gu), (half_down_ref.at[y], sum_down),
-            (saved_ref, saved), (weights_ref, weights), (gathered_ref, normed), (merged_ref, merged),
+            (weights_ref, weights), (gathered_ref, normed), (merged_ref, merged),
         ))
     ]
     for copy in loads:
         copy.start()
-    gather = Gather(g_mix, (a_send, a_recv))
-    scatter = Scatter(parts, scatter_scratch)
-    line_sum = LineSum([half_gu_ref, half_down_ref], [line_gu, line_down], [sum_gu, sum_down], (line_send, line_recv))
-    half = sum_gu.shape[2] // 2
-    quarter_rows = sum_gu.shape[1]
-
-    def columns(ref):
-        return lambda origin, quarter: ref.at[pl.ds(quarter * quarter_rows, quarter_rows), pl.ds(origin * half, half)]
-
-    exchange = Exchange(
-        [lambda to: sum_gu.at[to, :, 0:half], lambda to: sum_gu.at[to, :, half : 2 * half]],
-        [columns(grad_gate_out), columns(grad_up_out)], shards, (ex_a, ex_b, ex_c, ex_d),
-    )
-    down_exchange = Exchange(
-        [lambda to: sum_down], [lambda origin, quarter: grad_down_out.at[quarter]], 1, (dn_a, dn_b, dn_c, dn_d)
-    )
-    greet(all_peers())
-    line_sum.start()
+    saved_copy(0).start()
+    greet(all_peers() + [((3 - group, shard), True)])
     g_mix[shard] = g_middle_ref[...].astype(BF16)
     gather.start()
-    small_ref[...] = jnp.zeros_like(small_ref)
+    gate_exchange.start()
+    down_exchange.start()
+    down_exchange.spread()
+    total_small[...] = jnp.zeros_like(total_small)
     total_bd[...] = jnp.zeros_like(total_bd)
     gather.step(1)
     gather.step(2)
@@ -950,29 +1017,37 @@
         @pl.when(i == 1)
         def _():
             gather.step(3)
+            up_exchange.start()
+
+        @pl.when(i == 2)
+        def _():
+            gate_exchange.spread()
 
         origin = nearest(z, i)
         gather.wait_across(origin)
+        saved_copy(i).wait()
+
+        @pl.when(i < N_Z - 1)
+        def _():
+            saved_copy(i + 1).start()
+
         pair = pl.ds(origin * N_X, N_X)
         g_merged = mm_nt(g_mix[pair].reshape(N_X * rows, width), out_proj_ref[...])
         g_merged = jnp.concatenate([g_merged, jnp.zeros((N_X * rows, padded - chans), F32)], axis=1)
         where = normed[pair, :, width:].reshape(N_X * rows, normed.shape[2] - width)[:, :1].astype(F32)
         g_gate, g_linear, sums, low, g_rate, g_inp = mixer_backward(
-            g_merged, [saved[origin, j] for j in range(5)], where, vec_ref[...], gates_ref[...]
+            g_merged, [saved[i % 2, j] for j in range(5)], where, vec_ref[...], gates_ref[...]
         )
         grads[origin, :, :padded] = g_gate
         grads[origin, :, padded:] = g_linear
-        small_ref[...] += sums
-        total_bd[0] += mm_tn(low, g_rate)
-        total_bd[1] += mm_tn(low, g_inp)
+        total_small[...] += sums
+        total_bd[0] += mm_tn(g_rate, low)
+        total_bd[1] += mm_tn(g_inp, low)
         back = mm_nt(grads[origin], weights[...].reshape(width, 2 * padded))
         parts[pair] = back.astype(BF16).reshape(N_X, rows, width)
 
     for i in range(N_Z):
         scatter.start(i)
-    line_sum.add()
-    exchange.start()
-    down_exchange.start()
     tile = width // shards
 
     @pl.loop(0, shards)
@@ -981,278 +1056,206 @@
         term = mm_tn(left, grads[...].reshape(total, 2 * padded)).astype(BF16)
         term_gl[:, i] = term.reshape(term_gl.shape[0], term_gl.shape[2], 2 * padded)
 
+    core_sum.start(0)
+    up_exchange.spread()
     scatter.step(0)
-    down_exchange.spread()
-    exchange.spread()
     term = mm_tn(merged[...].reshape(total, padded), g_mix[...].reshape(total, width))
     term_out[...] = term[:chans].astype(BF16).reshape(term_out.shape)
-    outs = [
-        pltpu.make_async_copy(term_gl, term_gl_out, out_sem.at[0]),
-        pltpu.make_async_copy(term_out, term_out_out, out_sem.at[1]),
-    ]
-    for copy in outs:
-        copy.start()
+    size = term_bd.shape[0] * term_bd.shape[1] * term_bd.shape[2] // 2
+    both = []
+    for i in range(2):
+        heads = [slice(h * size, (h + 1) * size) for h in range(chans // size)]
+        both.append(jnp.concatenate([total_bd[i, part, part] for part in heads], axis=1))
+    term_bd[...] = jnp.concatenate(both, axis=0).astype(BF16).reshape(term_bd.shape)
+    core_sum.start(1)
+    core_sum.start(2)
+    for j in range(3):
+        line_sum.start(j)
     scatter.step(1)
-    size = term_bd_ref.shape[1] // 2
-    for h in range(chans // size):
-        part = slice(h * size, (h + 1) * size)
-        both = jnp.concatenate([total_bd[0, part, part], total_bd[1, part, part]], axis=1)
-        term_bd_ref[part] = both.astype(BF16)
     scatter.step(2)
-    down_exchange.relay()
-    exchange.relay()
-    scatter.last(g_normed)
+    scatter.last(result)
     _, live = positions_in_run([lengths_ref[0, i] for i in range(3)], rows)
     masked = tokens_ref[...].astype(F32) * live
     gain = jnp.concatenate([gains_ref[i] for i in range(shards)], axis=1)[0:1]
-    back, gain_term = norm_backward(masked, gain, g_normed[...])
+    back, gain_term = norm_backward(masked, gain, result[...])
     grad_tokens_ref[...] = ((g_middle_ref[...] + back) * live).astype(BF16)
-    gain_ref[...] = gain_in_ref[...]
-    split_gains(gain_ref, 0, gain_term)
-    gather.finish()
-    line_sum.finish()
-    for one in (down_exchange, exchange):
+    gain_terms[...] = gain_in_ref[...]
+    split_gains(gain_terms, 0, gain_term)
+    for i in range(1, shards):
+        gain_copy((shard + i) % shards, shard).start()
+    line_sum.add(0)
+    gl_exchange.start()
+    for j, one in ((1, out_exchange), (2, bd_exchange)):
+        line_sum.add(j)
+        one.start()
+        one.spread()
+    gl_exchange.spread()
+    down_exchange.relay()
+    gate_exchange.relay()
+    up_exchange.relay()
+    gain_sum = gain_terms[shard]
+    for i in range(1, shards):
+        origin = (shard + i) % shards
+        gain_copy(origin, origin).wait_recv()
+        gain_sum = gain_sum + gains_got[origin]
+    packed[0:8] = total_small[...]
+    packed[8:16] = jnp.concatenate([gain_sum, jnp.zeros((8, padded - gain_sum.shape[1]), F32)], axis=1)
+    for i in range(3):
+        pack_copy(i).start()
+    packs_sum = packed[...]
+    for i in range(3):
+        pack_copy(i).wait_recv()
+        packs_sum = packs_sum + packs[i]
+    small_out_ref[...] = packs_sum
+    for one in (out_exchange, bd_exchange, gl_exchange):
+        one.relay()
+    for i in range(1, shards):
+        gain_copy((shard + i) % shards, shard).wait_send()
+    for i in range(3):
+        pack_copy(i).wait_send()
+    for one in (gather, scatter, line_sum):
+        one.finish()
+    for one in (down_exchange, gate_exchange, up_exchange, out_exchange, bd_exchange, gl_exchange):
         one.arrive()
         one.finish()
-    scatter.finish()
-    for copy in outs:
-        copy.wait()
-
-
-def block_diagonal(weight):
-    size = weight.shape[1]
-    heads = weight.shape[0] // size
-    parts = []
-    for h in range(heads):
-        parts.append(
-            jnp.pad(weight[h * size : (h + 1) * size], ((0, 0), (h * size, (heads - 1 - h) * size)))
-        )
-    return jnp.concatenate(parts, axis=0)
 
 
 def backward_call(
-    head, lengths, tokens, g_middle, gains, gain_terms, vec, gates, out_proj, half_gu, half_down, weights, saved, merged, gathered
+    head, lengths, tokens, g_middle, gains, gain_terms, vec, gates, out_proj, quarter_gu, quarter_down, weights, saved, merged,
+    gathered,
 ):
     rows, width = tokens.shape
     shards, groups = N_Z * N_X, weights.shape[1]
-    quarter_rows, both = half_gu.shape[2:]
+    quarter_rows, both = quarter_gu.shape[1:]
     padded = vec.shape[1]
     chans = out_proj.shape[0]
     dma = pltpu.SemaphoreType.DMA
     shape = jax.ShapeDtypeStruct
-    gl_term = (groups, shards, quarter_rows, 2 * padded)
-    out_term = (groups, chans // groups // 16, 16, width)
+    terms = [
+        (groups, shards, quarter_rows, 2 * padded),
+        (groups, chans // groups // 16, 16, width),
+        (groups, 2 * head // groups // 16, 16, chans),
+    ]
+    packed = (16, padded)
+    scratch = [
+        ((shards, rows, width), BF16), (gathered.shape, BF16), (weights.shape, BF16), ((2,) + saved.shape[1:], F32),
+        (merged.shape, BF16), ((N_Z, N_X * rows, 2 * padded), BF16), ((shards, rows, width), BF16),
+        *[(term, BF16) for term in terms], ((2, padded, padded), F32), (vec.shape, F32), ((rows, width), F32),
+        *[((2,) + term[1:], BF16) for term in terms], *[(term[1:], BF16) for term in terms],
+        (gains.shape, F32), (gains.shape, F32), (packed, F32), ((3,) + packed, F32),
+    ]
     return pl.pallas_call(
         backward_kernel,
         out_shape=[
             shape((groups * quarter_rows, shards * both // 2), BF16),
             shape((groups * quarter_rows, shards * both // 2), BF16),
-            shape((groups,) + half_down.shape[1:], BF16),
-            shape(gl_term, BF16),
-            shape(out_term, BF16),
-            shape((rows, width), BF16),
-            shape(gains.shape, F32),
-            shape(vec.shape, F32),
-            shape((chans, 2 * head), BF16),
-        ],
-        in_specs=[pl.BlockSpec(memory_space=pltpu.SMEM)] + [vmem_spec()] * 7 + [any_spec()] * 6,
-        out_specs=[any_spec()] * 5 + [vmem_spec()] * 4,
-        scratch_shapes=[
-            pltpu.VMEM((shards, rows, width), BF16),
-            pltpu.VMEM(gathered.shape, BF16),
-            pltpu.VMEM(weights.shape, BF16),
-            pltpu.VMEM(saved.shape, F32),
-            pltpu.VMEM(merged.shape, BF16),
-            pltpu.VMEM((N_Z, N_X * rows, 2 * padded), BF16),
-            pltpu.VMEM((shards, rows, width), BF16),
-            pltpu.VMEM(gl_term, BF16),
-            pltpu.VMEM(out_term, BF16),
-            pltpu.VMEM((2, padded, padded), F32),
-            pltpu.VMEM((rows, width), F32),
-        ]
-        + [pltpu.VMEM(half.shape[1:], BF16) for half in (half_gu, half_down)] * 2
-        + Gather.scratch()
-        + LineSum.scratch(2)
-        + Exchange.scratch(shards, 2)
-        + Exchange.scratch(1, 1)
-        + [dma((6,)), dma((2,))]
-        + Scatter.scratch(rows, width),
-        compiler_params=pltpu.CompilerParams(collective_id=3, has_side_effects=True, vmem_limit_bytes=VMEM_LIMIT),
-        name="mixer_backward",
-    )(lengths, tokens, g_middle, gains, gain_terms, vec, gates, out_proj, half_gu, half_down, weights, saved, merged, gathered)
-
-
-def final_kernel(
-    lengths_ref, middle_ref, small_ref, gain_ref, parts_ref, term_gl_ref, term_out_ref, term_bd_ref,
-    gl_out, out_out, bd_out, mixed_ref, small_out_ref,
-    sum_gl, sum_out, sum_bd, core_gl, core_out, core_bd, line_gl, line_out, line_bd, gains, packed, packs, result,
-    core_send, core_recv, line_send, line_recv, ex_a, ex_b, ex_c, ex_d, sp_a, sp_b, sp_c, sp_d, sq_a, sq_b, sq_c, sq_d,
-    gain_send, gain_recv, pack_send, pack_recv, load_sem, *scatter_scratch,
-):
-    group, shard, z, x = place()
-    y, core = group // 2, group % 2
-    shards = N_Z * N_X
-    rows, width = middle_ref.shape
-    core_mate, y_mate = mates()
-    terms = [term_gl_ref, term_out_ref, term_bd_ref]
-    sums = [sum_gl, sum_out, sum_bd]
-    loads = [
-        pltpu.make_async_copy(term.at[2 * half + core], total.at[half], load_sem.at[j, half])
-        for j, (term, total) in enumerate(zip(terms, sums)) for half in (0, 1)
-    ]
-    for copy in loads:
-        copy.start()
-    core_sum = CoreSum(
-        terms, [core_gl, core_out, core_bd], [lambda half, total=total: total.at[half] for total in sums], (core_send, core_recv)
-    )
-    line_sum = LineSum(sums, [line_gl, line_out, line_bd], [total.at[y] for total in sums], (line_send, line_recv))
-    scatter = Scatter(parts_ref, scatter_scratch)
-    exchanges = [
-        Exchange(
-            [lambda to: sum_gl.at[y, to]], [lambda origin, quarter: gl_out.at[origin, quarter]], shards, (ex_a, ex_b, ex_c, ex_d)
-        ),
-        Exchange([lambda to: sum_out.at[y]], [lambda origin, quarter: out_out.at[quarter]], 1, (sp_a, sp_b, sp_c, sp_d)),
-        Exchange([lambda to: sum_bd.at[y]], [lambda origin, quarter: bd_out.at[quarter]], 1, (sq_a, sq_b, sq_c, sq_d)),
-    ]
-
-    def gain_copy(to, origin):
-        return pltpu.make_async_remote_copy(
-            src_ref=gain_ref.at[to], dst_ref=gains.at[origin], send_sem=gain_send.at[to], recv_sem=gain_recv.at[origin],
-            device_id=(group, to), device_id_type=MESH_ID,
-        )
-
-    def pack_copy(i):
-        return pltpu.make_async_remote_copy(
-            src_ref=packed, dst_ref=packs.at[i], send_sem=pack_send.at[i], recv_sem=pack_recv.at[i],
-            device_id=((core_mate, y_mate, 3 - group)[i], shard), device_id_type=MESH_ID,
-        )
-
-    greet(all_peers() + [((3 - group, shard), True)])
-    core_sum.start()
-    for i in range(1, shards):
-        gain_copy((shard + i) % shards, shard).start()
-    for i in range(N_Z):
-        scatter.start(i)
-    for copy in loads:
-        copy.wait()
-    core_sum.add(1 - y)
-    line_sum.start()
-    core_sum.add(y)
-    total = gain_ref[shard]
-    for i in range(1, shards):
-        origin = (shard + i) % shards
-        gain_copy(origin, origin).wait_recv()
-        total = total + gains[origin]
-    packed[0:8] = small_ref[...]
-    packed[8:16] = jnp.concatenate([total, jnp.zeros((8, packed.shape[1] - total.shape[1]), F32)], axis=1)
-    for i in range(3):
-        pack_copy(i).start()
-    scatter.step(0)
-    scatter.step(1)
-    line_sum.add()
-    for one in exchanges:
-        one.start()
-    for one in exchanges[1:]:
-        one.spread()
-    scatter.step(2)
-    exchanges[0].spread()
-    scatter.last(result)
-    _, live = positions_in_run([lengths_ref[0, i] for i in range(3)], rows)
-    mixed_ref[...] = ((middle_ref[...] + result[...]) * live).astype(BF16)
-    total = packed[...]
-    for i in range(3):
-        pack_copy(i).wait_recv()
-        total = total + packs[i]
-    small_out_ref[...] = total
-    for one in exchanges[1:] + exchanges[:1]:
-        one.relay()
-    for i in range(1, shards):
-        gain_copy((shard + i) % shards, shard).wait_send()
-    for i in range(3):
-        pack_copy(i).wait_send()
-    core_sum.finish()
-    line_sum.finish()
-    scatter.finish()
-    for one in exchanges:
-        one.arrive()
-        one.finish()
-
-
-def final_call(lengths, middle, small, gain_terms, parts, term_gl, term_out, term_bd):
-    rows, width = middle.shape
-    shards = N_Z * N_X
-    terms = (term_gl, term_out, term_bd)
-    dma = pltpu.SemaphoreType.DMA
-    shape = jax.ShapeDtypeStruct
-    groups = term_gl.shape[0]
-    packed = (16, small.shape[1])
-    return pl.pallas_call(
-        final_kernel,
-        out_shape=[
-            shape((shards, groups) + term_gl.shape[2:], BF16),
-            shape(term_out.shape, BF16),
-            shape(term_bd.shape, BF16),
+            shape((groups,) + quarter_down.shape, BF16),
+            shape((shards, groups) + terms[0][2:], BF16),
+            shape(terms[1], BF16),
+            shape(terms[2], BF16),
             shape((rows, width), BF16),
             shape(packed, F32),
         ],
-        in_specs=[pl.BlockSpec(memory_space=pltpu.SMEM)] + [vmem_spec()] * 4 + [any_spec()] * 3,
-        out_specs=[any_spec()] * 3 + [vmem_spec()] * 2,
-        scratch_shapes=[pltpu.VMEM((2,) + term.shape[1:], BF16) for term in terms] * 2
-        + [pltpu.VMEM(term.shape[1:], BF16) for term in terms]
-        + [
-            pltpu.VMEM(gain_terms.shape, F32),
-            pltpu.VMEM(packed, F32),
-            pltpu.VMEM((3,) + packed, F32),
-            pltpu.VMEM((rows, width), F32),
-        ]
+        in_specs=[pl.BlockSpec(memory_space=pltpu.SMEM)] + [vmem_spec()] * 7 + [any_spec()] * 6,
+        out_specs=[any_spec()] * 6 + [vmem_spec()] * 2,
+        scratch_shapes=[pltpu.VMEM(dims, kind) for dims, kind in scratch]
+        + [dma((3,)), dma((2,)), dma((shards,)), dma((shards,)), dma((3,)), dma((3,))]
+        + Gather.scratch()
+        + Scatter.scratch(rows, width)
         + CoreSum.scratch(3)
         + LineSum.scratch(3)
         + Exchange.scratch(shards, 1)
-        + Exchange.scratch(1, 1) * 2
-        + [dma((shards,)), dma((shards,)), dma((3,)), dma((3,)), dma((3, 2))]
-        + Scatter.scratch(rows, width),
-        compiler_params=pltpu.CompilerParams(collective_id=4, has_side_effects=True, vmem_limit_bytes=VMEM_LIMIT),
-        name="last_sums",
-    )(lengths, middle, small, gain_terms, parts, term_gl, term_out, term_bd)
+        + Exchange.scratch(shards, 1)
+        + Exchange.scratch(1, 1)
+        + Exchange.scratch(shards, 1)
+        + Exchange.scratch(1, 1) * 2,
+        compiler_params=pltpu.CompilerParams(collective_id=3, has_side_effects=True, vmem_limit_bytes=VMEM_LIMIT),
+        name="mixer_backward",
+    )(
+        lengths, tokens, g_middle, gains, gain_terms, vec, gates, out_proj, quarter_gu, quarter_down, weights, saved, merged,
+        gathered,
+    )
+
+
+def widen_kernel(
+    mixed_ref, tokens_ref, small_ref, gate_ref, up_ref, down_ref, gl_ref, out_ref, bd_ref,
+    mixed_out, tokens_out, gain1_out, gate_in_out, linear_in_out, kernel_out, bias_out, rate_out, rate_bias_out, input_out,
+    input_bias_out, decay_out, out_out, gain2_out, gate_out, up_out, down_out,
+):
+    mixed_out[...] = mixed_ref[...]
+    tokens_out[...] = tokens_ref[...]
+    for out, ref in ((gate_out, gate_ref), (up_out, up_ref), (down_out, down_ref), (out_out, out_ref)):
+        out[...] = ref[...].astype(F32)
+    shards = gl_ref.shape[0]
+    chans, padded = gate_in_out.shape[1] // shards, gl_ref.shape[3] // 2
+    for out, first in ((gate_in_out, 0), (linear_in_out, padded)):
+        for s in range(shards):
+            out[:, s * chans : (s + 1) * chans] = gl_ref[s, 0, :, first : first + chans].astype(F32)
+
+    @pl.when(pl.program_id(0) == 0)
+    def _():
+        size = rate_out.shape[0]
+        rate_out[...] = bd_ref[:size].astype(F32)
+        input_out[...] = bd_ref[size:].astype(F32)
+        kernel_out[...] = small_ref[0:4, :chans]
+        for i, out in ((4, bias_out), (5, rate_bias_out), (6, input_bias_out), (7, decay_out), (8, gain1_out), (9, gain2_out)):
+            out[...] = small_ref[i, : out.shape[0]]
+
+
+def widen_call(mixed, grad_tokens, small, gate, up, down, gl, out, bd, gain_size):
+    shards, groups, quarter_rows, both = gl.shape
+    chans = out.shape[0]
+
+    def rows_of(dims):
+        return pl.BlockSpec((dims[0] // groups, dims[1]), lambda i: (i, 0))
+
+    def whole(dims):
+        return pl.BlockSpec(dims, lambda i: (0,) * len(dims))
+
+    wide = (groups * quarter_rows, shards * chans)
+    block = (bd.shape[0] // 2, bd.shape[1])
+    shapes = [
+        mixed.shape, grad_tokens.shape, (gain_size,), wide, wide, (4, chans), (chans,), block, (chans,), block, (chans,), (chans,),
+        out.shape, (gain_size,), gate.shape, up.shape, down.shape,
+    ]
+    specs = [whole(dims) if len(dims) == 1 or dims in ((4, chans), block) else rows_of(dims) for dims in shapes]
+    return pl.pallas_call(
+        widen_kernel,
+        grid=(groups,),
+        in_specs=[rows_of(mixed.shape), rows_of(grad_tokens.shape), whole(small.shape)]
+        + [rows_of(a.shape) for a in (gate, up, down)]
+        + [pl.BlockSpec((shards, 1, quarter_rows, both), lambda i: (0, i, 0, 0)), rows_of(out.shape), whole(bd.shape)],
+        out_specs=specs,
+        out_shape=[jax.ShapeDtypeStruct(dims, BF16 if i < 2 else F32) for i, dims in enumerate(shapes)],
+        compiler_params=pltpu.CompilerParams(vmem_limit_bytes=VMEM_LIMIT),
+        name="widen",
+    )(mixed, grad_tokens, small, gate, up, down, gl, out, bd)
 
 
 def per_device_split(
     tokens, lengths, cotangent, norm1_gain, gate_in, linear_in, conv_kernel, conv_bias, rate_weight,
     rate_bias, input_weight, input_bias, decay_param, out_proj, norm2_gain, mlp_gate, mlp_up, mlp_down,
 ):
-    width = tokens.shape[1]
     chans, size = rate_weight.shape
-    padded = -(-chans // 128) * 128
-    own_gains = jnp.pad(jnp.stack([norm1_gain, norm2_gain]).astype(F32), ((0, 6), (0, 0)))
-    fill = ((0, padded - chans), (0, padded - chans))
-    gates = jnp.concatenate(
-        [jnp.pad(block_diagonal(rate_weight), fill), jnp.pad(block_diagonal(input_weight), fill)], axis=1
-    )
-    vec = jnp.concatenate([conv_kernel, jnp.stack([conv_bias, rate_bias, input_bias, decay_param])]).astype(F32)
-    vec = jnp.pad(vec, ((0, 0), (0, padded - chans)))
-    gathered, weights, mlp_weights, gains, saved, merged, middle, normed_two = forward_call(
-        lengths, tokens, own_gains, vec, gates, out_proj, gate_in, linear_in, mlp_gate, mlp_up
-    )
-    parts, half_gu, half_down, g_middle, gain_terms = mlp_call(
-        lengths, normed_two, cotangent, middle, gains, mlp_weights, mlp_down
-    )
-    grad_gate, grad_up, grad_down, term_gl, term_out, grad_tokens, gain_terms, small, term_bd = backward_call(
-        size, lengths, tokens, g_middle, gains, gain_terms, vec, gates, out_proj, half_gu, half_down, weights, saved, merged, gathered
-    )
-    groups = term_gl.shape[0]
-    gl, grad_out, bd, mixed, small = final_call(
-        lengths, middle, small, gain_terms, parts, term_gl, term_out, term_bd.reshape(groups, -1, 16, 2 * size)
-    )
-    gl = gl.transpose(1, 2, 0, 3).reshape(gate_in.shape[0], -1, 2 * padded)
-    grad_gate_in = gl[:, :, :chans].astype(F32).reshape(gate_in.shape)
-    grad_linear_in = gl[:, :, padded : padded + chans].astype(F32).reshape(gate_in.shape)
-    bd = bd.reshape(chans, 2 * size).astype(F32)
-    own = norm1_gain.shape[0]
-    return (
-        mixed, grad_tokens, small[8, :own], grad_gate_in, grad_linear_in, small[0:4, :chans], small[4, :chans], bd[:, :size],
-        small[5, :chans], bd[:, size:], small[6, :chans], small[7, :chans], grad_out.reshape(out_proj.shape).astype(F32),
-        small[9, :own], grad_gate.astype(F32), grad_up.astype(F32), grad_down.reshape(mlp_down.shape).astype(F32),
-    )
+    gathered, weights, mlp_weights, gains, saved, merged, middle, normed_two, vec, gates, g_low = forward_call(
+        lengths, tokens, cotangent,
+        (norm1_gain, norm2_gain, conv_kernel, conv_bias, rate_bias, input_bias, decay_param, rate_weight.T, input_weight.T),
+        out_proj, gate_in, linear_in, mlp_gate, mlp_up,
+    )
+    quarter_gu, quarter_down, mixed, g_middle, gain_terms = mlp_call(
+        lengths, normed_two, middle, gains, g_low, mlp_weights, mlp_down
+    )
+    grad_gate, grad_up, grad_down, gl, grad_out, bd, grad_tokens, small = backward_call(
+        size, lengths, tokens, g_middle, gains, gain_terms, vec, gates, out_proj, quarter_gu, quarter_down, weights, saved, merged,
+        gathered,
+    )
+    outs = list(widen_call(
+        mixed, grad_tokens, small, grad_gate, grad_up, grad_down.reshape(mlp_down.shape), gl, grad_out.reshape(out_proj.shape),
+        bd.reshape(2 * size, chans), norm1_gain.shape[0],
+    ))
+    for i in (7, 9):
+        outs[i] = outs[i].T
+    return tuple(outs)
 
 
 def as_sent(shard):

time: 574 us -> 516 us (0.90)
  local copies, waits for them, and re-layouts: 24.2 us -> 0 us
  other arithmetic: 19.2 us -> 0 us
  Pallas kernels: 529 us -> 515 us
    pallas_call x2, Pallas kernels: 228 us -> 179 us  [the longest x1 164 us: mlp_call(): pl.pallas_call(mlp_kernel, out_shape=[shape(gu_term, BF16), shape(down_te...]
    pallas_call x1, Pallas kernels: 148 us -> 178 us  [forward_call(): pl.pallas_call(forward_kernel, out_shape=out_shape, in_specs=[pl.BlockSpe...]
    convert_element_type x5 -> x0, other arithmetic: 14 us -> none  [the longest x1 3.75 us: per_device_split(): grad_down.reshape(mlp_down.shape).astype(F32)]
    unnamed x26 -> x0, local copies, waits for them, and re-layouts: 12 us -> none
    slice x7 -> x0, local copies, waits for them, and re-layouts: 7.45 us -> none  [the longest x1 3.42 us: per_device_split(): gl[:, :, padded:padded + chans].astype(F32).reshape(gate_in.shape)]
    pallas_call x1, Pallas kernels: 152 us -> 159 us  [backward_call(): pl.pallas_call(backward_kernel, out_shape=[shape((groups * quarter_rows,...]
where the time goes in v4:
time: 516 us
  Pallas kernels  515 us (100%)
    pallas_call x1, Pallas kernels, forward_call(): pl.pallas_call(forward_kernel, out_shape=out_shape, in_specs=[pl.BlockSpe...  178 us
    pallas_call x1, Pallas kernels, mlp_call(): pl.pallas_call(mlp_kernel, out_shape=[shape(gu_term, BF16), shape(down_te...  164 us
    pallas_call x1, Pallas kernels, backward_call(): pl.pallas_call(backward_kernel, out_shape=[shape((groups * quarter_rows,...  159 us
    pallas_call x1, Pallas kernels, widen_call(): pl.pallas_call(widen_kernel, grid=(groups,), in_specs=[rows_of(mixed.shap...  14.8 us

profile of v4, /device:TPU:0, one launch (start us, length us, event | category | flops | bytes accessed | tf_op | source)
XLA Modules:
  0.0 515.9 jit_solution(158685960621796282)
XLA Ops:
  0.7 177.7 %mixer_forward.1 = (bf16[8,128,2176]{2,1,0:T(8,128)(2,1)}, bf16[8,4,64,768]{3,2,1,0:T(8,128)(2,1)}, bf16[8,4,64,1536]{3,2,1,0:T(8,128)(2,1)}, f32[8,8,256]{2,1,0...) custom-call(s32[1,4]{1,0:T(1,128)} %lengths_ref.5, ...), custom_call_target="tpu_custom_call" | custom-call | tf_op jit(solution)/shard_map/mixer_forward/pallas_call | solution.py:614
  178.4 163.9 %mlp.1 = (bf16[8,64,1536]{2,1,0:T(8,128)(2,1)}, bf16[3,64,2048]{2,1,0:T(8,128)(2,1)}, bf16[128,2048]{1,0:T(8,128)(2,1)}, f32[128,2048]{1,0:T(8,128)}, f32[8,8,256]{2,1,0:T(8,128)}) custom-call(s32[1,4]{1,0:T(1,128)} %lengths_ref.5, bf16[128,2048]{1,0:T(8,128)(2,1)} %get-tuple-element.58.normed_ref, f32[128,2048]{1,0:T(8,128)} %get-tuple-element.59.middle_ref, ...), custom_call_target="tpu_custom_call" | custom-call | tf_op jit(solution)/shard_map/mlp/pallas_call | solution.py:875
  342.3 158.6 %mixer_backward.1 = (bf16[256,6144]{1,0:T(8,128)(2,1)}, bf16[256,6144]{1,0:T(8,128)(2,1)}, bf16[4,3,64,2048]{3,2,1,0:T(8,128)(2,1)}, bf16[8,4,64,768]{3,2,1,0:T(...) custom-call(s32[1,4]{1,0:T(1,128)} %lengths_ref.5, ...), custom_call_target="tpu_custom_call" | custom-call | tf_op jit(solution)/shard_map/mixer_backward/pallas_call | solution.py:1147
  501.0 14.8 %widen.1 = (bf16[128,2048]{1,0:T(8,128)(2,1)}, bf16[128,2048]{1,0:T(8,128)(2,1)}, f32[256]{0:T(256)}, f32[256,2560]{1,0:T(8,128)}, f32[256,2560]{1,0:T(8,128)}, ...) custom-call(bf16[128,2048]{1,0:T(8,128)(2,1)} %get-tuple-element.63., ...), custom_call_target="tpu_custom_call" | custom-call | tf_op jit(solution)/shard_map/widen/pallas_call | solution.py:1222

commit v5 on v4

--- a/solution.py
+++ b/solution.py
@@ -21,8 +21,8 @@
     first = counts[0]
     second = first + counts[1]
     third = second + counts[2]
-    rows = lax.broadcasted_iota(jnp.int32, (row_count, 1), 0)
-    start = jnp.where(rows >= first, first, 0)
+    rows = lax.broadcasted_iota(jnp.int32, (row_count, 1), 0).astype(F32)
+    start = jnp.where(rows >= first, first, 0.0)
     start = jnp.where(rows >= second, second, start)
     start = jnp.where(rows >= third, third, start)
     return rows - start, (rows < third).astype(F32)
@@ -415,6 +415,14 @@
             mult = mult * roll_rows(mult, step)
         step *= 2
     return rate_pre, input_pre, total, (gelu_value(gate) * total).astype(BF16)
+
+
+def pair_positions(gains, origin, rows):
+    places = []
+    for column in range(N_X):
+        lengths = gains[origin * N_X + column, 2:3]
+        places.append(positions_in_run([lengths[:, i : i + 1] for i in range(3)], rows)[0])
+    return jnp.concatenate(places, axis=0)
 
 
 def rms_scale(values):
@@ -445,6 +453,9 @@
     gains_ref[...] = jnp.zeros_like(gains_ref)
     gains_ref[0:1] = gain1_ref[...].astype(F32).reshape(1, -1)
     gains_ref[1:2] = gain2_ref[...].astype(F32).reshape(1, -1)
+    lane = lax.broadcasted_iota(jnp.int32, (1, gains_ref.shape[1]), 1)
+    for i in range(3):
+        gains_ref[2:3] += jnp.where(lane == i, lengths_ref[0, i].astype(F32), 0.0)
     greet(all_peers())
 
     def gain_copy(to, origin):
@@ -456,13 +467,11 @@
     for i in range(1, shards):
         gain_copy((shard + i) % shards, shard).start()
     gains_out[shard] = gains_ref[...]
-    inside = lax.broadcasted_iota(jnp.int32, (quarter_rows, padded), 1) < chans
-    for i, copy in enumerate(fetch):
+    for copy in fetch:
         copy.wait()
-        for to in range(shards):
-            piece = raw[i, :, to * chans : (to + 1) * chans].astype(F32)
-            piece = jnp.concatenate([piece, jnp.zeros((quarter_rows, padded - chans), F32)], axis=1)
-            quarter[to, :, i * padded : (i + 1) * padded] = piece.astype(BF16)
+    for to in range(shards):
+        part = slice(to * chans, (to + 1) * chans)
+        quarter[to] = jnp.concatenate([raw[0, :, part].astype(F32), raw[1, :, part].astype(F32)], axis=1).astype(BF16)
     exchange = Exchange(
         [lambda to: quarter.at[to]], [lambda origin, q: weights.at[origin, q]], shards, (ex_a, ex_b, ex_c, ex_d)
     )
@@ -477,7 +486,7 @@
         [lambda origin, q: mlp_out.at[origin, q, :, 0:hidden], lambda origin, q: mlp_out.at[origin, q, :, hidden : 2 * hidden]],
         shards, (mx_a, mx_b, mx_c, mx_d),
     )
-    pos, live = positions_in_run([lengths_ref[0, i] for i in range(3)], rows)
+    _, live = positions_in_run([lengths_ref[0, i].astype(F32) for i in range(3)], rows)
     masked[...] = tokens_ref[...].astype(F32) * live
     g_low[...] = (cotangent_ref[...].astype(F32) * live).astype(BF16)
     g_copy = pltpu.make_async_copy(g_low, g_low_out.at[shard], g_sem)
@@ -487,8 +496,7 @@
         gain_copy(shard, (shard + i) % shards).wait_recv()
     gains = jnp.concatenate([gains_out[i] for i in range(shards)], axis=1)
     gather = Gather(buf, (gather_a, gather_b))
-    buf[shard, :, :width] = (masked[...] * rms_scale(masked[...]) * gains[0:1]).astype(BF16)
-    buf[shard, :, width:] = jnp.broadcast_to(pos.astype(F32).astype(BF16), (rows, buf.shape[2] - width))
+    buf[shard] = (masked[...] * rms_scale(masked[...]) * gains[0:1]).astype(BF16)
     gather.start()
     vec_ref[...] = jnp.zeros_like(vec_ref)
     vec_ref[0:4, :chans] = kernel_ref[...].astype(F32)
@@ -525,10 +533,11 @@
         origin = nearest(z, i)
         gather.wait_across(origin)
         pair = pl.ds(origin * N_X, N_X)
-        both = buf[pair].reshape(N_X * rows, buf.shape[2])
-        pre = mm(both[:, :width], weights[...].reshape(width, 2 * padded))
-        gate, linear = pre[:, :padded], pre[:, padded:]
-        where = both[:, width : width + 1].astype(F32)
+        pre = mm(buf[pair].reshape(N_X * rows, width), weights[...].reshape(width, 2 * chans))
+        blank = jnp.zeros((N_X * rows, padded - chans), F32)
+        gate = jnp.concatenate([pre[:, :chans], blank], axis=1)
+        linear = jnp.concatenate([pre[:, chans:], blank], axis=1)
+        where = pair_positions(gains_out, origin, rows)
         rate_pre, input_pre, state, merge = mixer_forward(linear, gate, where, vec_ref[...], gates_ref[...])
         for j, value in enumerate((gate, linear, rate_pre, input_pre, state)):
             saved[origin, j] = value
@@ -592,15 +601,16 @@
 def forward_call(lengths, tokens, cotangent, small, out_proj, gate_in, linear_in, mlp_gate, mlp_up):
     rows, width = tokens.shape
     shards, groups = lax.axis_size("shard"), lax.axis_size("group")
-    padded = -(-out_proj.shape[0] // 128) * 128
+    chans = out_proj.shape[0]
+    padded = -(-chans // 128) * 128
     gains = (8, width // shards)
     quarter_rows = gate_in.shape[0] // groups
     hidden = mlp_up.shape[1] // shards
     dma = pltpu.SemaphoreType.DMA
     shape = jax.ShapeDtypeStruct
     out_shape = [
-        shape((shards, rows, width + 128), BF16),
-        shape((shards, groups, quarter_rows, 2 * padded), BF16),
+        shape((shards, rows, width), BF16),
+        shape((shards, groups, quarter_rows, 2 * chans), BF16),
         shape((shards, groups, quarter_rows, 2 * hidden), BF16),
         shape((shards,) + gains, F32),
         shape((N_Z, 5, N_X * rows, padded), F32),
@@ -619,9 +629,9 @@
         scratch_shapes=[
             pltpu.VMEM(gains, F32),
             pltpu.VMEM((rows, width), BF16),
-            pltpu.VMEM((shards, rows, width + 128), BF16),
-            pltpu.VMEM((shards, groups, quarter_rows, 2 * padded), BF16),
-            pltpu.VMEM((shards, quarter_rows, 2 * padded), BF16),
+            pltpu.VMEM((shards, rows, width), BF16),
+            pltpu.VMEM((shards, groups, quarter_rows, 2 * chans), BF16),
+            pltpu.VMEM((shards, quarter_rows, 2 * chans), BF16),
             pltpu.VMEM((2, quarter_rows, gate_in.shape[1]), BF16),
             pltpu.VMEM((rows, width), F32),
             pltpu.VMEM((N_Z, 5, N_X * rows, padded), F32),
@@ -834,7 +844,7 @@
     mixed_scatter.step(2)
     scatter.step(0)
     mixed_scatter.last(g_middle_ref)
-    _, live = positions_in_run([lengths_ref[0, i] for i in range(3)], rows)
+    _, live = positions_in_run([lengths_ref[0, i].astype(F32) for i in range(3)], rows)
     mixed_ref[...] = ((middle_ref[...] + g_middle_ref[...]) * live).astype(BF16)
     scatter.step(1)
     scatter.step(2)
@@ -905,7 +915,7 @@
     decay = vec[7:8]
     rate, a, weight_in = decay_terms(rate_pre, decay)
     act, slope = gelu_parts(gate)
-    g_gate = (g_merged * state * slope).astype(BF16)
+    g_gate = g_merged * state * slope
     lam = g_merged * act
     mult = roll_rows(a, -1) * later[0]
     step = 1
@@ -928,7 +938,7 @@
         sums.append(jnp.sum(g_conv * (roll_rows(linear, k) * masks[k - 1]), axis=0, keepdims=True))
     for value in (g_conv, g_rate.astype(F32), g_inp.astype(F32), g_decay):
         sums.append(jnp.sum(value, axis=0, keepdims=True))
-    return g_gate, g_linear.astype(BF16), jnp.concatenate(sums, axis=0), conv.astype(BF16), g_rate, g_inp
+    return g_gate, g_linear, jnp.concatenate(sums, axis=0), conv.astype(BF16), g_rate, g_inp
 
 
 def backward_kernel(
@@ -1034,16 +1044,15 @@
         pair = pl.ds(origin * N_X, N_X)
         g_merged = mm_nt(g_mix[pair].reshape(N_X * rows, width), out_proj_ref[...])
         g_merged = jnp.concatenate([g_merged, jnp.zeros((N_X * rows, padded - chans), F32)], axis=1)
-        where = normed[pair, :, width:].reshape(N_X * rows, normed.shape[2] - width)[:, :1].astype(F32)
+        where = pair_positions(gains_ref, origin, rows)
         g_gate, g_linear, sums, low, g_rate, g_inp = mixer_backward(
             g_merged, [saved[i % 2, j] for j in range(5)], where, vec_ref[...], gates_ref[...]
         )
-        grads[origin, :, :padded] = g_gate
-        grads[origin, :, padded:] = g_linear
+        grads[origin] = jnp.concatenate([g_gate[:, :chans], g_linear[:, :chans]], axis=1).astype(BF16)
         total_small[...] += sums
         total_bd[0] += mm_tn(g_rate, low)
         total_bd[1] += mm_tn(g_inp, low)
-        back = mm_nt(grads[origin], weights[...].reshape(width, 2 * padded))
+        back = mm_nt(grads[origin], weights[...].reshape(width, 2 * chans))
         parts[pair] = back.astype(BF16).reshape(N_X, rows, width)
 
     for i in range(N_Z):
@@ -1053,8 +1062,8 @@
     @pl.loop(0, shards)
     def _(i):
         left = normed[:, :, pl.ds(i * tile, tile)].reshape(total, tile)
-        term = mm_tn(left, grads[...].reshape(total, 2 * padded)).astype(BF16)
-        term_gl[:, i] = term.reshape(term_gl.shape[0], term_gl.shape[2], 2 * padded)
+        term = mm_tn(left, grads[...].reshape(total, 2 * chans)).astype(BF16)
+        term_gl[:, i] = term.reshape(term_gl.shape[0], term_gl.shape[2], 2 * chans)
 
     core_sum.start(0)
     up_exchange.spread()
@@ -1074,7 +1083,7 @@
     scatter.step(1)
     scatter.step(2)
     scatter.last(result)
-    _, live = positions_in_run([lengths_ref[0, i] for i in range(3)], rows)
+    _, live = positions_in_run([lengths_ref[0, i].astype(F32) for i in range(3)], rows)
     masked = tokens_ref[...].astype(F32) * live
     gain = jnp.concatenate([gains_ref[i] for i in range(shards)], axis=1)[0:1]
     back, gain_term = norm_backward(masked, gain, result[...])
@@ -1132,14 +1141,14 @@
     dma = pltpu.SemaphoreType.DMA
     shape = jax.ShapeDtypeStruct
     terms = [
-        (groups, shards, quarter_rows, 2 * padded),
+        (groups, shards, quarter_rows, 2 * chans),
         (groups, chans // groups // 16, 16, width),
         (groups, 2 * head // groups // 16, 16, chans),
     ]
     packed = (16, padded)
     scratch = [
         ((shards, rows, width), BF16), (gathered.shape, BF16), (weights.shape, BF16), ((2,) + saved.shape[1:], F32),
-        (merged.shape, BF16), ((N_Z, N_X * rows, 2 * padded), BF16), ((shards, rows, width), BF16),
+        (merged.shape, BF16), ((N_Z, N_X * rows, 2 * chans), BF16), ((shards, rows, width), BF16),
         *[(term, BF16) for term in terms], ((2, padded, padded), F32), (vec.shape, F32), ((rows, width), F32),
         *[((2,) + term[1:], BF16) for term in terms], *[(term[1:], BF16) for term in terms],
         (gains.shape, F32), (gains.shape, F32), (packed, F32), ((3,) + packed, F32),
@@ -1187,8 +1196,8 @@
     for out, ref in ((gate_out, gate_ref), (up_out, up_ref), (down_out, down_ref), (out_out, out_ref)):
         out[...] = ref[...].astype(F32)
     shards = gl_ref.shape[0]
-    chans, padded = gate_in_out.shape[1] // shards, gl_ref.shape[3] // 2
-    for out, first in ((gate_in_out, 0), (linear_in_out, padded)):
+    chans = gl_ref.shape[3] // 2
+    for out, first in ((gate_in_out, 0), (linear_in_out, chans)):
         for s in range(shards):
             out[:, s * chans : (s + 1) * chans] = gl_ref[s, 0, :, first : first + chans].astype(F32)
 

time: 516 us -> 506 us (0.981)
  Pallas kernels: 515 us -> 503 us
    pallas_call x1, Pallas kernels: 159 us -> 151 us  [backward_call(): pl.pallas_call(backward_kernel, out_shape=[shape((groups * quarter_rows,...]
where the time goes in v5:
time: 506 us; the launch traced here: 504 us
  Pallas kernels  503 us (99%)
    pallas_call x1, Pallas kernels, forward_call(): pl.pallas_call(forward_kernel, out_shape=out_shape, in_specs=[pl.BlockSpe...  173 us
    pallas_call x1, Pallas kernels, mlp_call(): pl.pallas_call(mlp_kernel, out_shape=[shape(gu_term, BF16), shape(down_te...  164 us
    pallas_call x1, Pallas kernels, backward_call(): pl.pallas_call(backward_kernel, out_shape=[shape((groups * quarter_rows,...  151 us
    pallas_call x1, Pallas kernels, widen_call(): pl.pallas_call(widen_kernel, grid=(groups,), in_specs=[rows_of(mixed.shap...  14.5 us

profile of v5, /device:TPU:0, one launch (start us, length us, event | category | flops | bytes accessed | tf_op | source)
XLA Modules:
  0.0 504.0 jit_solution(13053326852358411619)
XLA Ops:
  0.7 173.3 %mixer_forward.1 = (bf16[8,128,2048]{2,1,0:T(8,128)(2,1)}, bf16[8,4,64,640]{3,2,1,0:T(8,128)(2,1)}, bf16[8,4,64,1536]{3,2,1,0:T(8,128)(2,1)}, f32[8,8,256]{2,1,0...) custom-call(s32[1,4]{1,0:T(1,128)} %lengths_ref.5, ...), custom_call_target="tpu_custom_call" | custom-call | tf_op jit(solution)/shard_map/mixer_forward/pallas_call | solution.py:624
  174.0 163.9 %mlp.1 = (bf16[8,64,1536]{2,1,0:T(8,128)(2,1)}, bf16[3,64,2048]{2,1,0:T(8,128)(2,1)}, bf16[128,2048]{1,0:T(8,128)(2,1)}, f32[128,2048]{1,0:T(8,128)}, f32[8,8,256]{2,1,0:T(8,128)}) custom-call(s32[1,4]{1,0:T(1,128)} %lengths_ref.5, bf16[128,2048]{1,0:T(8,128)(2,1)} %get-tuple-element.58.normed_ref, f32[128,2048]{1,0:T(8,128)} %get-tuple-element.59.middle_ref, ...), custom_call_target="tpu_custom_call" | custom-call | tf_op jit(solution)/shard_map/mlp/pallas_call | solution.py:885
  337.9 151.3 %mixer_backward.1 = (bf16[256,6144]{1,0:T(8,128)(2,1)}, bf16[256,6144]{1,0:T(8,128)(2,1)}, bf16[4,3,64,2048]{3,2,1,0:T(8,128)(2,1)}, bf16[8,4,64,640]{3,2,1,0:T(...) custom-call(s32[1,4]{1,0:T(1,128)} %lengths_ref.5, ...), custom_call_target="tpu_custom_call" | custom-call | tf_op jit(solution)/shard_map/mixer_backward/pallas_call | solution.py:1156
  489.2 14.5 %widen.1 = (bf16[128,2048]{1,0:T(8,128)(2,1)}, bf16[128,2048]{1,0:T(8,128)(2,1)}, f32[256]{0:T(256)}, f32[256,2560]{1,0:T(8,128)}, f32[256,2560]{1,0:T(8,128)}, ...) custom-call(bf16[128,2048]{1,0:T(8,128)(2,1)} %get-tuple-element.63., ...), custom_call_target="tpu_custom_call" | custom-call | tf_op jit(solution)/shard_map/widen/pallas_call | solution.py:1231

commit v6 on v5

--- a/solution.py
+++ b/solution.py
@@ -283,6 +283,10 @@
                 @pl.when(dest != self.z)
                 def _():
                     self.copy_z(dest, 0, c, 0).wait_send()
+
+
+class FineScatter(Scatter):
+    CHUNKS = 4
 
 
 class Exchange:
@@ -743,7 +747,7 @@
     lengths_ref, normed_ref, middle_ref, gains_ref, g_low_ref, weights_ref, down_ref,
     quarter_gu_out, quarter_down_out, mixed_ref, g_middle_ref, gain_ref,
     normed, g_low, weights, down, hidden, grads, parts, mixed_parts, term_down,
-    core_down, core_first, core_second, line_down, line_first, line_second, *sems,
+    core_down, core_first, core_second, line_down, line_first, line_second, result, *sems,
 ):
     sems = list(sems)
 
@@ -764,8 +768,8 @@
     for copy in loads:
         copy.start()
     gather = Gather(normed, take(2))
-    scatter = Scatter.of(parts, take(5))
-    mixed_scatter = Scatter.of(mixed_parts, take(5))
+    scatter = FineScatter.of(parts, take(5))
+    mixed_scatter = FineScatter.of(mixed_parts, take(5))
     middle_tile = N_Z * N_X // 2
     core_sum = CoreSum(
         [lambda q: term_down.at[q], lambda q: weights.at[0:middle_tile, q], lambda q: weights.at[middle_tile : 2 * middle_tile, q]],
@@ -789,7 +793,7 @@
         @pl.when(i == N_Z - 1)
         def _():
             for k in range(1, N_Z):
-                mixed_scatter.start(k)
+                scatter.start(k)
 
         origin = nearest(z, i)
         gather.wait_across(origin)
@@ -808,9 +812,9 @@
         parts[pair] = back.astype(BF16).reshape(N_X, rows, width)
         mixed_parts[pair] = mm(hidden[origin], down[...]).astype(BF16).reshape(N_X, rows, width)
 
-    mixed_scatter.start(0)
+    scatter.start(0)
     for i in range(N_Z):
-        scatter.start(i)
+        mixed_scatter.start(i)
     tile = normed.shape[2] // (N_Z * N_X)
     total = N_Z * N_X * rows
 
@@ -838,27 +842,27 @@
     gu_terms(middle_tile, 2 * middle_tile)
     core_sum.start(2)
     line_sum.start(1)
-    mixed_scatter.step(0)
+    scatter.step(0)
     line_sum.start(2)
-    mixed_scatter.step(1)
-    mixed_scatter.step(2)
-    scatter.step(0)
-    mixed_scatter.last(g_middle_ref)
-    _, live = positions_in_run([lengths_ref[0, i].astype(F32) for i in range(3)], rows)
-    mixed_ref[...] = ((middle_ref[...] + g_middle_ref[...]) * live).astype(BF16)
     scatter.step(1)
     scatter.step(2)
-    outs = []
-    for j, out in enumerate((quarter_down_out, quarter_gu_out.at[0:middle_tile], quarter_gu_out.at[middle_tile : 2 * middle_tile])):
-        line_sum.add(j)
-        outs.append(pltpu.make_async_copy(core_sum.mine(j, group // 2), out, out_sem.at[j]))
-        outs[-1].start()
+    mixed_scatter.step(0)
     scatter.last(g_middle_ref)
     gain = jnp.concatenate([gains_ref[i] for i in range(N_Z * N_X)], axis=1)[1:2]
     back, gain_term = norm_backward(middle_ref[...], gain, g_middle_ref[...])
     g_middle_ref[...] = g_low[shard].astype(F32) + back
     gain_ref[...] = jnp.zeros_like(gain_ref)
     split_gains(gain_ref, 1, gain_term)
+    mixed_scatter.step(1)
+    mixed_scatter.step(2)
+    outs = []
+    for j, out in enumerate((quarter_down_out, quarter_gu_out.at[0:middle_tile], quarter_gu_out.at[middle_tile : 2 * middle_tile])):
+        line_sum.add(j)
+        outs.append(pltpu.make_async_copy(core_sum.mine(j, group // 2), out, out_sem.at[j]))
+        outs[-1].start()
+    mixed_scatter.last(result)
+    _, live = positions_in_run([lengths_ref[0, i].astype(F32) for i in range(3)], rows)
+    mixed_ref[...] = ((middle_ref[...] + result[...]) * live).astype(BF16)
     gather.finish()
     line_sum.finish()
     mixed_scatter.finish()
@@ -894,10 +898,10 @@
         in_specs=[pl.BlockSpec(memory_space=pltpu.SMEM)] + [vmem_spec()] * 3 + [any_spec()] * 3,
         out_specs=[any_spec()] * 2 + [vmem_spec()] * 3,
         scratch_shapes=[pltpu.VMEM(dims, BF16) for dims in scratch]
-        + [dma((3,)), dma((3,))]
+        + [pltpu.VMEM((rows, width), F32), dma((3,)), dma((3,))]
         + Gather.scratch()
-        + Scatter.scratch(rows, width)
-        + Scatter.scratch(rows, width)
+        + FineScatter.scratch(rows, width)
+        + FineScatter.scratch(rows, width)
         + CoreSum.scratch(3)
         + LineSum.scratch(3),
         compiler_params=pltpu.CompilerParams(collective_id=2, has_side_effects=True, vmem_limit_bytes=VMEM_LIMIT),
@@ -1012,7 +1016,6 @@
     greet(all_peers() + [((3 - group, shard), True)])
     g_mix[shard] = g_middle_ref[...].astype(BF16)
     gather.start()
-    gate_exchange.start()
     down_exchange.start()
     down_exchange.spread()
     total_small[...] = jnp.zeros_like(total_small)
@@ -1027,9 +1030,10 @@
         @pl.when(i == 1)
         def _():
             gather.step(3)
+            gate_exchange.start()
             up_exchange.start()
 
-        @pl.when(i == 2)
+        @pl.when(i == 3)
         def _():
             gate_exchange.spread()
 

time: 506 us -> 503 us (level)
  no operation moved by 1% of the time
where the time goes in v6:
time: 503 us
  Pallas kernels  502 us (100%)
    pallas_call x1, Pallas kernels, forward_call(): pl.pallas_call(forward_kernel, out_shape=out_shape, in_specs=[pl.BlockSpe...  173 us
    pallas_call x1, Pallas kernels, mlp_call(): pl.pallas_call(mlp_kernel, out_shape=[shape(gu_term, BF16), shape(down_te...  161 us
    pallas_call x1, Pallas kernels, backward_call(): pl.pallas_call(backward_kernel, out_shape=[shape((groups * quarter_rows,...  153 us
    pallas_call x1, Pallas kernels, widen_call(): pl.pallas_call(widen_kernel, grid=(groups,), in_specs=[rows_of(mixed.shap...  14.5 us

profile of v6, /device:TPU:0, one launch (start us, length us, event | category | flops | bytes accessed | tf_op | source)
XLA Modules:
  0.0 502.5 jit_solution(167470771913734128)
XLA Ops:
  0.7 173.3 %mixer_forward.1 = (bf16[8,128,2048]{2,1,0:T(8,128)(2,1)}, bf16[8,4,64,640]{3,2,1,0:T(8,128)(2,1)}, bf16[8,4,64,1536]{3,2,1,0:T(8,128)(2,1)}, f32[8,8,256]{2,1,0...) custom-call(s32[1,4]{1,0:T(1,128)} %lengths_ref.5, ...), custom_call_target="tpu_custom_call" | custom-call | tf_op jit(solution)/shard_map/mixer_forward/pallas_call | solution.py:628
  174.0 160.7 %mlp.1 = (bf16[8,64,1536]{2,1,0:T(8,128)(2,1)}, bf16[3,64,2048]{2,1,0:T(8,128)(2,1)}, bf16[128,2048]{1,0:T(8,128)(2,1)}, f32[128,2048]{1,0:T(8,128)}, f32[8,8,256]{2,1,0:T(8,128)}) custom-call(s32[1,4]{1,0:T(1,128)} %lengths_ref.5, bf16[128,2048]{1,0:T(8,128)(2,1)} %get-tuple-element.58.normed_ref, f32[128,2048]{1,0:T(8,128)} %get-tuple-element.59.middle_ref, ...), custom_call_target="tpu_custom_call" | custom-call | tf_op jit(solution)/shard_map/mlp/pallas_call | solution.py:889
  334.7 153.1 %mixer_backward.1 = (bf16[256,6144]{1,0:T(8,128)(2,1)}, bf16[256,6144]{1,0:T(8,128)(2,1)}, bf16[4,3,64,2048]{3,2,1,0:T(8,128)(2,1)}, bf16[8,4,64,640]{3,2,1,0:T(...) custom-call(s32[1,4]{1,0:T(1,128)} %lengths_ref.5, ...), custom_call_target="tpu_custom_call" | custom-call | tf_op jit(solution)/shard_map/mixer_backward/pallas_call | solution.py:1160
  487.8 14.5 %widen.1 = (bf16[128,2048]{1,0:T(8,128)(2,1)}, bf16[128,2048]{1,0:T(8,128)(2,1)}, f32[256]{0:T(256)}, f32[256,2560]{1,0:T(8,128)}, f32[256,2560]{1,0:T(8,128)}, ...) custom-call(bf16[128,2048]{1,0:T(8,128)(2,1)} %get-tuple-element.63., ...), custom_call_target="tpu_custom_call" | custom-call | tf_op jit(solution)/shard_map/widen/pallas_call | solution.py:1235
